TPU v7x, 32 devices: a whole 2x2x4 slice. The times are simulated.
32 devices in a mesh: groups: 2 (over x), expert: 16 (over z, y, core).
Axes of the slice: x: 2, y: 2, z: 4, core: 2. Of those that a mesh axis runs over, the one named last changes fastest.
Arguments:
- tokens: bfloat16 [1024, 3584], P(('groups', 'expert')), parts along dimension 0, may hold values from -6 to 6
- routes: int32 [1024, 8], P(('groups', 'expert')), parts along dimension 0, may hold values from 0 to 31, all different within a row; in each aligned block of 32 rows (0 to 31, 32 to 63, ...) at most 9 rows name the same one
- gate_code: int32 [1024, 8], P(('groups', 'expert')), parts along dimension 0, may hold values from 0 to 15
- base_weight: bfloat16 [3584, 1024], replicated, may hold values from -0.09375 to 0.09375
- delta_in: bfloat16 [32, 3584, 128], P('expert'), may hold values from -0.09375 to 0.09375
- delta_out: bfloat16 [32, 128, 1024], P('expert'), may hold values from -0.5 to 0.5
Outputs:
- combined: bfloat16 [1024, 1024], P(('groups', 'expert')), parts along dimension 0
There are 2 independent parts, one for each index of `groups`. A program takes and returns all parts, laid end to end along the dimension named above; an argument that names none is the same for every part. Nothing has to cross between parts.
Inputs may be any that keep to these rules, and one draw needn't show every extreme that they name: `routes`: each row names 8 different experts; the rows of one device name any expert at most 9 times, a bound that some block reaches.
All inputs are finite; a program needn't handle non-finite values.
Results may differ from a plain program's by a relative error of at most 0.0065.
Values may be sent and summed in bfloat16 or wider, within the bound.
No kernel may reach another device: no remote copies, remote signals or barrier semaphores. Data moves between devices by JAX's collectives and lax.ppermute only.
A program may use at most 64 MiB of HBM per device.

v0:
```python
import jax
import jax.numpy as jnp
from jax import lax
from jax.sharding import PartitionSpec as P

gate_levels = 16.0


def shards(tokens, routes, gate_code, base_weight, delta_in, delta_out):
    devices_count = lax.axis_size("expert")
    local_experts = delta_in.shape[0]
    experts = local_experts * devices_count
    tok_rows, top_count = routes.shape
    capacity = tok_rows * top_count // experts + 1 + tok_rows // 64
    features = tokens.shape[1]
    flat_routes = routes.reshape(-1)
    onehot = (flat_routes[:, None] == jnp.arange(experts, dtype=jnp.int32)[None, :]).astype(
        jnp.int32
    )
    earlier = jnp.cumsum(onehot, axis=0) - onehot
    position = jnp.sum(earlier * onehot, axis=1)
    slot_index = flat_routes * capacity + position
    repeated = jnp.repeat(tokens, top_count, axis=0)
    outgoing = jnp.zeros((experts * capacity, features), tokens.dtype).at[slot_index].set(repeated)
    outgoing = outgoing.reshape(devices_count, local_experts, capacity, features)
    local_shared = jnp.dot(tokens, base_weight, preferred_element_type=jnp.float32)
    latent = jnp.einsum(
        "secd,edr->secr",
        lax.all_to_all(outgoing, "expert", split_axis=0, concat_axis=0, tiled=True),
        delta_in,
        preferred_element_type=jnp.float32,
    ).astype(jnp.bfloat16)
    change = jnp.einsum(
        "secr,erf->secf", latent, delta_out, preferred_element_type=jnp.float32
    ).astype(jnp.bfloat16)
    returned = lax.all_to_all(change, "expert", split_axis=0, concat_axis=0, tiled=True)
    picked = returned.reshape(experts * capacity, -1)[slot_index].reshape(tok_rows, top_count, -1)
    hidden = jax.nn.silu(local_shared[:, None, :] + picked.astype(jnp.float32)).astype(jnp.bfloat16)
    weights = (gate_code.astype(jnp.float32) + 1.0) / gate_levels
    return jnp.sum(weights[:, :, None] * hidden.astype(jnp.float32), axis=1).astype(jnp.bfloat16)


def solution(mesh):
    placed = (
        P(("groups", "expert"), None),
        P(("groups", "expert"), None),
        P(("groups", "expert"), None),
        P(),
        P("expert", None, None),
        P("expert", None, None),
    )
    return jax.shard_map(
        shards, mesh=mesh, in_specs=placed, out_specs=P(("groups", "expert"), None), check_vma=False
    )
```

profile of v0, /device:TPU:0, one launch (start us, length us, event | category | flops | bytes accessed | tf_op | source)
XLA Modules:
  0.0 96.9 jit_solution(9512441901367317653)
XLA Ops:
  0.0 0.0 copy-start
  0.0 0.9 copy.25
  0.9 0.1 eq.29
  1.0 0.1 eq.25
  1.1 0.7 broadcast_multiply_fusion
  1.8 0.6 reduce-window.6
  2.4 0.2 slice_reduce_fusion
  2.6 0.1 copy.24
  2.7 0.1 mul.34
  2.8 0.1 fusion.28
  2.9 5.0 %scatter_custom_fusion = bf16[288,3584]{1,0:T(8,128)(2,1)} fusion(s32[256]{0:T(256)S(1)} %bitcast.47, bf16[]{:T(256)} %constant.5.clone.1, bf16[32,3584]{1,0:T(8,128)(2,1)} %param.6), kind=kCustom, calls=%fused_computation.5 | custom fusion | bytes 2293762 | tf_op jit(solution)/shard_map/scatter | solution.py:24
  7.9 4.4 %reshape.62 = bf16[16,2,9,3584]{3,2,1,0:T(8,128)(2,1)} reshape(bf16[288,3584]{1,0:T(8,128)(2,1)} %scatter_custom_fusion) | data formatting | bytes 4128768 | tf_op jit(solution)/shard_map/reshape | solution.py:25
  12.3 4.3 %copy.28 = bf16[16,2,9,3584]{3,1,2,0:T(2,128)(2,1)S(1)} copy(bf16[16,2,9,3584]{3,2,1,0:T(8,128)(2,1)} %reshape.62) | data formatting | bytes 4128768 | tf_op jit(solution)/shard_map/reshape | solution.py:25
  16.6 53.9 %all_to_all.10 = bf16[16,2,9,3584]{3,1,2,0:T(2,128)(2,1)S(1)} all-to-all(bf16[16,2,9,3584]{3,1,2,0:T(2,128)(2,1)S(1)} %copy.28), channel_id=1, replica_groups=mesh['groups'=2,'expert'=16] {'expert'}, dimensions={0} | all-to-all | bytes 4128768 | tf_op jit(solution)/shard_map/all_to_all | solution.py:29
  70.5 0.0 copy-done
  70.5 1.1 %fusion.11 = bf16[16,2,9,128]{3,2,0,1:T(8,128)(2,1)S(1)} fusion(bf16[2,3584,128]{2,1,0:T(8,128)(2,1)S(1)} %copy-done, bf16[16,2,9,3584]{3,1,2,0:T(2,128)(2,1)S(1)} %all_to_all.10), kind=kOutput, calls=%fused_computation.10 | convolution fusion | flops 264278016 | bytes 3973120 | tf_op jit(solution)/shard_map/secd,edr->secr/dot_general | solution.py:27
  71.7 0.0 copy-done.3
  71.7 0.0 copy-start.4
  71.7 0.0 copy-start.1
  71.7 0.3 fusion.5
  72.0 1.4 %copy.31 = bf16[16,2,9,1024]{3,1,2,0:T(2,128)(2,1)} copy(bf16[16,2,9,1024]{3,0,2,1:T(8,128)(2,1)S(1)} %fusion.5) | data formatting | bytes 1179648 | tf_op jit(solution)/shard_map/convert_element_type | solution.py:35
  73.4 4.9 %all-to-all-start.1 = ((bf16[16,2,9,1024]{3,1,2,0:T(2,128)(2,1)}), bf16[16,2,9,1024]{3,1,2,0:T(2,128)(2,1)S(1)}, u32[]{:S(2)}, u32[]{:S(2)}) async-start(bf16[16,2,9,1024]{3,1,2,0:T(2,128)(2,1)} %copy.31), calls=%async_computation.1 | async-start | bytes 1179648 | tf_op jit(solution)/shard_map/all_to_all | solution.py:36
  78.4 0.0 copy-done.4
  78.4 0.1 copy.23
  78.5 0.0 copy-done.1
  78.5 5.1 %fusion.30 = f32[32,1024]{1,0:T(8,128)} fusion(bf16[32,3584]{1,0:T(8,128)(2,1)S(1)} %copy-done.1, bf16[3584,1024]{1,0:T(8,128)(2,1)} %param.9), kind=kOutput, calls=%fused_computation.36 | convolution fusion | flops 234881024 | bytes 7700480 | tf_op jit(solution)/shard_map/dot_general | solution.py:26
  83.6 10.3 %all-to-all-done.1 = bf16[16,2,9,1024]{3,1,2,0:T(2,128)(2,1)S(1)} async-done(((bf16[16,2,9,1024]{3,1,2,0:T(2,128)(2,1)}), bf16[16,2,9,1024]{3,1,2,0:T(2,128)(2,1)S(1)}, u32[]{:S(2)}, u32[]{:S(2)}) %all-to-all-start.1) | async-done | bytes 589856 | tf_op jit(solution)/shard_map/all_to_all | solution.py:36
  93.9 0.2 copy.32
  94.1 0.3 reshape.63
  94.4 0.0 copy-start.2
  94.4 1.2 %gather_fusion = bf16[256,1024]{1,0:T(8,128)(2,1)S(1)} fusion(bf16[288,1024]{1,0:T(8,128)(2,1)S(1)} %reshape.63, s32[1024]{0:T(1024)S(1)} %pad_clamp_fusion), kind=kCustom, calls=%fused_computation | custom fusion | bytes 1049600 | tf_op jit(solution)/shard_map/gather | solution.py:37
  95.6 1.3 %multiply_reduce_fusion = bf16[32,1024]{1,0:T(8,128)(2,1)} fusion(bf16[256,1024]{1,0:T(8,128)(2,1)S(1)} %gather_fusion, f32[32,1024]{1,0:T(8,128)S(1)} %copy-done.2, f32[32,8]{1,0:T(8,128)S(1)} %copy.23), kind=kLoop, calls=%fused_computation.18 | loop fusion | flops 2588672 | bytes 721920 | tf_op jit(solution)/shard_map/reduce_sum | solution.py:40
  (8 shorter events, 0.1 us)
Async XLA Ops:
  0.0 70.5 %copy-start = (bf16[2,3584,128]{2,1,0:T(8,128)(2,1)S(1)}, bf16[2,3584,128]{2,1,0:T(8,128)(2,1)}, u32[]{:S(2)}) copy-start(bf16[2,3584,128]{2,1,0:T(8,128)(2,1)} %param.10) | copy-start | bytes 5505028
  70.5 1.1 %copy-start.3 = (bf16[2,128,1024]{2,1,0:T(8,128)(2,1)S(1)}, bf16[2,128,1024]{2,1,0:T(8,128)(2,1)}, u32[]{:S(2)}) copy-start(bf16[2,128,1024]{2,1,0:T(8,128)(2,1)} %param.11) | copy-start | bytes 1572868
  71.7 6.7 %copy-start.4 = (s32[32,8]{0,1:T(8,128)S(1)}, s32[32,8]{0,1:T(8,128)}, u32[]{:S(2)}) copy-start(s32[32,8]{0,1:T(8,128)} %param.8) | copy-start | bytes 3076
  71.7 6.8 %copy-start.1 = (bf16[32,3584]{1,0:T(8,128)(2,1)S(1)}, bf16[32,3584]{1,0:T(8,128)(2,1)}, u32[]{:S(2)}) copy-start(bf16[32,3584]{1,0:T(8,128)(2,1)} %param.6) | copy-start | bytes 688132
  73.4 20.5 %all-to-all-start.1 = ((bf16[16,2,9,1024]{3,1,2,0:T(2,128)(2,1)}), bf16[16,2,9,1024]{3,1,2,0:T(2,128)(2,1)S(1)}, u32[]{:S(2)}, u32[]{:S(2)}) async-start(bf16[16,2,9,1024]{3,1,2,0:T(2,128)(2,1)} %copy.31), calls=%async_computation.1 | async-start | bytes 1179648 | tf_op jit(solution)/shard_map/all_to_all | solution.py:36
  94.4 1.2 %copy-start.2 = (f32[32,1024]{1,0:T(8,128)S(1)}, f32[32,1024]{1,0:T(8,128)}, u32[]{:S(2)}) copy-start(f32[32,1024]{1,0:T(8,128)} %fusion.30) | copy-start | bytes 393220
where the time goes:
time: 97.3 us; the launch traced here: 96.9 us
  blocking collectives  53.9 us (55%)
  local copies, waits for them, and re-layouts  18.3 us (19%)
  waiting for transfers between devices  10.3 us (11%)
  matrix products  6.53 us (7%)
  starting transfers between devices  4.94 us (5%)
  other arithmetic  2.72 us (3%)
    all_to_all x1, blocking collectives, shards(): lax.all_to_all(outgoing, 'expert', split_axis=0, concat_axis=0, tiled=True)  53.9 us
    all_to_all x1, waiting for transfers between devices, shards(): lax.all_to_all(change, 'expert', split_axis=0, concat_axis=0, tiled=True)  10.3 us
    reshape x2, local copies, waits for them, and re-layouts, shards(): outgoing.reshape(devices_count, local_experts, capacity, features)  8.7 us
    dot_general x1, matrix products, shards(): jnp.dot(tokens, base_weight, preferred_element_type=jnp.float32)  5.09 us
    scatter x1, local copies, waits for them, and re-layouts, shards(): jnp.zeros((experts * capacity, features), tokens.dtype).at[slot_index]  5.02 us
    all_to_all x1, starting transfers between devices, shards(): lax.all_to_all(change, 'expert', split_axis=0, concat_axis=0, tiled=True)  4.94 us
  transfers between devices with their start and end apart: 1, of which 1 were waited for; matrix products, arithmetic and copies ran while one was open for 5% of the time, Pallas kernels for 0%

commit v1 on v0

v1 whole, which is shorter than its diff:
```python
import functools
import jax
import jax.numpy as jnp
from jax import lax
from jax.experimental import pallas as pl
from jax.experimental.pallas import tpu as pltpu
from jax.sharding import PartitionSpec as P

gate_levels = 16.0
lanes = 128
vmem = pl.BlockSpec(memory_space=pltpu.VMEM)


def pack_body(tokens_ref, routes_ref, codes_ref, out_ref):
    features = tokens_ref.shape[1]
    rows, top_count = routes_ref.shape
    width = out_ref.shape[1] - features
    out_ref[:, :features] = tokens_ref[...]
    lane = lax.broadcasted_iota(jnp.int32, (rows, width), 1)
    gates = jnp.zeros((rows, width), jnp.float32)
    for k in range(top_count):
        weight = (codes_ref[:, k : k + 1].astype(jnp.float32) + 1.0) / gate_levels
        gates = gates + jnp.where(routes_ref[:, k : k + 1] == lane, weight, 0.0)
    out_ref[:, features:] = gates.astype(out_ref.dtype)


def expert_body(features, blocks, *refs):
    first_ref, x_refs = refs[0], refs[1 : 1 + blocks]
    base_ref, down_ref, up_own_ref, up_peer_ref = refs[1 + blocks : 5 + blocks]
    out_refs = refs[5 + blocks :]
    rows = x_refs[0].shape[0]
    tokens = jnp.concatenate([x[:, :features] for x in x_refs], axis=0)
    gates = jnp.concatenate([x[:, features:] for x in x_refs], axis=0).astype(jnp.float32)
    lane = lax.broadcasted_iota(jnp.int32, gates.shape, 1)
    local, rank = up_own_ref.shape[:2]
    shared = jnp.dot(tokens, base_ref[...], preferred_element_type=jnp.float32)
    latent = jnp.dot(tokens, down_ref[...], preferred_element_type=jnp.float32)
    latent = latent.astype(jnp.bfloat16)
    total = jnp.zeros_like(shared)
    for j in range(2 * local):
        up = up_own_ref[j] if j < local else up_peer_ref[j - local]
        change = jnp.dot(
            latent[:, j * rank : (j + 1) * rank], up, preferred_element_type=jnp.float32
        )
        value = shared + change.astype(jnp.bfloat16).astype(jnp.float32)
        hidden = (value / (1.0 + jnp.exp(-value))).astype(jnp.bfloat16).astype(jnp.float32)
        expert = first_ref[j // local] + j % local
        gate = jnp.sum(jnp.where(lane == expert, gates, 0.0), axis=1, keepdims=True)
        total = total + gate * hidden
    for b, out_ref in enumerate(out_refs):
        out_ref[...] = total[b * rows : (b + 1) * rows].astype(out_ref.dtype)


def sum_body(*refs):
    total = refs[0][...].astype(jnp.float32)
    for ref in refs[1:-1]:
        total = total + ref[...].astype(jnp.float32)
    refs[-1][...] = total.astype(refs[-1].dtype)


def shards(tokens, routes, gate_code, base_weight, delta_in, delta_out):
    devices_count = lax.axis_size("expert")
    me = lax.axis_index("expert")
    local, features, rank = delta_in.shape
    rows = tokens.shape[0]
    hidden_units = base_weight.shape[1]
    experts = local * devices_count
    width = -(-experts // lanes) * lanes
    chips = devices_count // 2
    minor = 1 << ((chips.bit_length() - 1) // 2)

    def exchange(value, mask):
        return lax.ppermute(value, "expert", [(i, i ^ mask) for i in range(devices_count)])

    packed = pl.pallas_call(
        pack_body,
        out_shape=jax.ShapeDtypeStruct((rows, features + width), tokens.dtype),
        in_specs=[vmem] * 3,
        out_specs=vmem,
        cost_estimate=pl.CostEstimate(flops=0, bytes_accessed=500000, transcendentals=0),
    )(tokens, routes, gate_code)
    down_peer, up_peer = exchange(delta_in, 1), exchange(delta_out, 1)
    down = jnp.concatenate([*delta_in, *down_peer], axis=1)
    first = jnp.stack([me, me ^ 1]).astype(jnp.int32) * local

    def experts_on(blocks):
        count = len(blocks)
        return pl.pallas_call(
            functools.partial(expert_body, features, count),
            out_shape=[jax.ShapeDtypeStruct((rows, hidden_units), jnp.bfloat16)] * count,
            in_specs=[pl.BlockSpec(memory_space=pltpu.SMEM)] + [vmem] * (count + 4),
            out_specs=[vmem] * count,
            compiler_params=pltpu.CompilerParams(vmem_limit_bytes=36 << 20),
            cost_estimate=pl.CostEstimate(
                flops=2 * rows * count * features * (hidden_units + 2 * local * rank),
                bytes_accessed=9000000,
                transcendentals=0,
            ),
        )(first, *blocks, base_weight, down, delta_out, up_peer)

    majors = range(0, chips, minor)
    column = [packed if m == 0 else exchange(packed, 2 * m) for m in majors]
    partial = []
    for n in range(minor):
        held = column if n == 0 else [exchange(block, 2 * n) for block in column]
        for m, part in zip(majors, experts_on(held)):
            mask = 2 * (m + n)
            partial.append(part if mask == 0 else exchange(part, mask))
    return pl.pallas_call(
        sum_body,
        out_shape=jax.ShapeDtypeStruct((rows, hidden_units), jnp.bfloat16),
        in_specs=[vmem] * chips,
        out_specs=vmem,
    )(*partial)


def solution(mesh):
    placed = (
        P(("groups", "expert"), None),
        P(("groups", "expert"), None),
        P(("groups", "expert"), None),
        P(),
        P("expert", None, None),
        P("expert", None, None),
    )
    return jax.shard_map(
        shards, mesh=mesh, in_specs=placed, out_specs=P(("groups", "expert"), None), check_vma=False
    )
```

time: 97.3 us -> 74.9 us (0.77)
  blocking collectives: 53.9 us -> 0 us
  starting transfers between devices: 4.94 us -> 26.4 us
  waiting for transfers between devices: 10.3 us -> 28 us
  Pallas kernels: 0 us -> 10.9 us
  local copies, waits for them, and re-layouts: 18.3 us -> 8.49 us
  matrix products: 6.53 us -> 0 us
  other arithmetic: 2.72 us -> 0.52 us
    all_to_all x1 -> x0, blocking collectives: 53.9 us -> none  [shards(): lax.all_to_all(outgoing, 'expert', split_axis=0, concat_axis=0, tiled=True)]
    ppermute x0 -> x16, waiting for transfers between devices: none -> 28 us  [exchange(): lax.ppermute(value, 'expert', [(i, i ^ mask) for i in range(devices_count)])]
    ppermute x0 -> x16, starting transfers between devices: none -> 26.4 us  [exchange(): lax.ppermute(value, 'expert', [(i, i ^ mask) for i in range(devices_count)])]
    pallas_call x0 -> x4, Pallas kernels: none -> 10.9 us  [the longest x2 7.35 us: experts_on(): pl.pallas_call(functools.partial(expert_body, features, count), out_shape...]
    all_to_all x1 -> x0, waiting for transfers between devices: 10.3 us -> none  [shards(): lax.all_to_all(change, 'expert', split_axis=0, concat_axis=0, tiled=True)]
    reshape x3 -> x0, local copies, waits for them, and re-layouts: 8.95 us -> none  [the longest x2 8.7 us: shards(): outgoing.reshape(devices_count, local_experts, capacity, features)]
    dot_general x3 -> x0, matrix products: 6.53 us -> none  [the longest x1 5.09 us: shards(): jnp.dot(tokens, base_weight, preferred_element_type=jnp.float32)]
    scatter x1 -> x0, local copies, waits for them, and re-layouts: 5.02 us -> none  [shards(): jnp.zeros((experts * capacity, features), tokens.dtype).at[slot_index]]
  transfers between devices with their start and end apart: 1 -> 16, of which waited for: 1 -> 6; matrix products, arithmetic and copies ran while one was open for 5% -> 10% of each run, Pallas kernels for 0% -> 7%
where the time goes in v1:
time: 74.9 us; the launch traced here: 74.5 us
  waiting for transfers between devices  28 us (37%)
  starting transfers between devices  26.4 us (35%)
  Pallas kernels  10.9 us (15%)
  local copies, waits for them, and re-layouts  8.49 us (11%)
    ppermute x16, waiting for transfers between devices, exchange(): lax.ppermute(value, 'expert', [(i, i ^ mask) for i in range(devices_count)])  28 us
    ppermute x16, starting transfers between devices, exchange(): lax.ppermute(value, 'expert', [(i, i ^ mask) for i in range(devices_count)])  26.4 us
    pallas_call x2, Pallas kernels, experts_on(): pl.pallas_call(functools.partial(expert_body, features, count), out_shape...  7.35 us
    another operation x2, local copies, waits for them, and re-layouts, shards(): down = jnp.concatenate([*delta_in, *down_peer], axis=1)  4.52 us
    unnamed x30, local copies, waits for them, and re-layouts  3.97 us
    pallas_call x1, Pallas kernels, shards(): pl.pallas_call(pack_body, out_shape=jax.ShapeDtypeStruct((rows, features...  1.79 us
    pallas_call x1, Pallas kernels, shards(): pl.pallas_call(sum_body, out_shape=jax.ShapeDtypeStruct((rows, hidden_uni...  1.76 us
  transfers between devices with their start and end apart: 16, of which 6 were waited for; matrix products, arithmetic and copies ran while one was open for 10% of the time, Pallas kernels for 7%

profile of v1, /device:TPU:0, one launch (start us, length us, event | category | flops | bytes accessed | tf_op | source)
XLA Modules:
  0.0 74.5 jit_solution(6005568655970062946)
XLA Ops:
  0.0 0.5 collective-permute-start.3
  0.5 1.4 %copy.7.routes_ref = s32[32,8]{1,0:T(8,128)} copy(s32[32,8]{0,1:T(8,128)} %param.7) | data formatting | bytes 2048 | tf_op args[1]
  1.8 1.4 %copy.8.codes_ref = s32[32,8]{1,0:T(8,128)} copy(s32[32,8]{0,1:T(8,128)} %param.8) | data formatting | bytes 2048 | tf_op args[2]
  3.2 1.8 %shard_map.64.refs_1_ = bf16[32,3712]{1,0:T(8,128)(2,1)} custom-call(bf16[32,3584]{1,0:T(8,128)(2,1)} %tokens_ref.1, s32[32,8]{1,0:T(8,128)} %copy.7.routes_ref, s32[32,8]{1,0:T(8,128)} %copy.8.codes_ref), custom_call_target="tpu_custom_call" | custom-call | bytes 500000 | tf_op jit(solution)/shard_map/pallas_call | solution.py:75
  5.0 3.6 %collective-permute-start.1 = (bf16[32,3712]{1,0:T(8,128)(2,1)}, bf16[32,3712]{1,0:T(8,128)(2,1)S(1)}, u32[]{:S(2)}, u32[]{:S(2)}) collective-permute-start(bf16[32,3712]{1,0:T(8,128)(2,1)} %shard_map.64.refs_1_), channel_id=1, source_target_pairs={{0,8},{1,9},{2,10},{3,11},{4,12},{5,13},{6,14},{7,15},{8,0},{9,1},... | collective-permute-start | bytes 712712 | tf_op jit(solution)/shard_map/ppermute | solution.py:73
  8.6 1.3 %collective-permute-start.2 = (bf16[32,3712]{1,0:T(8,128)(2,1)}, bf16[32,3712]{1,0:T(8,128)(2,1)}, u32[]{:S(2)}, u32[]{:S(2)}) collective-permute-start(bf16[32,3712]{1,0:T(8,128)(2,1)} %shard_map.64.refs_1_), channel_id=1, source_target_pairs={{0,12},{1,13},{2,14},{3,15},{4,8},{5,9},{6,10},{7,11},{8,4},{9,5},... | collective-permute-start | bytes 712712 | tf_op jit(solution)/shard_map/ppermute | solution.py:73
  9.9 0.2 collective-permute-start
  10.1 1.5 %collective-permute-start.8 = (bf16[32,3712]{1,0:T(8,128)(2,1)}, bf16[32,3712]{1,0:T(8,128)(2,1)}, u32[]{:S(2)}, u32[]{:S(2)}) collective-permute-start(bf16[32,3712]{1,0:T(8,128)(2,1)} %shard_map.64.refs_1_), channel_id=1, source_target_pairs={{0,2},{1,3},{2,0},{3,1},{4,6},{5,7},{6,4},{7,5},{8,10},{9,11},{10,... | collective-permute-start | bytes 712712 | tf_op jit(solution)/shard_map/ppermute | solution.py:73
  11.7 2.9 %slice_bitcast_fusion.3 = (bf16[3584,128]{1,0:T(8,128)(2,1)}, bf16[3584,128]{1,0:T(8,128)(2,1)}) fusion(bf16[2,3584,128]{2,1,0:T(8,128)(2,1)} %param.10), kind=kLoop, calls=%fused_computation.4 | loop fusion | bytes 3670016 | tf_op jit(solution)/shard_map/unstack | solution.py:83
  14.7 10.9 %collective-permute-done.1.refs_3_ = bf16[32,3712]{1,0:T(8,128)(2,1)S(1)} collective-permute-done((bf16[32,3712]{1,0:T(8,128)(2,1)}, bf16[32,3712]{1,0:T(8,128)(2,1)S(1)}, u32[]{:S(2)}, u32[]{:S(2)}) %collective-permute-start.1) | collective-permute-done | bytes 237600 | tf_op jit(solution)/shard_map/ppermute | solution.py:73
  25.6 1.8 %collective-permute-start.10 = (bf16[32,3712]{1,0:T(8,128)(2,1)S(1)}, bf16[32,3712]{1,0:T(8,128)(2,1)S(1)}, u32[]{:S(2)}, u32[]{:S(2)}) collective-permute-start(bf16[32,3712]{1,0:T(8,128)(2,1)S(1)} %collective-permute-done.1.refs_3_), channel_id=1, source_target_pairs={{0,2},{1,3},{2,0},{3,1},{4,6},{5,7},{6,4},{7,5},{8,10},{9,11},{10,... | collective-permute-start | bytes 712712 | tf_op jit(solution)/shard_map/ppermute | solution.py:73
  27.4 1.0 %collective-permute-start.11 = (bf16[32,3712]{1,0:T(8,128)(2,1)}, bf16[32,3712]{1,0:T(8,128)(2,1)S(1)}, u32[]{:S(2)}, u32[]{:S(2)}) collective-permute-start(bf16[32,3712]{1,0:T(8,128)(2,1)} %collective-permute-done.2.refs_4_), channel_id=1, source_target_pairs={{0,2},{1,3},{2,0},{3,1},{4,6},{5,7},{6,4},{7,5},{8,10},{9,11},{10,... | collective-permute-start | bytes 712712 | tf_op jit(solution)/shard_map/ppermute | solution.py:73
  28.4 1.0 %collective-permute-start.9 = (bf16[32,3712]{1,0:T(8,128)(2,1)}, bf16[32,3712]{1,0:T(8,128)(2,1)S(1)}, u32[]{:S(2)}, u32[]{:S(2)}) collective-permute-start(bf16[32,3712]{1,0:T(8,128)(2,1)} %collective-permute-done.refs_2_), channel_id=1, source_target_pairs={{0,2},{1,3},{2,0},{3,1},{4,6},{5,7},{6,4},{7,5},{8,10},{9,11},{10,... | collective-permute-start | bytes 712712 | tf_op jit(solution)/shard_map/ppermute | solution.py:73
  29.4 1.6 %slice_bitcast_fusion.1 = (bf16[3584,128]{1,0:T(8,128)(2,1)S(1)}, bf16[3584,128]{1,0:T(8,128)(2,1)S(1)}) fusion(bf16[2,3584,128]{2,1,0:T(8,128)(2,1)} %collective-permute-done.3), kind=kLoop, calls=%fused_computation.2 | loop fusion | bytes 3670016 | tf_op jit(solution)/shard_map/unstack | solution.py:83
  31.1 0.4 pad_maximum_fusion.refs_6_
  31.5 2.7 %collective-permute-done.10.refs_3_ = bf16[32,3712]{1,0:T(8,128)(2,1)S(1)} collective-permute-done((bf16[32,3712]{1,0:T(8,128)(2,1)S(1)}, bf16[32,3712]{1,0:T(8,128)(2,1)S(1)}, u32[]{:S(2)}, u32[]{:S(2)}) %collective-permute-start.10) | collective-permute-done | bytes 237600 | tf_op jit(solution)/shard_map/ppermute | solution.py:73
  34.2 5.1 %collective-permute-done.11.refs_4_ = bf16[32,3712]{1,0:T(8,128)(2,1)S(1)} collective-permute-done((bf16[32,3712]{1,0:T(8,128)(2,1)}, bf16[32,3712]{1,0:T(8,128)(2,1)S(1)}, u32[]{:S(2)}, u32[]{:S(2)}) %collective-permute-start.11) | collective-permute-done | bytes 237600 | tf_op jit(solution)/shard_map/ppermute | solution.py:73
  39.3 4.7 %collective-permute-done.9.refs_2_ = bf16[32,3712]{1,0:T(8,128)(2,1)S(1)} collective-permute-done((bf16[32,3712]{1,0:T(8,128)(2,1)}, bf16[32,3712]{1,0:T(8,128)(2,1)S(1)}, u32[]{:S(2)}, u32[]{:S(2)}) %collective-permute-start.9) | collective-permute-done | bytes 237600 | tf_op jit(solution)/shard_map/ppermute | solution.py:73
  44.1 3.6 %shard_map.66 = (bf16[32,1024]{1,0:T(8,128)(2,1)S(1)}, bf16[32,1024]{1,0:T(8,128)(2,1)S(1)}, bf16[32,1024]{1,0:T(8,128)(2,1)S(1)}, bf16[32,1024]{1,0:T(8,128)(2,1)S(1)}) custom-call(s32[2]{0:T(128)S(1)} %add_multiply_fusion.refs_0_, bf16[32,3712]{1,0:T(8,128)(2,1)} %collective-permute-done.8.refs_1_, bf16[32,3712]{1,0:T(8,128)(2,1)S(1)} %collective-permute-done.9.refs_2_, ...), custom_call_target="tpu_custom_call" | custom-call | flops 1409286144 | bytes 9000000 | tf_op jit(solution)/shard_map/pallas_call | solution.py:88
  47.7 1.8 %collective-permute-start.12 = (bf16[32,1024]{1,0:T(8,128)(2,1)S(1)}, bf16[32,1024]{1,0:T(8,128)(2,1)S(1)}, u32[]{:S(2)}, u32[]{:S(2)}) collective-permute-start(bf16[32,1024]{1,0:T(8,128)(2,1)S(1)} %get-tuple-element.17), channel_id=1, source_target_pairs={{0,2},{1,3},{2,0},{3,1},{4,6},{5,7},{6,4},{7,5},{8,10},{9,11},{10,... | collective-permute-start | bytes 196616 | tf_op jit(solution)/shard_map/ppermute | solution.py:73
  49.5 5.0 %collective-permute-start.13 = (bf16[32,1024]{1,0:T(8,128)(2,1)S(1)}, bf16[32,1024]{1,0:T(8,128)(2,1)S(1)}, u32[]{:S(2)}, u32[]{:S(2)}) collective-permute-start(bf16[32,1024]{1,0:T(8,128)(2,1)S(1)} %get-tuple-element.18), channel_id=1, source_target_pairs={{0,6},{1,7},{2,4},{3,5},{4,2},{5,3},{6,0},{7,1},{8,14},{9,15},{10,... | collective-permute-start | bytes 196616 | tf_op jit(solution)/shard_map/ppermute | solution.py:73
  54.5 1.9 %collective-permute-start.14 = (bf16[32,1024]{1,0:T(8,128)(2,1)S(1)}, bf16[32,1024]{1,0:T(8,128)(2,1)S(1)}, u32[]{:S(2)}, u32[]{:S(2)}) collective-permute-start(bf16[32,1024]{1,0:T(8,128)(2,1)S(1)} %get-tuple-element.19), channel_id=1, source_target_pairs={{0,10},{1,11},{2,8},{3,9},{4,14},{5,15},{6,12},{7,13},{8,2},{9,3},... | collective-permute-start | bytes 196616 | tf_op jit(solution)/shard_map/ppermute | solution.py:73
  56.4 2.4 %collective-permute-start.15 = (bf16[32,1024]{1,0:T(8,128)(2,1)S(1)}, bf16[32,1024]{1,0:T(8,128)(2,1)S(1)}, u32[]{:S(2)}, u32[]{:S(2)}) collective-permute-start(bf16[32,1024]{1,0:T(8,128)(2,1)S(1)} %get-tuple-element.20), channel_id=1, source_target_pairs={{0,14},{1,15},{2,12},{3,13},{4,10},{5,11},{6,8},{7,9},{8,6},{9,7},... | collective-permute-start | bytes 196616 | tf_op jit(solution)/shard_map/ppermute | solution.py:73
  58.8 3.7 %shard_map.65 = (bf16[32,1024]{1,0:T(8,128)(2,1)S(1)}, bf16[32,1024]{1,0:T(8,128)(2,1)S(1)}, bf16[32,1024]{1,0:T(8,128)(2,1)S(1)}, bf16[32,1024]{1,0:T(8,128)(2,1)S(1)}) custom-call(s32[2]{0:T(128)S(1)} %add_multiply_fusion.refs_0_, bf16[32,3712]{1,0:T(8,128)(2,1)S(1)} %copy-done.1, bf16[32,3712]{1,0:T(8,128)(2,1)} %collective-permute-done.refs_2_, ...), custom_call_target="tpu_custom_call" | custom-call | flops 1409286144 | bytes 9000000 | tf_op jit(solution)/shard_map/pallas_call | solution.py:88
  62.6 0.6 copy-done.2
  63.2 0.6 collective-permute-start.5
  63.7 2.4 %collective-permute-start.6 = (bf16[32,1024]{1,0:T(8,128)(2,1)S(1)}, bf16[32,1024]{1,0:T(8,128)(2,1)S(1)}, u32[]{:S(2)}, u32[]{:S(2)}) collective-permute-start(bf16[32,1024]{1,0:T(8,128)(2,1)S(1)} %get-tuple-element.15), channel_id=1, source_target_pairs={{0,8},{1,9},{2,10},{3,11},{4,12},{5,13},{6,14},{7,15},{8,0},{9,1},... | collective-permute-start | bytes 196616 | tf_op jit(solution)/shard_map/ppermute | solution.py:73
  66.1 1.5 %collective-permute-start.7 = (bf16[32,1024]{1,0:T(8,128)(2,1)S(1)}, bf16[32,1024]{1,0:T(8,128)(2,1)S(1)}, u32[]{:S(2)}, u32[]{:S(2)}) collective-permute-start(bf16[32,1024]{1,0:T(8,128)(2,1)S(1)} %get-tuple-element.16), channel_id=1, source_target_pairs={{0,12},{1,13},{2,14},{3,15},{4,8},{5,9},{6,10},{7,11},{8,4},{9,5},... | collective-permute-start | bytes 196616 | tf_op jit(solution)/shard_map/ppermute | solution.py:73
  67.6 1.8 %collective-permute-done.6.refs_2_ = bf16[32,1024]{1,0:T(8,128)(2,1)S(1)} collective-permute-done((bf16[32,1024]{1,0:T(8,128)(2,1)S(1)}, bf16[32,1024]{1,0:T(8,128)(2,1)S(1)}, u32[]{:S(2)}, u32[]{:S(2)}) %collective-permute-start.6) | collective-permute-done | bytes 65568 | tf_op jit(solution)/shard_map/ppermute | solution.py:73
  69.4 2.8 %collective-permute-done.7.refs_3_ = bf16[32,1024]{1,0:T(8,128)(2,1)S(1)} collective-permute-done((bf16[32,1024]{1,0:T(8,128)(2,1)S(1)}, bf16[32,1024]{1,0:T(8,128)(2,1)S(1)}, u32[]{:S(2)}, u32[]{:S(2)}) %collective-permute-start.7) | collective-permute-done | bytes 65568 | tf_op jit(solution)/shard_map/ppermute | solution.py:73
  72.2 0.6 copy-done.11
  72.8 1.8 %shard_map.67 = bf16[32,1024]{1,0:T(8,128)(2,1)} custom-call(bf16[32,1024]{1,0:T(8,128)(2,1)} %copy-done.2, bf16[32,1024]{1,0:T(8,128)(2,1)} %copy-done.9, bf16[32,1024]{1,0:T(8,128)(2,1)} %copy-done.10, bf16[32,1024]{1,0:T(8,128)(2,1)} %copy-done.11, bf16[32,1024]{1,0:T(8,128)(2,1)} %copy-done.5, bf16[32,1024]{1,0:T(8,128)(2,1)} %copy-done.6, ...), custom_call_target="tpu_custom_call" | custom-call | tf_op jit(solution)/shard_map/pallas_call | solution.py:109
  (39 shorter events, 0.2 us)
Async XLA Ops:
  0.0 28.4 %collective-permute-start.3 = (bf16[2,3584,128]{2,1,0:T(8,128)(2,1)}, bf16[2,3584,128]{2,1,0:T(8,128)(2,1)}, u32[]{:S(2)}, u32[]{:S(2)}) collective-permute-start(bf16[2,3584,128]{2,1,0:T(8,128)(2,1)} %param.10), channel_id=1, source_target_pairs={{0,1},{1,0},{2,3},{3,2},{4,5},{5,4},{6,7},{7,6},{8,9},{9,8},{10,11... | collective-permute-start | bytes 5505032 | tf_op jit(solution)/shard_map/ppermute | solution.py:73
  5.0 20.7 %collective-permute-start.1 = (bf16[32,3712]{1,0:T(8,128)(2,1)}, bf16[32,3712]{1,0:T(8,128)(2,1)S(1)}, u32[]{:S(2)}, u32[]{:S(2)}) collective-permute-start(bf16[32,3712]{1,0:T(8,128)(2,1)} %shard_map.64.refs_1_), channel_id=1, source_target_pairs={{0,8},{1,9},{2,10},{3,11},{4,12},{5,13},{6,14},{7,15},{8,0},{9,1},... | collective-permute-start | bytes 712712 | tf_op jit(solution)/shard_map/ppermute | solution.py:73
  8.6 17.1 %collective-permute-start.2 = (bf16[32,3712]{1,0:T(8,128)(2,1)}, bf16[32,3712]{1,0:T(8,128)(2,1)}, u32[]{:S(2)}, u32[]{:S(2)}) collective-permute-start(bf16[32,3712]{1,0:T(8,128)(2,1)} %shard_map.64.refs_1_), channel_id=1, source_target_pairs={{0,12},{1,13},{2,14},{3,15},{4,8},{5,9},{6,10},{7,11},{8,4},{9,5},... | collective-permute-start | bytes 712712 | tf_op jit(solution)/shard_map/ppermute | solution.py:73
  9.9 17.5 %collective-permute-start = (bf16[32,3712]{1,0:T(8,128)(2,1)}, bf16[32,3712]{1,0:T(8,128)(2,1)}, u32[]{:S(2)}, u32[]{:S(2)}) collective-permute-start(bf16[32,3712]{1,0:T(8,128)(2,1)} %shard_map.64.refs_1_), channel_id=1, source_target_pairs={{0,4},{1,5},{2,6},{3,7},{4,0},{5,1},{6,2},{7,3},{8,12},{9,13},{10,... | collective-permute-start | bytes 712712 | tf_op jit(solution)/shard_map/ppermute | solution.py:73
  10.1 21.4 %collective-permute-start.8 = (bf16[32,3712]{1,0:T(8,128)(2,1)}, bf16[32,3712]{1,0:T(8,128)(2,1)}, u32[]{:S(2)}, u32[]{:S(2)}) collective-permute-start(bf16[32,3712]{1,0:T(8,128)(2,1)} %shard_map.64.refs_1_), channel_id=1, source_target_pairs={{0,2},{1,3},{2,0},{3,1},{4,6},{5,7},{6,4},{7,5},{8,10},{9,11},{10,... | collective-permute-start | bytes 712712 | tf_op jit(solution)/shard_map/ppermute | solution.py:73
  11.7 32.4 %slice-start = ((s8[7340032]{0:T(1024)(128)(4,1)}), s8[3145728]{0:T(1024)(128)(4,1)S(1)}, s32[]{:S(2)}) async-start(s8[7340032]{0:T(1024)(128)(4,1)} %bitcast.10), calls=%async_computation | async-start | bytes 6291456
  14.6 16.4 %copy-start.3 = (bf16[3584,128]{1,0:T(8,128)(2,1)S(1)}, bf16[3584,128]{1,0:T(8,128)(2,1)}, u32[]{:S(2)}) copy-start(bf16[3584,128]{1,0:T(8,128)(2,1)} %get-tuple-element.21) | copy-start | bytes 2752516
  14.6 16.4 %copy-start.4 = (bf16[3584,128]{1,0:T(8,128)(2,1)S(1)}, bf16[3584,128]{1,0:T(8,128)(2,1)}, u32[]{:S(2)}) copy-start(bf16[3584,128]{1,0:T(8,128)(2,1)} %get-tuple-element.22) | copy-start | bytes 2752516
  14.7 29.4 %slice-start.1 = ((s8[7340032]{0:T(1024)(128)(4,1)}), s8[4194304]{0:T(1024)(128)(4,1)S(1)}, s32[]{:S(2)}) async-start(s8[7340032]{0:T(1024)(128)(4,1)} %bitcast.10), calls=%async_computation.1 | async-start | bytes 8388608
  25.6 18.4 %collective-permute-start.4 = (bf16[2,128,1024]{2,1,0:T(8,128)(2,1)}, bf16[2,128,1024]{2,1,0:T(8,128)(2,1)S(1)}, u32[]{:S(2)}, u32[]{:S(2)}) collective-permute-start(bf16[2,128,1024]{2,1,0:T(8,128)(2,1)} %refs_7_.3), channel_id=1, source_target_pairs={{0,1},{1,0},{2,3},{3,2},{4,5},{5,4},{6,7},{7,6},{8,9},{9,8},{10,11... | collective-permute-start | bytes 1572872 | tf_op jit(solution)/shard_map/ppermute | solution.py:73
  25.6 8.6 %collective-permute-start.10 = (bf16[32,3712]{1,0:T(8,128)(2,1)S(1)}, bf16[32,3712]{1,0:T(8,128)(2,1)S(1)}, u32[]{:S(2)}, u32[]{:S(2)}) collective-permute-start(bf16[32,3712]{1,0:T(8,128)(2,1)S(1)} %collective-permute-done.1.refs_3_), channel_id=1, source_target_pairs={{0,2},{1,3},{2,0},{3,1},{4,6},{5,7},{6,4},{7,5},{8,10},{9,11},{10,... | collective-permute-start | bytes 712712 | tf_op jit(solution)/shard_map/ppermute | solution.py:73
  27.4 11.9 %collective-permute-start.11 = (bf16[32,3712]{1,0:T(8,128)(2,1)}, bf16[32,3712]{1,0:T(8,128)(2,1)S(1)}, u32[]{:S(2)}, u32[]{:S(2)}) collective-permute-start(bf16[32,3712]{1,0:T(8,128)(2,1)} %collective-permute-done.2.refs_4_), channel_id=1, source_target_pairs={{0,2},{1,3},{2,0},{3,1},{4,6},{5,7},{6,4},{7,5},{8,10},{9,11},{10,... | collective-permute-start | bytes 712712 | tf_op jit(solution)/shard_map/ppermute | solution.py:73
  28.4 15.6 %collective-permute-start.9 = (bf16[32,3712]{1,0:T(8,128)(2,1)}, bf16[32,3712]{1,0:T(8,128)(2,1)S(1)}, u32[]{:S(2)}, u32[]{:S(2)}) collective-permute-start(bf16[32,3712]{1,0:T(8,128)(2,1)} %collective-permute-done.refs_2_), channel_id=1, source_target_pairs={{0,2},{1,3},{2,0},{3,1},{4,6},{5,7},{6,4},{7,5},{8,10},{9,11},{10,... | collective-permute-start | bytes 712712 | tf_op jit(solution)/shard_map/ppermute | solution.py:73
  31.0 13.0 %copy-start = (bf16[2,128,1024]{2,1,0:T(8,128)(2,1)S(1)}, bf16[2,128,1024]{2,1,0:T(8,128)(2,1)}, u32[]{:S(2)}) copy-start(bf16[2,128,1024]{2,1,0:T(8,128)(2,1)} %refs_7_.3) | copy-start | bytes 1572868
  31.5 27.3 %copy-start.1 = (bf16[32,3712]{1,0:T(8,128)(2,1)S(1)}, bf16[32,3712]{1,0:T(8,128)(2,1)}, u32[]{:S(2)}) copy-start(bf16[32,3712]{1,0:T(8,128)(2,1)} %shard_map.64.refs_1_) | copy-start | bytes 712708
  47.7 16.0 %collective-permute-start.12 = (bf16[32,1024]{1,0:T(8,128)(2,1)S(1)}, bf16[32,1024]{1,0:T(8,128)(2,1)S(1)}, u32[]{:S(2)}, u32[]{:S(2)}) collective-permute-start(bf16[32,1024]{1,0:T(8,128)(2,1)S(1)} %get-tuple-element.17), channel_id=1, source_target_pairs={{0,2},{1,3},{2,0},{3,1},{4,6},{5,7},{6,4},{7,5},{8,10},{9,11},{10,... | collective-permute-start | bytes 196616 | tf_op jit(solution)/shard_map/ppermute | solution.py:73
  49.5 16.6 %collective-permute-start.13 = (bf16[32,1024]{1,0:T(8,128)(2,1)S(1)}, bf16[32,1024]{1,0:T(8,128)(2,1)S(1)}, u32[]{:S(2)}, u32[]{:S(2)}) collective-permute-start(bf16[32,1024]{1,0:T(8,128)(2,1)S(1)} %get-tuple-element.18), channel_id=1, source_target_pairs={{0,6},{1,7},{2,4},{3,5},{4,2},{5,3},{6,0},{7,1},{8,14},{9,15},{10,... | collective-permute-start | bytes 196616 | tf_op jit(solution)/shard_map/ppermute | solution.py:73
  54.5 13.1 %collective-permute-start.14 = (bf16[32,1024]{1,0:T(8,128)(2,1)S(1)}, bf16[32,1024]{1,0:T(8,128)(2,1)S(1)}, u32[]{:S(2)}, u32[]{:S(2)}) collective-permute-start(bf16[32,1024]{1,0:T(8,128)(2,1)S(1)} %get-tuple-element.19), channel_id=1, source_target_pairs={{0,10},{1,11},{2,8},{3,9},{4,14},{5,15},{6,12},{7,13},{8,2},{9,3},... | collective-permute-start | bytes 196616 | tf_op jit(solution)/shard_map/ppermute | solution.py:73
  56.4 11.2 %collective-permute-start.15 = (bf16[32,1024]{1,0:T(8,128)(2,1)S(1)}, bf16[32,1024]{1,0:T(8,128)(2,1)S(1)}, u32[]{:S(2)}, u32[]{:S(2)}) collective-permute-start(bf16[32,1024]{1,0:T(8,128)(2,1)S(1)} %get-tuple-element.20), channel_id=1, source_target_pairs={{0,14},{1,15},{2,12},{3,13},{4,10},{5,11},{6,8},{7,9},{8,6},{9,7},... | collective-permute-start | bytes 196616 | tf_op jit(solution)/shard_map/ppermute | solution.py:73
  62.5 0.6 copy-start.2
  63.2 4.4 %collective-permute-start.5 = (bf16[32,1024]{1,0:T(8,128)(2,1)S(1)}, bf16[32,1024]{1,0:T(8,128)(2,1)S(1)}, u32[]{:S(2)}, u32[]{:S(2)}) collective-permute-start(bf16[32,1024]{1,0:T(8,128)(2,1)S(1)} %get-tuple-element.14), channel_id=1, source_target_pairs={{0,4},{1,5},{2,6},{3,7},{4,0},{5,1},{6,2},{7,3},{8,12},{9,13},{10,... | collective-permute-start | bytes 196616 | tf_op jit(solution)/shard_map/ppermute | solution.py:73
  63.7 8.4 %copy-start.5 = (bf16[32,1024]{1,0:T(8,128)(2,1)}, bf16[32,1024]{1,0:T(8,128)(2,1)S(1)}, u32[]{:S(2)}) copy-start(bf16[32,1024]{1,0:T(8,128)(2,1)S(1)} %collective-permute-done.12.refs_4_) | copy-start | bytes 196612
  63.7 5.7 %collective-permute-start.6 = (bf16[32,1024]{1,0:T(8,128)(2,1)S(1)}, bf16[32,1024]{1,0:T(8,128)(2,1)S(1)}, u32[]{:S(2)}, u32[]{:S(2)}) collective-permute-start(bf16[32,1024]{1,0:T(8,128)(2,1)S(1)} %get-tuple-element.15), channel_id=1, source_target_pairs={{0,8},{1,9},{2,10},{3,11},{4,12},{5,13},{6,14},{7,15},{8,0},{9,1},... | collective-permute-start | bytes 196616 | tf_op jit(solution)/shard_map/ppermute | solution.py:73
  66.1 6.1 %copy-start.6 = (bf16[32,1024]{1,0:T(8,128)(2,1)}, bf16[32,1024]{1,0:T(8,128)(2,1)S(1)}, u32[]{:S(2)}) copy-start(bf16[32,1024]{1,0:T(8,128)(2,1)S(1)} %collective-permute-done.13.refs_5_) | copy-start | bytes 196612
  66.1 6.1 %collective-permute-start.7 = (bf16[32,1024]{1,0:T(8,128)(2,1)S(1)}, bf16[32,1024]{1,0:T(8,128)(2,1)S(1)}, u32[]{:S(2)}, u32[]{:S(2)}) collective-permute-start(bf16[32,1024]{1,0:T(8,128)(2,1)S(1)} %get-tuple-element.16), channel_id=1, source_target_pairs={{0,12},{1,13},{2,14},{3,15},{4,8},{5,9},{6,10},{7,11},{8,4},{9,5},... | collective-permute-start | bytes 196616 | tf_op jit(solution)/shard_map/ppermute | solution.py:73
  67.6 4.6 %copy-start.7 = (bf16[32,1024]{1,0:T(8,128)(2,1)}, bf16[32,1024]{1,0:T(8,128)(2,1)S(1)}, u32[]{:S(2)}) copy-start(bf16[32,1024]{1,0:T(8,128)(2,1)S(1)} %collective-permute-done.14.refs_6_) | copy-start | bytes 196612
  67.6 4.6 %copy-start.8 = (bf16[32,1024]{1,0:T(8,128)(2,1)}, bf16[32,1024]{1,0:T(8,128)(2,1)S(1)}, u32[]{:S(2)}) copy-start(bf16[32,1024]{1,0:T(8,128)(2,1)S(1)} %collective-permute-done.15.refs_7_) | copy-start | bytes 196612
  67.6 4.6 %copy-start.9 = (bf16[32,1024]{1,0:T(8,128)(2,1)}, bf16[32,1024]{1,0:T(8,128)(2,1)S(1)}, u32[]{:S(2)}) copy-start(bf16[32,1024]{1,0:T(8,128)(2,1)S(1)} %collective-permute-done.5.refs_1_) | copy-start | bytes 196612
  69.4 2.8 %copy-start.10 = (bf16[32,1024]{1,0:T(8,128)(2,1)}, bf16[32,1024]{1,0:T(8,128)(2,1)S(1)}, u32[]{:S(2)}) copy-start(bf16[32,1024]{1,0:T(8,128)(2,1)S(1)} %collective-permute-done.6.refs_2_) | copy-start | bytes 196612
  72.2 0.6 copy-start.11

commit v2 on v1

v2 whole, which is shorter than its diff:
```python
import functools
import jax
import jax.numpy as jnp
from jax import lax
from jax.experimental import pallas as pl
from jax.experimental.pallas import tpu as pltpu
from jax.sharding import PartitionSpec as P

gate_levels = 16.0
lanes = 128
most = 8
vmem = pl.BlockSpec(memory_space=pltpu.VMEM)


def pack_body(tokens_ref, routes_ref, codes_ref, out_ref, routes_buf, codes_buf, sems):
    rows, features = tokens_ref.shape
    width = out_ref.shape[1] - features
    copies = [
        pltpu.make_async_copy(routes_ref, routes_buf, sems.at[0]),
        pltpu.make_async_copy(codes_ref, codes_buf, sems.at[1]),
        pltpu.make_async_copy(tokens_ref, out_ref.at[:, pl.ds(0, features)], sems.at[2]),
    ]
    for copy in copies:
        copy.start()
    copies[0].wait()
    copies[1].wait()
    lane = lax.broadcasted_iota(jnp.int32, (rows, width), 1)
    routes = routes_buf[...].T
    weights = (codes_buf[...].astype(jnp.float32).T + 1.0) / gate_levels
    gates = jnp.zeros((rows, width), jnp.float32)
    for k in range(routes.shape[1]):
        gates = gates + jnp.where(routes[:, k : k + 1] == lane, weights[:, k : k + 1], 0.0)
    out_ref[:, features:] = gates.astype(out_ref.dtype)
    copies[2].wait()


def weave_body(own_ref, peer_ref, out_ref):
    local, _, rank = own_ref.shape
    for j in range(local):
        out_ref[:, j * rank : (j + 1) * rank] = own_ref[j]
        out_ref[:, (local + j) * rank : (local + j + 1) * rank] = peer_ref[j]


def expert_body(features, blocks, *refs):
    x_refs = refs[:blocks]
    base_ref, down_ref, up_own_ref, up_peer_ref = refs[blocks : 4 + blocks]
    out_refs = refs[4 + blocks :]
    me = lax.axis_index("expert")
    rows = x_refs[0].shape[0]
    tokens = jnp.concatenate([x[:, :features] for x in x_refs], axis=0)
    gates = jnp.concatenate([x[:, features:] for x in x_refs], axis=0).astype(jnp.float32)
    lane = lax.broadcasted_iota(jnp.int32, gates.shape, 1)
    local, rank = up_own_ref.shape[:2]
    shared = jnp.dot(tokens, base_ref[...], preferred_element_type=jnp.float32)
    latent = jnp.dot(tokens, down_ref[...], preferred_element_type=jnp.float32)
    latent = latent.astype(jnp.bfloat16)
    total = jnp.zeros_like(shared)
    for j in range(2 * local):
        up = up_own_ref[j] if j < local else up_peer_ref[j - local]
        change = jnp.dot(
            latent[:, j * rank : (j + 1) * rank], up, preferred_element_type=jnp.float32
        )
        value = shared + change.astype(jnp.bfloat16).astype(jnp.float32)
        hidden = (value / (1.0 + jnp.exp(-value))).astype(jnp.bfloat16).astype(jnp.float32)
        expert = (me if j < local else me ^ 1) * local + j % local
        gate = jnp.sum(jnp.where(lane == expert, gates, 0.0), axis=1, keepdims=True)
        total = total + gate * hidden
    for b, out_ref in enumerate(out_refs):
        out_ref[...] = total[b * rows : (b + 1) * rows].astype(out_ref.dtype)


def sum_body(*refs):
    total = refs[0][...].astype(jnp.float32)
    for ref in refs[1:-1]:
        total = total + ref[...].astype(jnp.float32)
    refs[-1][...] = total.astype(refs[-1].dtype)


def shards(tokens, routes, gate_code, base_weight, delta_in, delta_out):
    devices_count = lax.axis_size("expert")
    local, features, rank = delta_in.shape
    rows = tokens.shape[0]
    hidden_units = base_weight.shape[1]
    experts = local * devices_count
    width = -(-experts // lanes) * lanes
    chips = devices_count // 2
    minor = 1 << ((chips.bit_length() - 1) // 2)

    def exchange(value, mask):
        return lax.ppermute(value, "expert", [(i, i ^ mask) for i in range(devices_count)])

    def small(body, shape, count, megabytes, moved):
        return pl.pallas_call(
            body,
            out_shape=jax.ShapeDtypeStruct(shape, jnp.bfloat16),
            in_specs=[vmem] * count,
            out_specs=vmem,
            compiler_params=pltpu.CompilerParams(vmem_limit_bytes=megabytes << 20),
            cost_estimate=pl.CostEstimate(flops=0, bytes_accessed=moved, transcendentals=0),
        )

    def experts_on(blocks):
        count = len(blocks)
        return pl.pallas_call(
            functools.partial(expert_body, features, count),
            out_shape=[jax.ShapeDtypeStruct((rows, hidden_units), jnp.bfloat16)] * count,
            in_specs=[vmem] * (count + 4),
            out_specs=[vmem] * count,
            compiler_params=pltpu.CompilerParams(vmem_limit_bytes=26 << 20),
            cost_estimate=pl.CostEstimate(
                flops=2 * rows * count * features * (hidden_units + 2 * local * rank),
                bytes_accessed=9000000,
                transcendentals=0,
            ),
        )(*blocks, base_weight, down, delta_out, up_peer)

    down_peer, up_peer = exchange(delta_in, 1), exchange(delta_out, 1)
    packed = pl.pallas_call(
        pack_body,
        out_shape=jax.ShapeDtypeStruct((rows, features + width), tokens.dtype),
        in_specs=[pl.BlockSpec(memory_space=pltpu.HBM)] * 3,
        out_specs=vmem,
        scratch_shapes=[
            pltpu.VMEM(routes.shape[::-1], jnp.int32),
            pltpu.VMEM(routes.shape[::-1], jnp.int32),
            pltpu.SemaphoreType.DMA((3,)),
        ],
        compiler_params=pltpu.CompilerParams(vmem_limit_bytes=4 << 20),
        cost_estimate=pl.CostEstimate(flops=0, bytes_accessed=2000000, transcendentals=0),
    )(tokens, routes.T, gate_code.T)
    down = small(weave_body, (features, 2 * local * rank), 2, 9, 4000000)(delta_in, down_peer)

    held = {0: packed}
    partial = list(experts_on([packed]))
    for stage in range(1, chips.bit_length()):
        if stage == 2:
            firsts = [m for m in held if m]
            *blocks, partial[0] = lax.optimization_barrier([*(held[m] for m in firsts), partial[0]])
            held.update(zip(firsts, blocks))
        for m in range(chips):
            if m.bit_count() == stage:
                high = m & -minor
                rest = m if high == m or high.bit_count() > 1 else m ^ high
                hop = rest & -rest
                if high.bit_count() > 1:
                    hop = high & -high
                held[m] = exchange(held[m ^ hop], 2 * hop)
    for stage in range(1, chips.bit_length()):
        masks = [m for m in range(chips) if m.bit_count() == stage]
        for at in range(0, len(masks), most):
            some = masks[at : at + most]
            for m, part in zip(some, experts_on([held[m] for m in some])):
                partial.append(exchange(part, 2 * m))
    return small(sum_body, (rows, hidden_units), chips, 8, 2000000)(*partial)


def solution(mesh):
    placed = (
        P(("groups", "expert"), None),
        P(("groups", "expert"), None),
        P(("groups", "expert"), None),
        P(),
        P("expert", None, None),
        P("expert", None, None),
    )
    return jax.shard_map(
        shards, mesh=mesh, in_specs=placed, out_specs=P(("groups", "expert"), None), check_vma=False
    )
```

time: 74.9 us -> 53.7 us (0.72)
  waiting for transfers between devices: 28 us -> 13 us
  local copies, waits for them, and re-layouts: 8.49 us -> 4.86 us
  starting transfers between devices: 26.4 us -> 23.8 us
  Pallas kernels: 10.9 us -> 11.7 us
    ppermute x16, waiting for transfers between devices: 28 us -> 13 us  [exchange(): lax.ppermute(value, 'expert', [(i, i ^ mask) for i in range(devices_count)])]
    another operation x2 -> x0, local copies, waits for them, and re-layouts: 4.52 us -> none  [shards(): down = jnp.concatenate([*delta_in, *down_peer], axis=1)]
    pallas_call x2 -> x4, Pallas kernels: 7.35 us -> 10 us  [experts_on(): pl.pallas_call(functools.partial(expert_body, features, count), out_shape...]
    ppermute x16, starting transfers between devices: 26.4 us -> 23.8 us  [exchange(): lax.ppermute(value, 'expert', [(i, i ^ mask) for i in range(devices_count)])]
    pallas_call x1, Pallas kernels: 1.79 us -> 0.34 us  [shards(): pl.pallas_call(pack_body, out_shape=jax.ShapeDtypeStruct((rows, features...]
    unnamed x30 -> x14, local copies, waits for them, and re-layouts: 3.97 us -> 4.86 us
    pallas_call x1 -> x2, Pallas kernels: 1.76 us -> 1.33 us  [the longest x1 0.7 us: shards(): return small(sum_body, (rows, hidden_units), chips, 8, 2000000)(*partial)]
  transfers between devices with their start and end apart: 16 -> 16, of which waited for: 6 -> 5; matrix products, arithmetic and copies ran while one was open for 10% -> 0% of each run, Pallas kernels for 7% -> 21%
where the time goes in v2:
time: 53.7 us; the launch traced here: 53.4 us
  starting transfers between devices  23.8 us (44%)
  waiting for transfers between devices  13 us (24%)
  Pallas kernels  11.7 us (22%)
  local copies, waits for them, and re-layouts  4.86 us (9%)
    ppermute x16, starting transfers between devices, exchange(): lax.ppermute(value, 'expert', [(i, i ^ mask) for i in range(devices_count)])  23.8 us
    ppermute x16, waiting for transfers between devices, exchange(): lax.ppermute(value, 'expert', [(i, i ^ mask) for i in range(devices_count)])  13 us
    pallas_call x4, Pallas kernels, experts_on(): pl.pallas_call(functools.partial(expert_body, features, count), out_shape...  10 us
    unnamed x14, local copies, waits for them, and re-layouts  4.86 us
  transfers between devices with their start and end apart: 16, of which 5 were waited for; matrix products, arithmetic and copies ran while one was open for 0% of the time, Pallas kernels for 21%

profile of v2, /device:TPU:0, one launch (start us, length us, event | category | flops | bytes accessed | tf_op | source)
XLA Modules:
  0.0 53.4 jit_solution(7608109030380189182)
XLA Ops:
  0.0 0.5 collective-permute-start.3
  0.5 0.9 %copy-done.4 = bf16[32,3584]{1,0:T(8,128)(2,1)S(1)} copy-done((bf16[32,3584]{1,0:T(8,128)(2,1)S(1)}, bf16[32,3584]{1,0:T(8,128)(2,1)}, u32[]{:S(2)}) %copy-start.4) | copy-done | bytes 229400
  1.5 0.7 %copy-done.5 = s32[32,8]{0,1:T(8,128)S(1)} copy-done((s32[32,8]{0,1:T(8,128)S(1)}, s32[32,8]{0,1:T(8,128)}, u32[]{:S(2)}) %copy-start.5) | copy-done | bytes 1048
  2.1 0.7 %copy-done.6 = s32[32,8]{0,1:T(8,128)S(1)} copy-done((s32[32,8]{0,1:T(8,128)S(1)}, s32[32,8]{0,1:T(8,128)}, u32[]{:S(2)}) %copy-start.6) | copy-done | bytes 1048
  2.8 0.3 shard_map.64.refs_0_
  3.2 3.0 %collective-permute-start = (bf16[32,3712]{1,0:T(8,128)(2,1)S(1)}, bf16[32,3712]{1,0:T(8,128)(2,1)S(1)}, u32[]{:S(2)}, u32[]{:S(2)}) collective-permute-start(bf16[32,3712]{1,0:T(8,128)(2,1)S(1)} %shard_map.64.refs_0_), channel_id=1, source_target_pairs={{0,2},{1,3},{2,0},{3,1},{4,6},{5,7},{6,4},{7,5},{8,10},{9,11},{10,... | collective-permute-start | bytes 712712 | tf_op jit(solution)/shard_map/ppermute | solution.py:90
  6.2 1.6 %collective-permute-start.1 = (bf16[32,3712]{1,0:T(8,128)(2,1)S(1)}, bf16[32,3712]{1,0:T(8,128)(2,1)S(1)}, u32[]{:S(2)}, u32[]{:S(2)}) collective-permute-start(bf16[32,3712]{1,0:T(8,128)(2,1)S(1)} %shard_map.64.refs_0_), channel_id=1, source_target_pairs={{0,4},{1,5},{2,6},{3,7},{4,0},{5,1},{6,2},{7,3},{8,12},{9,13},{10,... | collective-permute-start | bytes 712712 | tf_op jit(solution)/shard_map/ppermute | solution.py:90
  7.8 2.6 %collective-permute-start.2 = (bf16[32,3712]{1,0:T(8,128)(2,1)S(1)}, bf16[32,3712]{1,0:T(8,128)(2,1)S(1)}, u32[]{:S(2)}, u32[]{:S(2)}) collective-permute-start(bf16[32,3712]{1,0:T(8,128)(2,1)S(1)} %shard_map.64.refs_0_), channel_id=1, source_target_pairs={{0,8},{1,9},{2,10},{3,11},{4,12},{5,13},{6,14},{7,15},{8,0},{9,1},... | collective-permute-start | bytes 712712 | tf_op jit(solution)/shard_map/ppermute | solution.py:90
  10.4 1.5 %copy-done.3 = bf16[2,3584,128]{2,1,0:T(8,128)(2,1)S(1)} copy-done((bf16[2,3584,128]{2,1,0:T(8,128)(2,1)S(1)}, bf16[2,3584,128]{2,1,0:T(8,128)(2,1)}, u32[]{:S(2)}) %copy-start.3) | copy-done | bytes 1835032
  11.9 0.6 %shard_map.65.refs_2_.refs_4_ = bf16[3584,512]{1,0:T(8,128)(2,1)S(1)} custom-call(bf16[2,3584,128]{2,1,0:T(8,128)(2,1)S(1)} %copy-done.3, bf16[2,3584,128]{2,1,0:T(8,128)(2,1)S(1)} %collective-permute-done.3.peer_ref), custom_call_target="tpu_custom_call" | custom-call | bytes 4000000 | tf_op jit(solution)/shard_map/pallas_call | solution.py:131
  12.6 1.0 %copy-done.1 = bf16[2,128,1024]{2,1,0:T(8,128)(2,1)S(1)} copy-done((bf16[2,128,1024]{2,1,0:T(8,128)(2,1)S(1)}, bf16[2,128,1024]{2,1,0:T(8,128)(2,1)}, u32[]{:S(2)}) %copy-start.1) | copy-done | bytes 524312
  13.6 2.3 %shard_map.66.refs_0_ = bf16[32,1024]{1,0:T(8,128)(2,1)S(1)} custom-call(bf16[32,3712]{1,0:T(8,128)(2,1)S(1)} %shard_map.64.refs_0_, bf16[3584,1024]{1,0:T(8,128)(2,1)S(1)} %copy-done, bf16[3584,512]{1,0:T(8,128)(2,1)S(1)} %shard_map.65.refs_2_.refs_4_, bf16[2,128,1024]{2,1,0:T(8,128)(2,1)S(1)} %copy-done.1, ...), custom_call_target="tpu_custom_call" | custom-call | flops 352321536 | bytes 9000000 | tf_op jit(solution)/shard_map/pallas_call | solution.py:104
  15.9 2.7 %collective-permute-done.1.refs_1_ = bf16[32,3712]{1,0:T(8,128)(2,1)S(1)} collective-permute-done((bf16[32,3712]{1,0:T(8,128)(2,1)S(1)}, bf16[32,3712]{1,0:T(8,128)(2,1)S(1)}, u32[]{:S(2)}, u32[]{:S(2)}) %collective-permute-start.1) | collective-permute-done | bytes 237600 | tf_op jit(solution)/shard_map/ppermute | solution.py:90
  18.6 2.4 %collective-permute-done.2.refs_2_ = bf16[32,3712]{1,0:T(8,128)(2,1)S(1)} collective-permute-done((bf16[32,3712]{1,0:T(8,128)(2,1)S(1)}, bf16[32,3712]{1,0:T(8,128)(2,1)S(1)}, u32[]{:S(2)}, u32[]{:S(2)}) %collective-permute-start.2) | collective-permute-done | bytes 237600 | tf_op jit(solution)/shard_map/ppermute | solution.py:90
  21.0 0.5 collective-permute-start.9
  21.5 0.4 collective-permute-start.10
  21.9 1.5 %collective-permute-start.8 = (bf16[32,3712]{1,0:T(8,128)(2,1)S(1)}, bf16[32,3712]{1,0:T(8,128)(2,1)S(1)}, u32[]{:S(2)}, u32[]{:S(2)}) collective-permute-start(bf16[32,3712]{1,0:T(8,128)(2,1)S(1)} %collective-permute-done.1.refs_1_), channel_id=1, source_target_pairs={{0,2},{1,3},{2,0},{3,1},{4,6},{5,7},{6,4},{7,5},{8,10},{9,11},{10,... | collective-permute-start | bytes 712712 | tf_op jit(solution)/shard_map/ppermute | solution.py:90
  23.4 4.4 %collective-permute-done.9.refs_1_ = bf16[32,3712]{1,0:T(8,128)(2,1)S(1)} collective-permute-done((bf16[32,3712]{1,0:T(8,128)(2,1)S(1)}, bf16[32,3712]{1,0:T(8,128)(2,1)S(1)}, u32[]{:S(2)}, u32[]{:S(2)}) %collective-permute-start.9) | collective-permute-done | bytes 237600 | tf_op jit(solution)/shard_map/ppermute | solution.py:90
  27.8 2.3 %collective-permute-start.14 = (bf16[32,3712]{1,0:T(8,128)(2,1)S(1)}, bf16[32,3712]{1,0:T(8,128)(2,1)S(1)}, u32[]{:S(2)}, u32[]{:S(2)}) collective-permute-start(bf16[32,3712]{1,0:T(8,128)(2,1)S(1)} %collective-permute-done.9.refs_1_), channel_id=1, source_target_pairs={{0,4},{1,5},{2,6},{3,7},{4,0},{5,1},{6,2},{7,3},{8,12},{9,13},{10,... | collective-permute-start | bytes 712712 | tf_op jit(solution)/shard_map/ppermute | solution.py:90
  30.1 2.7 %shard_map.67 = (bf16[32,1024]{1,0:T(8,128)(2,1)S(1)}, bf16[32,1024]{1,0:T(8,128)(2,1)S(1)}, bf16[32,1024]{1,0:T(8,128)(2,1)S(1)}) custom-call(bf16[32,3712]{1,0:T(8,128)(2,1)S(1)} %collective-permute-done.refs_0_, bf16[32,3712]{1,0:T(8,128)(2,1)S(1)} %collective-permute-done.1.refs_1_, bf16[32,3712]{1,0:T(8,128)(2,1)S(1)} %collective-permute-done.2.refs_2_, ...), custom_call_target="tpu_custom_call" | custom-call | flops 1056964608 | bytes 9000000 | tf_op jit(solution)/shard_map/pallas_call | solution.py:104
  32.8 0.6 %collective-permute-start.5 = (bf16[32,1024]{1,0:T(8,128)(2,1)S(1)}, bf16[32,1024]{1,0:T(8,128)(2,1)S(1)}, u32[]{:S(2)}, u32[]{:S(2)}) collective-permute-start(bf16[32,1024]{1,0:T(8,128)(2,1)S(1)} %get-tuple-element.19), channel_id=1, source_target_pairs={{0,2},{1,3},{2,0},{3,1},{4,6},{5,7},{6,4},{7,5},{8,10},{9,11},{10,... | collective-permute-start | bytes 196616 | tf_op jit(solution)/shard_map/ppermute | solution.py:90
  33.4 0.7 %collective-permute-start.6 = (bf16[32,1024]{1,0:T(8,128)(2,1)S(1)}, bf16[32,1024]{1,0:T(8,128)(2,1)S(1)}, u32[]{:S(2)}, u32[]{:S(2)}) collective-permute-start(bf16[32,1024]{1,0:T(8,128)(2,1)S(1)} %get-tuple-element.20), channel_id=1, source_target_pairs={{0,4},{1,5},{2,6},{3,7},{4,0},{5,1},{6,2},{7,3},{8,12},{9,13},{10,... | collective-permute-start | bytes 196616 | tf_op jit(solution)/shard_map/ppermute | solution.py:90
  34.1 1.2 %collective-permute-start.7 = (bf16[32,1024]{1,0:T(8,128)(2,1)S(1)}, bf16[32,1024]{1,0:T(8,128)(2,1)S(1)}, u32[]{:S(2)}, u32[]{:S(2)}) collective-permute-start(bf16[32,1024]{1,0:T(8,128)(2,1)S(1)} %get-tuple-element.21), channel_id=1, source_target_pairs={{0,8},{1,9},{2,10},{3,11},{4,12},{5,13},{6,14},{7,15},{8,0},{9,1},... | collective-permute-start | bytes 196616 | tf_op jit(solution)/shard_map/ppermute | solution.py:90
  35.3 2.7 %shard_map.68 = (bf16[32,1024]{1,0:T(8,128)(2,1)S(1)}, bf16[32,1024]{1,0:T(8,128)(2,1)S(1)}, bf16[32,1024]{1,0:T(8,128)(2,1)S(1)}) custom-call(bf16[32,3712]{1,0:T(8,128)(2,1)S(1)} %collective-permute-done.8.refs_0_, bf16[32,3712]{1,0:T(8,128)(2,1)S(1)} %collective-permute-done.9.refs_1_, bf16[32,3712]{1,0:T(8,128)(2,1)S(1)} %collective-permute-done.10.refs_2_, ...), custom_call_target="tpu_custom_call" | custom-call | flops 1056964608 | bytes 9000000 | tf_op jit(solution)/shard_map/pallas_call | solution.py:104
  38.0 1.8 %collective-permute-start.11 = (bf16[32,1024]{1,0:T(8,128)(2,1)S(1)}, bf16[32,1024]{1,0:T(8,128)(2,1)S(1)}, u32[]{:S(2)}, u32[]{:S(2)}) collective-permute-start(bf16[32,1024]{1,0:T(8,128)(2,1)S(1)} %get-tuple-element.22), channel_id=1, source_target_pairs={{0,6},{1,7},{2,4},{3,5},{4,2},{5,3},{6,0},{7,1},{8,14},{9,15},{10,... | collective-permute-start | bytes 196616 | tf_op jit(solution)/shard_map/ppermute | solution.py:90
  39.8 2.2 %collective-permute-start.12 = (bf16[32,1024]{1,0:T(8,128)(2,1)S(1)}, bf16[32,1024]{1,0:T(8,128)(2,1)S(1)}, u32[]{:S(2)}, u32[]{:S(2)}) collective-permute-start(bf16[32,1024]{1,0:T(8,128)(2,1)S(1)} %get-tuple-element.23), channel_id=1, source_target_pairs={{0,10},{1,11},{2,8},{3,9},{4,14},{5,15},{6,12},{7,13},{8,2},{9,3},... | collective-permute-start | bytes 196616 | tf_op jit(solution)/shard_map/ppermute | solution.py:90
  42.0 2.3 %shard_map.69 = bf16[32,1024]{1,0:T(8,128)(2,1)S(1)} custom-call(bf16[32,3712]{1,0:T(8,128)(2,1)S(1)} %collective-permute-done.14.refs_0_, bf16[3584,1024]{1,0:T(8,128)(2,1)S(1)} %copy-done, bf16[3584,512]{1,0:T(8,128)(2,1)S(1)} %shard_map.65.refs_2_.refs_4_, bf16[2,128,1024]{2,1,0:T(8,128)(2,1)S(1)} %copy-done.2, ...), custom_call_target="tpu_custom_call" | custom-call | flops 352321536 | bytes 9000000 | tf_op jit(solution)/shard_map/pallas_call | solution.py:104
  44.4 1.4 %collective-permute-start.13 = (bf16[32,1024]{1,0:T(8,128)(2,1)S(1)}, bf16[32,1024]{1,0:T(8,128)(2,1)S(1)}, u32[]{:S(2)}, u32[]{:S(2)}) collective-permute-start(bf16[32,1024]{1,0:T(8,128)(2,1)S(1)} %get-tuple-element.24), channel_id=1, source_target_pairs={{0,12},{1,13},{2,14},{3,15},{4,8},{5,9},{6,10},{7,11},{8,4},{9,5},... | collective-permute-start | bytes 196616 | tf_op jit(solution)/shard_map/ppermute | solution.py:90
  45.8 3.4 %collective-permute-start.15 = (bf16[32,1024]{1,0:T(8,128)(2,1)S(1)}, bf16[32,1024]{1,0:T(8,128)(2,1)S(1)}, u32[]{:S(2)}, u32[]{:S(2)}) collective-permute-start(bf16[32,1024]{1,0:T(8,128)(2,1)S(1)} %shard_map.69), channel_id=1, source_target_pairs={{0,14},{1,15},{2,12},{3,13},{4,10},{5,11},{6,8},{7,9},{8,6},{9,7},... | collective-permute-start | bytes 196616 | tf_op jit(solution)/shard_map/ppermute | solution.py:90
  49.2 1.4 %collective-permute-done.13.refs_6_ = bf16[32,1024]{1,0:T(8,128)(2,1)S(1)} collective-permute-done((bf16[32,1024]{1,0:T(8,128)(2,1)S(1)}, bf16[32,1024]{1,0:T(8,128)(2,1)S(1)}, u32[]{:S(2)}, u32[]{:S(2)}) %collective-permute-start.13) | collective-permute-done | bytes 65568 | tf_op jit(solution)/shard_map/ppermute | solution.py:90
  50.6 2.1 %collective-permute-done.15.refs_7_ = bf16[32,1024]{1,0:T(8,128)(2,1)S(1)} collective-permute-done((bf16[32,1024]{1,0:T(8,128)(2,1)S(1)}, bf16[32,1024]{1,0:T(8,128)(2,1)S(1)}, u32[]{:S(2)}, u32[]{:S(2)}) %collective-permute-start.15) | collective-permute-done | bytes 65568 | tf_op jit(solution)/shard_map/ppermute | solution.py:90
  52.7 0.7 %shard_map.70 = bf16[32,1024]{1,0:T(8,128)(2,1)} custom-call(bf16[32,1024]{1,0:T(8,128)(2,1)S(1)} %shard_map.66.refs_0_, bf16[32,1024]{1,0:T(8,128)(2,1)S(1)} %collective-permute-done.5.refs_1_, bf16[32,1024]{1,0:T(8,128)(2,1)S(1)} %collective-permute-done.6.refs_2_, bf16[32,1024]{1,0:T(8,128)(2,1)S(1)} %collective-permute-done.7.refs_3_, ...), custom_call_target="tpu_custom_call" | custom-call | bytes 2000000 | tf_op jit(solution)/shard_map/pallas_call | solution.py:154
  (21 shorter events, 0.1 us)
Async XLA Ops:
  0.0 10.4 %collective-permute-start.3 = (bf16[2,3584,128]{2,1,0:T(8,128)(2,1)}, bf16[2,3584,128]{2,1,0:T(8,128)(2,1)S(1)}, u32[]{:S(2)}, u32[]{:S(2)}) collective-permute-start(bf16[2,3584,128]{2,1,0:T(8,128)(2,1)} %own_ref.1), channel_id=1, source_target_pairs={{0,1},{1,0},{2,3},{3,2},{4,5},{5,4},{6,7},{7,6},{8,9},{9,8},{10,11... | collective-permute-start | bytes 5505032 | tf_op jit(solution)/shard_map/ppermute | solution.py:90
  0.5 12.1 %collective-permute-start.4 = (bf16[2,128,1024]{2,1,0:T(8,128)(2,1)}, bf16[2,128,1024]{2,1,0:T(8,128)(2,1)S(1)}, u32[]{:S(2)}, u32[]{:S(2)}) collective-permute-start(bf16[2,128,1024]{2,1,0:T(8,128)(2,1)} %refs_3_.7), channel_id=1, source_target_pairs={{0,1},{1,0},{2,3},{3,2},{4,5},{5,4},{6,7},{7,6},{8,9},{9,8},{10,11... | collective-permute-start | bytes 1572872 | tf_op jit(solution)/shard_map/ppermute | solution.py:90
  0.5 0.9 %copy-start.4 = (bf16[32,3584]{1,0:T(8,128)(2,1)S(1)}, bf16[32,3584]{1,0:T(8,128)(2,1)}, u32[]{:S(2)}) copy-start(bf16[32,3584]{1,0:T(8,128)(2,1)} %tokens_ref.1) | copy-start | bytes 688132
  1.5 0.7 %copy-start.5 = (s32[32,8]{0,1:T(8,128)S(1)}, s32[32,8]{0,1:T(8,128)}, u32[]{:S(2)}) copy-start(s32[32,8]{0,1:T(8,128)} %param.7) | copy-start | bytes 3076
  2.1 0.7 %copy-start.6 = (s32[32,8]{0,1:T(8,128)S(1)}, s32[32,8]{0,1:T(8,128)}, u32[]{:S(2)}) copy-start(s32[32,8]{0,1:T(8,128)} %param.8) | copy-start | bytes 3076
  3.2 9.4 %copy-start = (bf16[3584,1024]{1,0:T(8,128)(2,1)S(1)}, bf16[3584,1024]{1,0:T(8,128)(2,1)}, u32[]{:S(2)}) copy-start(bf16[3584,1024]{1,0:T(8,128)(2,1)} %refs_1_.3) | copy-start | bytes 22020100
  3.2 12.7 %collective-permute-start = (bf16[32,3712]{1,0:T(8,128)(2,1)S(1)}, bf16[32,3712]{1,0:T(8,128)(2,1)S(1)}, u32[]{:S(2)}, u32[]{:S(2)}) collective-permute-start(bf16[32,3712]{1,0:T(8,128)(2,1)S(1)} %shard_map.64.refs_0_), channel_id=1, source_target_pairs={{0,2},{1,3},{2,0},{3,1},{4,6},{5,7},{6,4},{7,5},{8,10},{9,11},{10,... | collective-permute-start | bytes 712712 | tf_op jit(solution)/shard_map/ppermute | solution.py:90
  6.2 12.4 %collective-permute-start.1 = (bf16[32,3712]{1,0:T(8,128)(2,1)S(1)}, bf16[32,3712]{1,0:T(8,128)(2,1)S(1)}, u32[]{:S(2)}, u32[]{:S(2)}) collective-permute-start(bf16[32,3712]{1,0:T(8,128)(2,1)S(1)} %shard_map.64.refs_0_), channel_id=1, source_target_pairs={{0,4},{1,5},{2,6},{3,7},{4,0},{5,1},{6,2},{7,3},{8,12},{9,13},{10,... | collective-permute-start | bytes 712712 | tf_op jit(solution)/shard_map/ppermute | solution.py:90
  7.8 13.2 %collective-permute-start.2 = (bf16[32,3712]{1,0:T(8,128)(2,1)S(1)}, bf16[32,3712]{1,0:T(8,128)(2,1)S(1)}, u32[]{:S(2)}, u32[]{:S(2)}) collective-permute-start(bf16[32,3712]{1,0:T(8,128)(2,1)S(1)} %shard_map.64.refs_0_), channel_id=1, source_target_pairs={{0,8},{1,9},{2,10},{3,11},{4,12},{5,13},{6,14},{7,15},{8,0},{9,1},... | collective-permute-start | bytes 712712 | tf_op jit(solution)/shard_map/ppermute | solution.py:90
  10.4 1.5 %copy-start.3 = (bf16[2,3584,128]{2,1,0:T(8,128)(2,1)S(1)}, bf16[2,3584,128]{2,1,0:T(8,128)(2,1)}, u32[]{:S(2)}) copy-start(bf16[2,3584,128]{2,1,0:T(8,128)(2,1)} %own_ref.1) | copy-start | bytes 5505028
  12.5 1.0 %copy-start.1 = (bf16[2,128,1024]{2,1,0:T(8,128)(2,1)S(1)}, bf16[2,128,1024]{2,1,0:T(8,128)(2,1)}, u32[]{:S(2)}) copy-start(bf16[2,128,1024]{2,1,0:T(8,128)(2,1)} %refs_3_.7) | copy-start | bytes 1572868
  13.6 16.5 %copy-start.2 = (bf16[2,128,1024]{2,1,0:T(8,128)(2,1)S(1)}, bf16[2,128,1024]{2,1,0:T(8,128)(2,1)}, u32[]{:S(2)}) copy-start(bf16[2,128,1024]{2,1,0:T(8,128)(2,1)} %refs_3_.7) | copy-start | bytes 1572868
  21.0 6.9 %collective-permute-start.9 = (bf16[32,3712]{1,0:T(8,128)(2,1)S(1)}, bf16[32,3712]{1,0:T(8,128)(2,1)S(1)}, u32[]{:S(2)}, u32[]{:S(2)}) collective-permute-start(bf16[32,3712]{1,0:T(8,128)(2,1)S(1)} %collective-permute-done.2.refs_2_), channel_id=1, source_target_pairs={{0,2},{1,3},{2,0},{3,1},{4,6},{5,7},{6,4},{7,5},{8,10},{9,11},{10,... | collective-permute-start | bytes 712712 | tf_op jit(solution)/shard_map/ppermute | solution.py:90
  21.5 12.7 %collective-permute-start.10 = (bf16[32,3712]{1,0:T(8,128)(2,1)S(1)}, bf16[32,3712]{1,0:T(8,128)(2,1)S(1)}, u32[]{:S(2)}, u32[]{:S(2)}) collective-permute-start(bf16[32,3712]{1,0:T(8,128)(2,1)S(1)} %collective-permute-done.2.refs_2_), channel_id=1, source_target_pairs={{0,4},{1,5},{2,6},{3,7},{4,0},{5,1},{6,2},{7,3},{8,12},{9,13},{10,... | collective-permute-start | bytes 712712 | tf_op jit(solution)/shard_map/ppermute | solution.py:90
  21.9 13.4 %collective-permute-start.8 = (bf16[32,3712]{1,0:T(8,128)(2,1)S(1)}, bf16[32,3712]{1,0:T(8,128)(2,1)S(1)}, u32[]{:S(2)}, u32[]{:S(2)}) collective-permute-start(bf16[32,3712]{1,0:T(8,128)(2,1)S(1)} %collective-permute-done.1.refs_1_), channel_id=1, source_target_pairs={{0,2},{1,3},{2,0},{3,1},{4,6},{5,7},{6,4},{7,5},{8,10},{9,11},{10,... | collective-permute-start | bytes 712712 | tf_op jit(solution)/shard_map/ppermute | solution.py:90
  27.8 12.0 %collective-permute-start.14 = (bf16[32,3712]{1,0:T(8,128)(2,1)S(1)}, bf16[32,3712]{1,0:T(8,128)(2,1)S(1)}, u32[]{:S(2)}, u32[]{:S(2)}) collective-permute-start(bf16[32,3712]{1,0:T(8,128)(2,1)S(1)} %collective-permute-done.9.refs_1_), channel_id=1, source_target_pairs={{0,4},{1,5},{2,6},{3,7},{4,0},{5,1},{6,2},{7,3},{8,12},{9,13},{10,... | collective-permute-start | bytes 712712 | tf_op jit(solution)/shard_map/ppermute | solution.py:90
  32.8 11.5 %collective-permute-start.5 = (bf16[32,1024]{1,0:T(8,128)(2,1)S(1)}, bf16[32,1024]{1,0:T(8,128)(2,1)S(1)}, u32[]{:S(2)}, u32[]{:S(2)}) collective-permute-start(bf16[32,1024]{1,0:T(8,128)(2,1)S(1)} %get-tuple-element.19), channel_id=1, source_target_pairs={{0,2},{1,3},{2,0},{3,1},{4,6},{5,7},{6,4},{7,5},{8,10},{9,11},{10,... | collective-permute-start | bytes 196616 | tf_op jit(solution)/shard_map/ppermute | solution.py:90
  33.4 12.4 %collective-permute-start.6 = (bf16[32,1024]{1,0:T(8,128)(2,1)S(1)}, bf16[32,1024]{1,0:T(8,128)(2,1)S(1)}, u32[]{:S(2)}, u32[]{:S(2)}) collective-permute-start(bf16[32,1024]{1,0:T(8,128)(2,1)S(1)} %get-tuple-element.20), channel_id=1, source_target_pairs={{0,4},{1,5},{2,6},{3,7},{4,0},{5,1},{6,2},{7,3},{8,12},{9,13},{10,... | collective-permute-start | bytes 196616 | tf_op jit(solution)/shard_map/ppermute | solution.py:90
  34.1 15.1 %collective-permute-start.7 = (bf16[32,1024]{1,0:T(8,128)(2,1)S(1)}, bf16[32,1024]{1,0:T(8,128)(2,1)S(1)}, u32[]{:S(2)}, u32[]{:S(2)}) collective-permute-start(bf16[32,1024]{1,0:T(8,128)(2,1)S(1)} %get-tuple-element.21), channel_id=1, source_target_pairs={{0,8},{1,9},{2,10},{3,11},{4,12},{5,13},{6,14},{7,15},{8,0},{9,1},... | collective-permute-start | bytes 196616 | tf_op jit(solution)/shard_map/ppermute | solution.py:90
  38.0 11.2 %collective-permute-start.11 = (bf16[32,1024]{1,0:T(8,128)(2,1)S(1)}, bf16[32,1024]{1,0:T(8,128)(2,1)S(1)}, u32[]{:S(2)}, u32[]{:S(2)}) collective-permute-start(bf16[32,1024]{1,0:T(8,128)(2,1)S(1)} %get-tuple-element.22), channel_id=1, source_target_pairs={{0,6},{1,7},{2,4},{3,5},{4,2},{5,3},{6,0},{7,1},{8,14},{9,15},{10,... | collective-permute-start | bytes 196616 | tf_op jit(solution)/shard_map/ppermute | solution.py:90
  39.8 9.4 %collective-permute-start.12 = (bf16[32,1024]{1,0:T(8,128)(2,1)S(1)}, bf16[32,1024]{1,0:T(8,128)(2,1)S(1)}, u32[]{:S(2)}, u32[]{:S(2)}) collective-permute-start(bf16[32,1024]{1,0:T(8,128)(2,1)S(1)} %get-tuple-element.23), channel_id=1, source_target_pairs={{0,10},{1,11},{2,8},{3,9},{4,14},{5,15},{6,12},{7,13},{8,2},{9,3},... | collective-permute-start | bytes 196616 | tf_op jit(solution)/shard_map/ppermute | solution.py:90
  44.4 6.2 %collective-permute-start.13 = (bf16[32,1024]{1,0:T(8,128)(2,1)S(1)}, bf16[32,1024]{1,0:T(8,128)(2,1)S(1)}, u32[]{:S(2)}, u32[]{:S(2)}) collective-permute-start(bf16[32,1024]{1,0:T(8,128)(2,1)S(1)} %get-tuple-element.24), channel_id=1, source_target_pairs={{0,12},{1,13},{2,14},{3,15},{4,8},{5,9},{6,10},{7,11},{8,4},{9,5},... | collective-permute-start | bytes 196616 | tf_op jit(solution)/shard_map/ppermute | solution.py:90
  45.8 7.0 %collective-permute-start.15 = (bf16[32,1024]{1,0:T(8,128)(2,1)S(1)}, bf16[32,1024]{1,0:T(8,128)(2,1)S(1)}, u32[]{:S(2)}, u32[]{:S(2)}) collective-permute-start(bf16[32,1024]{1,0:T(8,128)(2,1)S(1)} %shard_map.69), channel_id=1, source_target_pairs={{0,14},{1,15},{2,12},{3,13},{4,10},{5,11},{6,8},{7,9},{8,6},{9,7},... | collective-permute-start | bytes 196616 | tf_op jit(solution)/shard_map/ppermute | solution.py:90

commit v3 on v2

--- a/solution.py
+++ b/solution.py
@@ -6,32 +6,24 @@
 from jax.experimental.pallas import tpu as pltpu
 from jax.sharding import PartitionSpec as P
 
-gate_levels = 16.0
+levels = 16
 lanes = 128
 most = 8
 vmem = pl.BlockSpec(memory_space=pltpu.VMEM)
 
 
-def pack_body(tokens_ref, routes_ref, codes_ref, out_ref, routes_buf, codes_buf, sems):
+def pack_body(tokens_ref, marks_ref, out_ref):
     rows, features = tokens_ref.shape
     width = out_ref.shape[1] - features
-    copies = [
-        pltpu.make_async_copy(routes_ref, routes_buf, sems.at[0]),
-        pltpu.make_async_copy(codes_ref, codes_buf, sems.at[1]),
-        pltpu.make_async_copy(tokens_ref, out_ref.at[:, pl.ds(0, features)], sems.at[2]),
-    ]
-    for copy in copies:
-        copy.start()
-    copies[0].wait()
-    copies[1].wait()
+    out_ref[:, :features] = tokens_ref[...]
     lane = lax.broadcasted_iota(jnp.int32, (rows, width), 1)
-    routes = routes_buf[...].T
-    weights = (codes_buf[...].astype(jnp.float32).T + 1.0) / gate_levels
+    marks = marks_ref[...].T
+    routes = marks // levels
+    weights = (marks % levels + 1).astype(jnp.float32) / levels
     gates = jnp.zeros((rows, width), jnp.float32)
-    for k in range(routes.shape[1]):
+    for k in range(marks.shape[1]):
         gates = gates + jnp.where(routes[:, k : k + 1] == lane, weights[:, k : k + 1], 0.0)
     out_ref[:, features:] = gates.astype(out_ref.dtype)
-    copies[2].wait()
 
 
 def weave_body(own_ref, peer_ref, out_ref):
@@ -115,42 +107,46 @@
         )(*blocks, base_weight, down, delta_out, up_peer)
 
     down_peer, up_peer = exchange(delta_in, 1), exchange(delta_out, 1)
-    packed = pl.pallas_call(
-        pack_body,
-        out_shape=jax.ShapeDtypeStruct((rows, features + width), tokens.dtype),
-        in_specs=[pl.BlockSpec(memory_space=pltpu.HBM)] * 3,
-        out_specs=vmem,
-        scratch_shapes=[
-            pltpu.VMEM(routes.shape[::-1], jnp.int32),
-            pltpu.VMEM(routes.shape[::-1], jnp.int32),
-            pltpu.SemaphoreType.DMA((3,)),
-        ],
-        compiler_params=pltpu.CompilerParams(vmem_limit_bytes=4 << 20),
-        cost_estimate=pl.CostEstimate(flops=0, bytes_accessed=2000000, transcendentals=0),
-    )(tokens, routes.T, gate_code.T)
+    marks = routes.T * levels + gate_code.T
+    packed = small(pack_body, (rows, features + width), 2, 4, 2000000)(tokens, marks)
     down = small(weave_body, (features, 2 * local * rank), 2, 9, 4000000)(delta_in, down_peer)
 
-    held = {0: packed}
-    partial = list(experts_on([packed]))
-    for stage in range(1, chips.bit_length()):
-        if stage == 2:
-            firsts = [m for m in held if m]
-            *blocks, partial[0] = lax.optimization_barrier([*(held[m] for m in firsts), partial[0]])
-            held.update(zip(firsts, blocks))
-        for m in range(chips):
-            if m.bit_count() == stage:
-                high = m & -minor
-                rest = m if high == m or high.bit_count() > 1 else m ^ high
-                hop = rest & -rest
-                if high.bit_count() > 1:
-                    hop = high & -high
-                held[m] = exchange(held[m ^ hop], 2 * hop)
-    for stage in range(1, chips.bit_length()):
-        masks = [m for m in range(chips) if m.bit_count() == stage]
+    stages = chips.bit_length()
+    of = [[m for m in range(chips - 1, -1, -1) if m.bit_count() == s] for s in range(stages)]
+
+    def hop_of(m):
+        high = m & -minor
+        rest = high if high == m or high.bit_count() > 1 else m ^ high
+        return rest & -rest
+
+    held, parts, home = {0: packed}, {}, {}
+
+    def tie(*stores):
+        keys = [(store, m) for store, masks in stores for m in masks]
+        for (store, m), value in zip(keys, lax.optimization_barrier([s[m] for s, m in keys])):
+            store[m] = value
+
+    def compute(masks):
         for at in range(0, len(masks), most):
             some = masks[at : at + most]
-            for m, part in zip(some, experts_on([held[m] for m in some])):
-                partial.append(exchange(part, 2 * m))
+            parts.update(zip(some, experts_on([held[m] for m in some])))
+
+    def send_home(masks):
+        home.update((m, exchange(parts[m], 2 * m) if m else parts[m]) for m in masks)
+
+    for stage in range(1, stages):
+        sources = sorted({m ^ hop_of(m) for m in of[stage]}, reverse=True)
+        if stage >= 2:
+            tie((held, sources), (parts, of[stage - 2]))
+            send_home(of[stage - 2])
+        for m in of[stage]:
+            held[m] = exchange(held[m ^ hop_of(m)], 2 * hop_of(m))
+        compute(of[stage - 1])
+    tie((held, of[-1]), (home, of[-3]), (parts, of[-2]))
+    compute(of[-1])
+    tie((parts, of[-2] + of[-1]))
+    send_home(of[-2] + of[-1])
+    partial = list(home.values())
     return small(sum_body, (rows, hidden_units), chips, 8, 2000000)(*partial)
 
 

time: 53.7 us -> 51 us (0.950)
  waiting for transfers between devices: 13 us -> 8.44 us
  starting transfers between devices: 23.8 us -> 26.5 us
  local copies, waits for them, and re-layouts: 4.86 us -> 3.48 us
  other arithmetic: 0 us -> 0.71 us
    ppermute x16, waiting for transfers between devices: 13 us -> 8.44 us  [exchange(): lax.ppermute(value, 'expert', [(i, i ^ mask) for i in range(devices_count)])]
    ppermute x16, starting transfers between devices: 23.8 us -> 26.5 us  [exchange(): lax.ppermute(value, 'expert', [(i, i ^ mask) for i in range(devices_count)])]
    unnamed x14 -> x10, local copies, waits for them, and re-layouts: 4.86 us -> 3.48 us
    add x0 -> x1, other arithmetic: none -> 0.71 us  [shards(): marks = routes.T * levels + gate_code.T]
  transfers between devices with their start and end apart: 16 -> 16, of which waited for: 5 -> 7; matrix products, arithmetic and copies ran while one was open for 0% -> 1% of each run, Pallas kernels for 21% -> 17%
where the time goes in v3:
time: 51 us; the launch traced here: 50.8 us
  starting transfers between devices  26.5 us (52%)
  Pallas kernels  11.6 us (23%)
  waiting for transfers between devices  8.44 us (17%)
  local copies, waits for them, and re-layouts  3.48 us (7%)
  other arithmetic  0.71 us (1%)
    ppermute x16, starting transfers between devices, exchange(): lax.ppermute(value, 'expert', [(i, i ^ mask) for i in range(devices_count)])  26.5 us
    pallas_call x4, Pallas kernels, experts_on(): pl.pallas_call(functools.partial(expert_body, features, count), out_shape...  10 us
    ppermute x16, waiting for transfers between devices, exchange(): lax.ppermute(value, 'expert', [(i, i ^ mask) for i in range(devices_count)])  8.44 us
    unnamed x10, local copies, waits for them, and re-layouts  3.48 us
  transfers between devices with their start and end apart: 16, of which 7 were waited for; matrix products, arithmetic and copies ran while one was open for 1% of the time, Pallas kernels for 17%

profile of v3, /device:TPU:0, one launch (start us, length us, event | category | flops | bytes accessed | tf_op | source)
XLA Modules:
  0.0 50.8 jit_solution(718889895127647251)
XLA Ops:
  0.0 0.5 collective-permute-start.2
  0.5 0.7 %add_bitcast_fusion.marks_ref = s32[8,32]{1,0:T(8,128)S(1)} fusion(s32[32,8]{0,1:T(8,128)} %param.8, s32[32,8]{0,1:T(8,128)} %param.7), kind=kLoop, calls=%fused_computation | loop fusion | flops 512 | bytes 3072 | tf_op jit(solution)/shard_map/add | solution.py:110
  1.2 0.9 %copy-done.4 = bf16[32,3584]{1,0:T(8,128)(2,1)S(1)} copy-done((bf16[32,3584]{1,0:T(8,128)(2,1)S(1)}, bf16[32,3584]{1,0:T(8,128)(2,1)}, u32[]{:S(2)}) %copy-start.4) | copy-done | bytes 229400
  2.2 0.2 shard_map.64.refs_0_
  2.4 4.1 %collective-permute-start = (bf16[32,3712]{1,0:T(8,128)(2,1)S(1)}, bf16[32,3712]{1,0:T(8,128)(2,1)S(1)}, u32[]{:S(2)}, u32[]{:S(2)}) collective-permute-start(bf16[32,3712]{1,0:T(8,128)(2,1)S(1)} %shard_map.64.refs_0_), channel_id=1, source_target_pairs={{0,8},{1,9},{2,10},{3,11},{4,12},{5,13},{6,14},{7,15},{8,0},{9,1},... | collective-permute-start | bytes 712712 | tf_op jit(solution)/shard_map/ppermute | solution.py:82
  6.5 1.6 %collective-permute-start.1 = (bf16[32,3712]{1,0:T(8,128)(2,1)S(1)}, bf16[32,3712]{1,0:T(8,128)(2,1)S(1)}, u32[]{:S(2)}, u32[]{:S(2)}) collective-permute-start(bf16[32,3712]{1,0:T(8,128)(2,1)S(1)} %shard_map.64.refs_0_), channel_id=1, source_target_pairs={{0,4},{1,5},{2,6},{3,7},{4,0},{5,1},{6,2},{7,3},{8,12},{9,13},{10,... | collective-permute-start | bytes 712712 | tf_op jit(solution)/shard_map/ppermute | solution.py:82
  8.1 1.5 %collective-permute-start.5 = (bf16[32,3712]{1,0:T(8,128)(2,1)S(1)}, bf16[32,3712]{1,0:T(8,128)(2,1)S(1)}, u32[]{:S(2)}, u32[]{:S(2)}) collective-permute-start(bf16[32,3712]{1,0:T(8,128)(2,1)S(1)} %shard_map.64.refs_0_), channel_id=1, source_target_pairs={{0,2},{1,3},{2,0},{3,1},{4,6},{5,7},{6,4},{7,5},{8,10},{9,11},{10,... | collective-permute-start | bytes 712712 | tf_op jit(solution)/shard_map/ppermute | solution.py:82
  9.6 1.5 %copy-done.3 = bf16[2,3584,128]{2,1,0:T(8,128)(2,1)S(1)} copy-done((bf16[2,3584,128]{2,1,0:T(8,128)(2,1)S(1)}, bf16[2,3584,128]{2,1,0:T(8,128)(2,1)}, u32[]{:S(2)}) %copy-start.3) | copy-done | bytes 1835032
  11.1 0.6 %shard_map.65.refs_2_.refs_4_ = bf16[3584,512]{1,0:T(8,128)(2,1)S(1)} custom-call(bf16[2,3584,128]{2,1,0:T(8,128)(2,1)S(1)} %copy-done.3, bf16[2,3584,128]{2,1,0:T(8,128)(2,1)S(1)} %collective-permute-done.2.peer_ref), custom_call_target="tpu_custom_call" | custom-call | bytes 4000000 | tf_op jit(solution)/shard_map/pallas_call | solution.py:112
  11.8 1.0 %copy-done.1 = bf16[2,128,1024]{2,1,0:T(8,128)(2,1)S(1)} copy-done((bf16[2,128,1024]{2,1,0:T(8,128)(2,1)S(1)}, bf16[2,128,1024]{2,1,0:T(8,128)(2,1)}, u32[]{:S(2)}) %copy-start.1) | copy-done | bytes 524312
  12.8 2.3 %shard_map.66.refs_0_ = bf16[32,1024]{1,0:T(8,128)(2,1)S(1)} custom-call(bf16[32,3712]{1,0:T(8,128)(2,1)S(1)} %shard_map.64.refs_0_, bf16[3584,1024]{1,0:T(8,128)(2,1)S(1)} %copy-done, bf16[3584,512]{1,0:T(8,128)(2,1)S(1)} %shard_map.65.refs_2_.refs_4_, bf16[2,128,1024]{2,1,0:T(8,128)(2,1)S(1)} %copy-done.1, ...), custom_call_target="tpu_custom_call" | custom-call | flops 352321536 | bytes 9000000 | tf_op jit(solution)/shard_map/pallas_call | solution.py:96
  15.1 2.5 %collective-permute-done.refs_0_ = bf16[32,3712]{1,0:T(8,128)(2,1)S(1)} collective-permute-done((bf16[32,3712]{1,0:T(8,128)(2,1)S(1)}, bf16[32,3712]{1,0:T(8,128)(2,1)S(1)}, u32[]{:S(2)}, u32[]{:S(2)}) %collective-permute-start) | collective-permute-done | bytes 237600 | tf_op jit(solution)/shard_map/ppermute | solution.py:82
  17.7 0.2 collective-permute-done.1.refs_1_
  17.9 1.6 %collective-permute-start.4 = (bf16[32,3712]{1,0:T(8,128)(2,1)S(1)}, bf16[32,3712]{1,0:T(8,128)(2,1)S(1)}, u32[]{:S(2)}, u32[]{:S(2)}) collective-permute-start(bf16[32,3712]{1,0:T(8,128)(2,1)S(1)} %collective-permute-done.refs_0_), channel_id=1, source_target_pairs={{0,2},{1,3},{2,0},{3,1},{4,6},{5,7},{6,4},{7,5},{8,10},{9,11},{10,... | collective-permute-start | bytes 712712 | tf_op jit(solution)/shard_map/ppermute | solution.py:82
  19.4 1.4 %collective-permute-start.10 = (bf16[32,3712]{1,0:T(8,128)(2,1)S(1)}, bf16[32,3712]{1,0:T(8,128)(2,1)S(1)}, u32[]{:S(2)}, u32[]{:S(2)}) collective-permute-start(bf16[32,3712]{1,0:T(8,128)(2,1)S(1)} %collective-permute-done.refs_0_), channel_id=1, source_target_pairs={{0,4},{1,5},{2,6},{3,7},{4,0},{5,1},{6,2},{7,3},{8,12},{9,13},{10,... | collective-permute-start | bytes 712712 | tf_op jit(solution)/shard_map/ppermute | solution.py:82
  20.9 0.5 collective-permute-start.11
  21.4 2.7 %shard_map.67 = (bf16[32,1024]{1,0:T(8,128)(2,1)S(1)}, bf16[32,1024]{1,0:T(8,128)(2,1)S(1)}, bf16[32,1024]{1,0:T(8,128)(2,1)S(1)}) custom-call(bf16[32,3712]{1,0:T(8,128)(2,1)S(1)} %collective-permute-done.refs_0_, bf16[32,3712]{1,0:T(8,128)(2,1)S(1)} %collective-permute-done.1.refs_1_, bf16[32,3712]{1,0:T(8,128)(2,1)S(1)} %collective-permute-done.5.refs_2_, ...), custom_call_target="tpu_custom_call" | custom-call | flops 1056964608 | bytes 9000000 | tf_op jit(solution)/shard_map/pallas_call | solution.py:96
  24.1 2.5 %collective-permute-done.4.refs_1_ = bf16[32,3712]{1,0:T(8,128)(2,1)S(1)} collective-permute-done((bf16[32,3712]{1,0:T(8,128)(2,1)S(1)}, bf16[32,3712]{1,0:T(8,128)(2,1)S(1)}, u32[]{:S(2)}, u32[]{:S(2)}) %collective-permute-start.4) | collective-permute-done | bytes 237600 | tf_op jit(solution)/shard_map/ppermute | solution.py:82
  26.6 1.5 %collective-permute-start.6 = (bf16[32,3712]{1,0:T(8,128)(2,1)S(1)}, bf16[32,3712]{1,0:T(8,128)(2,1)S(1)}, u32[]{:S(2)}, u32[]{:S(2)}) collective-permute-start(bf16[32,3712]{1,0:T(8,128)(2,1)S(1)} %collective-permute-done.4.refs_1_), channel_id=1, source_target_pairs={{0,4},{1,5},{2,6},{3,7},{4,0},{5,1},{6,2},{7,3},{8,12},{9,13},{10,... | collective-permute-start | bytes 712712 | tf_op jit(solution)/shard_map/ppermute | solution.py:82
  28.1 2.2 %collective-permute-start.7 = (bf16[32,1024]{1,0:T(8,128)(2,1)S(1)}, bf16[32,1024]{1,0:T(8,128)(2,1)S(1)}, u32[]{:S(2)}, u32[]{:S(2)}) collective-permute-start(bf16[32,1024]{1,0:T(8,128)(2,1)S(1)} %get-tuple-element.36), channel_id=1, source_target_pairs={{0,8},{1,9},{2,10},{3,11},{4,12},{5,13},{6,14},{7,15},{8,0},{9,1},... | collective-permute-start | bytes 196616 | tf_op jit(solution)/shard_map/ppermute | solution.py:82
  30.3 1.5 %collective-permute-start.9 = (bf16[32,1024]{1,0:T(8,128)(2,1)S(1)}, bf16[32,1024]{1,0:T(8,128)(2,1)S(1)}, u32[]{:S(2)}, u32[]{:S(2)}) collective-permute-start(bf16[32,1024]{1,0:T(8,128)(2,1)S(1)} %get-tuple-element.38), channel_id=1, source_target_pairs={{0,2},{1,3},{2,0},{3,1},{4,6},{5,7},{6,4},{7,5},{8,10},{9,11},{10,... | collective-permute-start | bytes 196616 | tf_op jit(solution)/shard_map/ppermute | solution.py:82
  31.8 2.7 %shard_map.68 = (bf16[32,1024]{1,0:T(8,128)(2,1)S(1)}, bf16[32,1024]{1,0:T(8,128)(2,1)S(1)}, bf16[32,1024]{1,0:T(8,128)(2,1)S(1)}) custom-call(bf16[32,3712]{1,0:T(8,128)(2,1)S(1)} %collective-permute-done.10.refs_0_, bf16[32,3712]{1,0:T(8,128)(2,1)S(1)} %collective-permute-done.4.refs_1_, bf16[32,3712]{1,0:T(8,128)(2,1)S(1)} %collective-permute-done.11.refs_2_, ...), custom_call_target="tpu_custom_call" | custom-call | flops 1056964608 | bytes 9000000 | tf_op jit(solution)/shard_map/pallas_call | solution.py:96
  34.5 0.3 collective-permute-done.8.refs_2_
  34.8 2.3 %shard_map.69 = bf16[32,1024]{1,0:T(8,128)(2,1)S(1)} custom-call(bf16[32,3712]{1,0:T(8,128)(2,1)S(1)} %collective-permute-done.6.refs_0_, bf16[3584,1024]{1,0:T(8,128)(2,1)S(1)} %copy-done, bf16[3584,512]{1,0:T(8,128)(2,1)S(1)} %shard_map.65.refs_2_.refs_4_, bf16[2,128,1024]{2,1,0:T(8,128)(2,1)S(1)} %copy-done.2, ...), custom_call_target="tpu_custom_call" | custom-call | flops 352321536 | bytes 9000000 | tf_op jit(solution)/shard_map/pallas_call | solution.py:96
  37.1 3.8 %collective-permute-start.12 = (bf16[32,1024]{1,0:T(8,128)(2,1)S(1)}, bf16[32,1024]{1,0:T(8,128)(2,1)S(1)}, u32[]{:S(2)}, u32[]{:S(2)}) collective-permute-start(bf16[32,1024]{1,0:T(8,128)(2,1)S(1)} %get-tuple-element.49), channel_id=1, source_target_pairs={{0,12},{1,13},{2,14},{3,15},{4,8},{5,9},{6,10},{7,11},{8,4},{9,5},... | collective-permute-start | bytes 196616 | tf_op jit(solution)/shard_map/ppermute | solution.py:82
  40.9 0.5 %collective-permute-start.13 = (bf16[32,1024]{1,0:T(8,128)(2,1)S(1)}, bf16[32,1024]{1,0:T(8,128)(2,1)S(1)}, u32[]{:S(2)}, u32[]{:S(2)}) collective-permute-start(bf16[32,1024]{1,0:T(8,128)(2,1)S(1)} %get-tuple-element.50), channel_id=1, source_target_pairs={{0,10},{1,11},{2,8},{3,9},{4,14},{5,15},{6,12},{7,13},{8,2},{9,3},... | collective-permute-start | bytes 196616 | tf_op jit(solution)/shard_map/ppermute | solution.py:82
  41.4 1.1 %collective-permute-start.14 = (bf16[32,1024]{1,0:T(8,128)(2,1)S(1)}, bf16[32,1024]{1,0:T(8,128)(2,1)S(1)}, u32[]{:S(2)}, u32[]{:S(2)}) collective-permute-start(bf16[32,1024]{1,0:T(8,128)(2,1)S(1)} %get-tuple-element.51), channel_id=1, source_target_pairs={{0,6},{1,7},{2,4},{3,5},{4,2},{5,3},{6,0},{7,1},{8,14},{9,15},{10,... | collective-permute-start | bytes 196616 | tf_op jit(solution)/shard_map/ppermute | solution.py:82
  42.5 4.6 %collective-permute-start.15 = (bf16[32,1024]{1,0:T(8,128)(2,1)S(1)}, bf16[32,1024]{1,0:T(8,128)(2,1)S(1)}, u32[]{:S(2)}, u32[]{:S(2)}) collective-permute-start(bf16[32,1024]{1,0:T(8,128)(2,1)S(1)} %shard_map.69), channel_id=1, source_target_pairs={{0,14},{1,15},{2,12},{3,13},{4,10},{5,11},{6,8},{7,9},{8,6},{9,7},... | collective-permute-start | bytes 196616 | tf_op jit(solution)/shard_map/ppermute | solution.py:82
  47.1 0.8 %collective-permute-done.13.refs_5_ = bf16[32,1024]{1,0:T(8,128)(2,1)S(1)} collective-permute-done((bf16[32,1024]{1,0:T(8,128)(2,1)S(1)}, bf16[32,1024]{1,0:T(8,128)(2,1)S(1)}, u32[]{:S(2)}, u32[]{:S(2)}) %collective-permute-start.13) | collective-permute-done | bytes 65568 | tf_op jit(solution)/shard_map/ppermute | solution.py:82
  47.9 0.1 collective-permute-done.14.refs_6_
  48.0 2.1 %collective-permute-done.15.refs_7_ = bf16[32,1024]{1,0:T(8,128)(2,1)S(1)} collective-permute-done((bf16[32,1024]{1,0:T(8,128)(2,1)S(1)}, bf16[32,1024]{1,0:T(8,128)(2,1)S(1)}, u32[]{:S(2)}, u32[]{:S(2)}) %collective-permute-start.15) | collective-permute-done | bytes 65568 | tf_op jit(solution)/shard_map/ppermute | solution.py:82
  50.1 0.7 %shard_map.70 = bf16[32,1024]{1,0:T(8,128)(2,1)} custom-call(bf16[32,1024]{1,0:T(8,128)(2,1)S(1)} %shard_map.66.refs_0_, bf16[32,1024]{1,0:T(8,128)(2,1)S(1)} %collective-permute-done.7.refs_1_, bf16[32,1024]{1,0:T(8,128)(2,1)S(1)} %collective-permute-done.8.refs_2_, bf16[32,1024]{1,0:T(8,128)(2,1)S(1)} %collective-permute-done.9.refs_3_, ...), custom_call_target="tpu_custom_call" | custom-call | bytes 2000000 | tf_op jit(solution)/shard_map/pallas_call | solution.py:150
  (18 shorter events, 0.1 us)
Async XLA Ops:
  0.0 9.6 %collective-permute-start.2 = (bf16[2,3584,128]{2,1,0:T(8,128)(2,1)}, bf16[2,3584,128]{2,1,0:T(8,128)(2,1)S(1)}, u32[]{:S(2)}, u32[]{:S(2)}) collective-permute-start(bf16[2,3584,128]{2,1,0:T(8,128)(2,1)} %own_ref.1), channel_id=1, source_target_pairs={{0,1},{1,0},{2,3},{3,2},{4,5},{5,4},{6,7},{7,6},{8,9},{9,8},{10,11... | collective-permute-start | bytes 5505032 | tf_op jit(solution)/shard_map/ppermute | solution.py:82
  0.5 11.3 %collective-permute-start.3 = (bf16[2,128,1024]{2,1,0:T(8,128)(2,1)}, bf16[2,128,1024]{2,1,0:T(8,128)(2,1)S(1)}, u32[]{:S(2)}, u32[]{:S(2)}) collective-permute-start(bf16[2,128,1024]{2,1,0:T(8,128)(2,1)} %refs_3_.7), channel_id=1, source_target_pairs={{0,1},{1,0},{2,3},{3,2},{4,5},{5,4},{6,7},{7,6},{8,9},{9,8},{10,11... | collective-permute-start | bytes 1572872 | tf_op jit(solution)/shard_map/ppermute | solution.py:82
  1.2 0.9 %copy-start.4 = (bf16[32,3584]{1,0:T(8,128)(2,1)S(1)}, bf16[32,3584]{1,0:T(8,128)(2,1)}, u32[]{:S(2)}) copy-start(bf16[32,3584]{1,0:T(8,128)(2,1)} %tokens_ref.1) | copy-start | bytes 688132
  2.4 9.4 %copy-start = (bf16[3584,1024]{1,0:T(8,128)(2,1)S(1)}, bf16[3584,1024]{1,0:T(8,128)(2,1)}, u32[]{:S(2)}) copy-start(bf16[3584,1024]{1,0:T(8,128)(2,1)} %refs_1_.3) | copy-start | bytes 22020100
  2.4 15.2 %collective-permute-start = (bf16[32,3712]{1,0:T(8,128)(2,1)S(1)}, bf16[32,3712]{1,0:T(8,128)(2,1)S(1)}, u32[]{:S(2)}, u32[]{:S(2)}) collective-permute-start(bf16[32,3712]{1,0:T(8,128)(2,1)S(1)} %shard_map.64.refs_0_), channel_id=1, source_target_pairs={{0,8},{1,9},{2,10},{3,11},{4,12},{5,13},{6,14},{7,15},{8,0},{9,1},... | collective-permute-start | bytes 712712 | tf_op jit(solution)/shard_map/ppermute | solution.py:82
  6.5 11.3 %collective-permute-start.1 = (bf16[32,3712]{1,0:T(8,128)(2,1)S(1)}, bf16[32,3712]{1,0:T(8,128)(2,1)S(1)}, u32[]{:S(2)}, u32[]{:S(2)}) collective-permute-start(bf16[32,3712]{1,0:T(8,128)(2,1)S(1)} %shard_map.64.refs_0_), channel_id=1, source_target_pairs={{0,4},{1,5},{2,6},{3,7},{4,0},{5,1},{6,2},{7,3},{8,12},{9,13},{10,... | collective-permute-start | bytes 712712 | tf_op jit(solution)/shard_map/ppermute | solution.py:82
  8.1 13.3 %collective-permute-start.5 = (bf16[32,3712]{1,0:T(8,128)(2,1)S(1)}, bf16[32,3712]{1,0:T(8,128)(2,1)S(1)}, u32[]{:S(2)}, u32[]{:S(2)}) collective-permute-start(bf16[32,3712]{1,0:T(8,128)(2,1)S(1)} %shard_map.64.refs_0_), channel_id=1, source_target_pairs={{0,2},{1,3},{2,0},{3,1},{4,6},{5,7},{6,4},{7,5},{8,10},{9,11},{10,... | collective-permute-start | bytes 712712 | tf_op jit(solution)/shard_map/ppermute | solution.py:82
  9.6 1.5 %copy-start.3 = (bf16[2,3584,128]{2,1,0:T(8,128)(2,1)S(1)}, bf16[2,3584,128]{2,1,0:T(8,128)(2,1)}, u32[]{:S(2)}) copy-start(bf16[2,3584,128]{2,1,0:T(8,128)(2,1)} %own_ref.1) | copy-start | bytes 5505028
  11.8 1.0 %copy-start.1 = (bf16[2,128,1024]{2,1,0:T(8,128)(2,1)S(1)}, bf16[2,128,1024]{2,1,0:T(8,128)(2,1)}, u32[]{:S(2)}) copy-start(bf16[2,128,1024]{2,1,0:T(8,128)(2,1)} %refs_3_.7) | copy-start | bytes 1572868
  12.8 8.6 %copy-start.2 = (bf16[2,128,1024]{2,1,0:T(8,128)(2,1)S(1)}, bf16[2,128,1024]{2,1,0:T(8,128)(2,1)}, u32[]{:S(2)}) copy-start(bf16[2,128,1024]{2,1,0:T(8,128)(2,1)} %refs_3_.7) | copy-start | bytes 1572868
  17.9 8.7 %collective-permute-start.4 = (bf16[32,3712]{1,0:T(8,128)(2,1)S(1)}, bf16[32,3712]{1,0:T(8,128)(2,1)S(1)}, u32[]{:S(2)}, u32[]{:S(2)}) collective-permute-start(bf16[32,3712]{1,0:T(8,128)(2,1)S(1)} %collective-permute-done.refs_0_), channel_id=1, source_target_pairs={{0,2},{1,3},{2,0},{3,1},{4,6},{5,7},{6,4},{7,5},{8,10},{9,11},{10,... | collective-permute-start | bytes 712712 | tf_op jit(solution)/shard_map/ppermute | solution.py:82
  19.4 10.9 %collective-permute-start.10 = (bf16[32,3712]{1,0:T(8,128)(2,1)S(1)}, bf16[32,3712]{1,0:T(8,128)(2,1)S(1)}, u32[]{:S(2)}, u32[]{:S(2)}) collective-permute-start(bf16[32,3712]{1,0:T(8,128)(2,1)S(1)} %collective-permute-done.refs_0_), channel_id=1, source_target_pairs={{0,4},{1,5},{2,6},{3,7},{4,0},{5,1},{6,2},{7,3},{8,12},{9,13},{10,... | collective-permute-start | bytes 712712 | tf_op jit(solution)/shard_map/ppermute | solution.py:82
  20.9 11.0 %collective-permute-start.11 = (bf16[32,3712]{1,0:T(8,128)(2,1)S(1)}, bf16[32,3712]{1,0:T(8,128)(2,1)S(1)}, u32[]{:S(2)}, u32[]{:S(2)}) collective-permute-start(bf16[32,3712]{1,0:T(8,128)(2,1)S(1)} %collective-permute-done.1.refs_1_), channel_id=1, source_target_pairs={{0,2},{1,3},{2,0},{3,1},{4,6},{5,7},{6,4},{7,5},{8,10},{9,11},{10,... | collective-permute-start | bytes 712712 | tf_op jit(solution)/shard_map/ppermute | solution.py:82
  26.6 8.2 %collective-permute-start.6 = (bf16[32,3712]{1,0:T(8,128)(2,1)S(1)}, bf16[32,3712]{1,0:T(8,128)(2,1)S(1)}, u32[]{:S(2)}, u32[]{:S(2)}) collective-permute-start(bf16[32,3712]{1,0:T(8,128)(2,1)S(1)} %collective-permute-done.4.refs_1_), channel_id=1, source_target_pairs={{0,4},{1,5},{2,6},{3,7},{4,0},{5,1},{6,2},{7,3},{8,12},{9,13},{10,... | collective-permute-start | bytes 712712 | tf_op jit(solution)/shard_map/ppermute | solution.py:82
  28.1 6.5 %collective-permute-start.7 = (bf16[32,1024]{1,0:T(8,128)(2,1)S(1)}, bf16[32,1024]{1,0:T(8,128)(2,1)S(1)}, u32[]{:S(2)}, u32[]{:S(2)}) collective-permute-start(bf16[32,1024]{1,0:T(8,128)(2,1)S(1)} %get-tuple-element.36), channel_id=1, source_target_pairs={{0,8},{1,9},{2,10},{3,11},{4,12},{5,13},{6,14},{7,15},{8,0},{9,1},... | collective-permute-start | bytes 196616 | tf_op jit(solution)/shard_map/ppermute | solution.py:82
  30.3 4.5 %collective-permute-start.8 = (bf16[32,1024]{1,0:T(8,128)(2,1)S(1)}, bf16[32,1024]{1,0:T(8,128)(2,1)S(1)}, u32[]{:S(2)}, u32[]{:S(2)}) collective-permute-start(bf16[32,1024]{1,0:T(8,128)(2,1)S(1)} %get-tuple-element.37), channel_id=1, source_target_pairs={{0,4},{1,5},{2,6},{3,7},{4,0},{5,1},{6,2},{7,3},{8,12},{9,13},{10,... | collective-permute-start | bytes 196616 | tf_op jit(solution)/shard_map/ppermute | solution.py:82
  30.3 4.5 %collective-permute-start.9 = (bf16[32,1024]{1,0:T(8,128)(2,1)S(1)}, bf16[32,1024]{1,0:T(8,128)(2,1)S(1)}, u32[]{:S(2)}, u32[]{:S(2)}) collective-permute-start(bf16[32,1024]{1,0:T(8,128)(2,1)S(1)} %get-tuple-element.38), channel_id=1, source_target_pairs={{0,2},{1,3},{2,0},{3,1},{4,6},{5,7},{6,4},{7,5},{8,10},{9,11},{10,... | collective-permute-start | bytes 196616 | tf_op jit(solution)/shard_map/ppermute | solution.py:82
  37.1 10.0 %collective-permute-start.12 = (bf16[32,1024]{1,0:T(8,128)(2,1)S(1)}, bf16[32,1024]{1,0:T(8,128)(2,1)S(1)}, u32[]{:S(2)}, u32[]{:S(2)}) collective-permute-start(bf16[32,1024]{1,0:T(8,128)(2,1)S(1)} %get-tuple-element.49), channel_id=1, source_target_pairs={{0,12},{1,13},{2,14},{3,15},{4,8},{5,9},{6,10},{7,11},{8,4},{9,5},... | collective-permute-start | bytes 196616 | tf_op jit(solution)/shard_map/ppermute | solution.py:82
  40.9 7.0 %collective-permute-start.13 = (bf16[32,1024]{1,0:T(8,128)(2,1)S(1)}, bf16[32,1024]{1,0:T(8,128)(2,1)S(1)}, u32[]{:S(2)}, u32[]{:S(2)}) collective-permute-start(bf16[32,1024]{1,0:T(8,128)(2,1)S(1)} %get-tuple-element.50), channel_id=1, source_target_pairs={{0,10},{1,11},{2,8},{3,9},{4,14},{5,15},{6,12},{7,13},{8,2},{9,3},... | collective-permute-start | bytes 196616 | tf_op jit(solution)/shard_map/ppermute | solution.py:82
  41.4 6.6 %collective-permute-start.14 = (bf16[32,1024]{1,0:T(8,128)(2,1)S(1)}, bf16[32,1024]{1,0:T(8,128)(2,1)S(1)}, u32[]{:S(2)}, u32[]{:S(2)}) collective-permute-start(bf16[32,1024]{1,0:T(8,128)(2,1)S(1)} %get-tuple-element.51), channel_id=1, source_target_pairs={{0,6},{1,7},{2,4},{3,5},{4,2},{5,3},{6,0},{7,1},{8,14},{9,15},{10,... | collective-permute-start | bytes 196616 | tf_op jit(solution)/shard_map/ppermute | solution.py:82
  42.5 7.6 %collective-permute-start.15 = (bf16[32,1024]{1,0:T(8,128)(2,1)S(1)}, bf16[32,1024]{1,0:T(8,128)(2,1)S(1)}, u32[]{:S(2)}, u32[]{:S(2)}) collective-permute-start(bf16[32,1024]{1,0:T(8,128)(2,1)S(1)} %shard_map.69), channel_id=1, source_target_pairs={{0,14},{1,15},{2,12},{3,13},{4,10},{5,11},{6,8},{7,9},{8,6},{9,7},... | collective-permute-start | bytes 196616 | tf_op jit(solution)/shard_map/ppermute | solution.py:82

commit v4 on v3

--- a/solution.py
+++ b/solution.py
@@ -111,13 +111,17 @@
     packed = small(pack_body, (rows, features + width), 2, 4, 2000000)(tokens, marks)
     down = small(weave_body, (features, 2 * local * rank), 2, 9, 4000000)(delta_in, down_peer)
 
-    stages = chips.bit_length()
-    of = [[m for m in range(chips - 1, -1, -1) if m.bit_count() == s] for s in range(stages)]
+    def hop_of(m):
+        major, low = m & -minor, m & (minor - 1)
+        if major and low:
+            return low if major.bit_count() == 1 else major
+        return m & -m
 
-    def hop_of(m):
-        high = m & -minor
-        rest = high if high == m or high.bit_count() > 1 else m ^ high
-        return rest & -rest
+    def depth(m):
+        return 1 + depth(m ^ hop_of(m)) if m else 0
+
+    stages = 1 + max(depth(m) for m in range(chips))
+    of = [[m for m in range(chips - 1, -1, -1) if depth(m) == s] for s in range(stages)]
 
     held, parts, home = {0: packed}, {}, {}
 
@@ -134,18 +138,28 @@
     def send_home(masks):
         home.update((m, exchange(parts[m], 2 * m) if m else parts[m]) for m in masks)
 
-    for stage in range(1, stages):
-        sources = sorted({m ^ hop_of(m) for m in of[stage]}, reverse=True)
-        if stage >= 2:
-            tie((held, sources), (parts, of[stage - 2]))
-            send_home(of[stage - 2])
-        for m in of[stage]:
+    def fetch(masks):
+        for m in masks:
             held[m] = exchange(held[m ^ hop_of(m)], 2 * hop_of(m))
+
+    fetch(of[1])
+    near = of[1][-1]
+    held[near], down = lax.optimization_barrier((held[near], down))
+    compute(of[0])
+    send_home(of[0])
+    crossing = [m for m in of[2] if hop_of(m) >= minor and m & (minor - 1)]
+    fetch(crossing)
+    tie((held, [m for m in of[1] if m >= minor]), (parts, of[0]))
+    fetch([m for m in of[2] if m not in crossing])
+    compute(of[1])
+    send_home(of[1])
+    for stage in range(3, stages):
+        fetch(of[stage])
         compute(of[stage - 1])
-    tie((held, of[-1]), (home, of[-3]), (parts, of[-2]))
-    compute(of[-1])
-    tie((parts, of[-2] + of[-1]))
-    send_home(of[-2] + of[-1])
+        send_home(of[stage - 1])
+    last = sorted(of[-1], key=lambda m: (m not in crossing, hop_of(m) >= minor, -m))
+    compute(last)
+    send_home(last)
     partial = list(home.values())
     return small(sum_body, (rows, hidden_units), chips, 8, 2000000)(*partial)
 

time: 51 us -> 49 us (0.961)
  waiting for transfers between devices: 8.44 us -> 12.1 us
  starting transfers between devices: 26.5 us -> 23.1 us
  Pallas kernels: 11.6 us -> 9.22 us
    ppermute x16, waiting for transfers between devices: 8.44 us -> 12.1 us  [exchange(): lax.ppermute(value, 'expert', [(i, i ^ mask) for i in range(devices_count)])]
    ppermute x16, starting transfers between devices: 26.5 us -> 23.1 us  [exchange(): lax.ppermute(value, 'expert', [(i, i ^ mask) for i in range(devices_count)])]
    pallas_call x4 -> x3, Pallas kernels: 10 us -> 7.65 us  [experts_on(): pl.pallas_call(functools.partial(expert_body, features, count), out_shape...]
  transfers between devices with their start and end apart: 16 -> 16, of which waited for: 7 -> 4; matrix products, arithmetic and copies ran while one was open for 1% -> 1% of each run, Pallas kernels for 17% -> 17%
where the time goes in v4:
time: 49 us; the launch traced here: 48.7 us
  starting transfers between devices  23.1 us (47%)
  waiting for transfers between devices  12.1 us (25%)
  Pallas kernels  9.22 us (19%)
  local copies, waits for them, and re-layouts  3.49 us (7%)
  other arithmetic  0.71 us (1%)
    ppermute x16, starting transfers between devices, exchange(): lax.ppermute(value, 'expert', [(i, i ^ mask) for i in range(devices_count)])  23.1 us
    ppermute x16, waiting for transfers between devices, exchange(): lax.ppermute(value, 'expert', [(i, i ^ mask) for i in range(devices_count)])  12.1 us
    pallas_call x3, Pallas kernels, experts_on(): pl.pallas_call(functools.partial(expert_body, features, count), out_shape...  7.65 us
    unnamed x10, local copies, waits for them, and re-layouts  3.49 us
  transfers between devices with their start and end apart: 16, of which 4 were waited for; matrix products, arithmetic and copies ran while one was open for 1% of the time, Pallas kernels for 17%

profile of v4, /device:TPU:0, one launch (start us, length us, event | category | flops | bytes accessed | tf_op | source)
XLA Modules:
  0.0 48.7 jit_solution(2446880630690494310)
XLA Ops:
  0.0 0.5 collective-permute-start.1
  0.5 0.1 collective-permute-start.2
  0.5 0.7 %add_bitcast_fusion.marks_ref = s32[8,32]{1,0:T(8,128)S(1)} fusion(s32[32,8]{0,1:T(8,128)} %param.8, s32[32,8]{0,1:T(8,128)} %param.7), kind=kLoop, calls=%fused_computation | loop fusion | flops 512 | bytes 3072 | tf_op jit(solution)/shard_map/add | solution.py:110
  1.2 0.9 %copy-done.4 = bf16[32,3584]{1,0:T(8,128)(2,1)S(1)} copy-done((bf16[32,3584]{1,0:T(8,128)(2,1)S(1)}, bf16[32,3584]{1,0:T(8,128)(2,1)}, u32[]{:S(2)}) %copy-start.4) | copy-done | bytes 229400
  2.2 0.2 shard_map.64.refs_0_
  2.4 0.0 copy-start
  2.4 3.0 %collective-permute-start = (bf16[32,3712]{1,0:T(8,128)(2,1)S(1)}, bf16[32,3712]{1,0:T(8,128)(2,1)S(1)}, u32[]{:S(2)}, u32[]{:S(2)}) collective-permute-start(bf16[32,3712]{1,0:T(8,128)(2,1)S(1)} %shard_map.64.refs_0_), channel_id=1, source_target_pairs={{0,2},{1,3},{2,0},{3,1},{4,6},{5,7},{6,4},{7,5},{8,10},{9,11},{10,... | collective-permute-start | bytes 712712 | tf_op jit(solution)/shard_map/ppermute | solution.py:82
  5.5 2.6 %collective-permute-start.3 = (bf16[32,3712]{1,0:T(8,128)(2,1)S(1)}, bf16[32,3712]{1,0:T(8,128)(2,1)S(1)}, u32[]{:S(2)}, u32[]{:S(2)}) collective-permute-start(bf16[32,3712]{1,0:T(8,128)(2,1)S(1)} %shard_map.64.refs_0_), channel_id=1, source_target_pairs={{0,8},{1,9},{2,10},{3,11},{4,12},{5,13},{6,14},{7,15},{8,0},{9,1},... | collective-permute-start | bytes 712712 | tf_op jit(solution)/shard_map/ppermute | solution.py:82
  8.0 1.6 %collective-permute-start.4 = (bf16[32,3712]{1,0:T(8,128)(2,1)S(1)}, bf16[32,3712]{1,0:T(8,128)(2,1)S(1)}, u32[]{:S(2)}, u32[]{:S(2)}) collective-permute-start(bf16[32,3712]{1,0:T(8,128)(2,1)S(1)} %shard_map.64.refs_0_), channel_id=1, source_target_pairs={{0,4},{1,5},{2,6},{3,7},{4,0},{5,1},{6,2},{7,3},{8,12},{9,13},{10,... | collective-permute-start | bytes 712712 | tf_op jit(solution)/shard_map/ppermute | solution.py:82
  9.6 0.0 collective-permute-done.1.peer_ref
  9.6 1.5 %copy-done.3 = bf16[2,3584,128]{2,1,0:T(8,128)(2,1)S(1)} copy-done((bf16[2,3584,128]{2,1,0:T(8,128)(2,1)S(1)}, bf16[2,3584,128]{2,1,0:T(8,128)(2,1)}, u32[]{:S(2)}) %copy-start.3) | copy-done | bytes 1835032
  11.1 0.6 %shard_map.65.refs_2_.refs_4_.refs_5_ = bf16[3584,512]{1,0:T(8,128)(2,1)S(1)} custom-call(bf16[2,3584,128]{2,1,0:T(8,128)(2,1)S(1)} %copy-done.3, bf16[2,3584,128]{2,1,0:T(8,128)(2,1)S(1)} %collective-permute-done.1.peer_ref), custom_call_target="tpu_custom_call" | custom-call | bytes 4000000 | tf_op jit(solution)/shard_map/pallas_call | solution.py:112
  11.8 0.0 collective-permute-done.refs_2_
  11.8 3.5 %collective-permute-start.8 = (bf16[32,3712]{1,0:T(8,128)(2,1)S(1)}, bf16[32,3712]{1,0:T(8,128)(2,1)S(1)}, u32[]{:S(2)}, u32[]{:S(2)}) collective-permute-start(bf16[32,3712]{1,0:T(8,128)(2,1)S(1)} %collective-permute-done.refs_2_), channel_id=1, source_target_pairs={{0,12},{1,13},{2,14},{3,15},{4,8},{5,9},{6,10},{7,11},{8,4},{9,5},... | collective-permute-start | bytes 712712 | tf_op jit(solution)/shard_map/ppermute | solution.py:82
  15.2 0.0 collective-permute-done.2.refs_4_.refs_6_.refs_7_
  15.2 1.0 %copy-done.1 = bf16[2,128,1024]{2,1,0:T(8,128)(2,1)S(1)} copy-done((bf16[2,128,1024]{2,1,0:T(8,128)(2,1)S(1)}, bf16[2,128,1024]{2,1,0:T(8,128)(2,1)}, u32[]{:S(2)}) %copy-start.1) | copy-done | bytes 524312
  16.3 2.3 %shard_map.66.refs_0_ = bf16[32,1024]{1,0:T(8,128)(2,1)S(1)} custom-call(bf16[32,3712]{1,0:T(8,128)(2,1)S(1)} %shard_map.64.refs_0_, bf16[3584,1024]{1,0:T(8,128)(2,1)S(1)} %copy-done, bf16[3584,512]{1,0:T(8,128)(2,1)S(1)} %shard_map.65.refs_2_.refs_4_.refs_5_, bf16[2,128,1024]{2,1,0:T(8,128)(2,1)S(1)} %copy-done.1, ...), custom_call_target="tpu_custom_call" | custom-call | flops 352321536 | bytes 9000000 | tf_op jit(solution)/shard_map/pallas_call | solution.py:96
  18.6 6.6 %collective-permute-done.3.refs_0_ = bf16[32,3712]{1,0:T(8,128)(2,1)S(1)} collective-permute-done((bf16[32,3712]{1,0:T(8,128)(2,1)S(1)}, bf16[32,3712]{1,0:T(8,128)(2,1)S(1)}, u32[]{:S(2)}, u32[]{:S(2)}) %collective-permute-start.3) | collective-permute-done | bytes 237600 | tf_op jit(solution)/shard_map/ppermute | solution.py:82
  25.2 0.0 collective-permute-done.4.refs_1_
  25.2 2.0 %collective-permute-start.10 = (bf16[32,3712]{1,0:T(8,128)(2,1)S(1)}, bf16[32,3712]{1,0:T(8,128)(2,1)S(1)}, u32[]{:S(2)}, u32[]{:S(2)}) collective-permute-start(bf16[32,3712]{1,0:T(8,128)(2,1)S(1)} %collective-permute-done.4.refs_1_), channel_id=1, source_target_pairs={{0,2},{1,3},{2,0},{3,1},{4,6},{5,7},{6,4},{7,5},{8,10},{9,11},{10,... | collective-permute-start | bytes 712712 | tf_op jit(solution)/shard_map/ppermute | solution.py:82
  27.2 2.7 %shard_map.67 = (bf16[32,1024]{1,0:T(8,128)(2,1)S(1)}, bf16[32,1024]{1,0:T(8,128)(2,1)S(1)}, bf16[32,1024]{1,0:T(8,128)(2,1)S(1)}) custom-call(bf16[32,3712]{1,0:T(8,128)(2,1)S(1)} %collective-permute-done.3.refs_0_, bf16[32,3712]{1,0:T(8,128)(2,1)S(1)} %collective-permute-done.4.refs_1_, bf16[32,3712]{1,0:T(8,128)(2,1)S(1)} %collective-permute-done.refs_2_, ...), custom_call_target="tpu_custom_call" | custom-call | flops 1056964608 | bytes 9000000 | tf_op jit(solution)/shard_map/pallas_call | solution.py:96
  29.9 0.1 collective-permute-start.5
  30.0 2.1 %collective-permute-start.6 = (bf16[32,1024]{1,0:T(8,128)(2,1)S(1)}, bf16[32,1024]{1,0:T(8,128)(2,1)S(1)}, u32[]{:S(2)}, u32[]{:S(2)}) collective-permute-start(bf16[32,1024]{1,0:T(8,128)(2,1)S(1)} %get-tuple-element.21), channel_id=1, source_target_pairs={{0,4},{1,5},{2,6},{3,7},{4,0},{5,1},{6,2},{7,3},{8,12},{9,13},{10,... | collective-permute-start | bytes 196616 | tf_op jit(solution)/shard_map/ppermute | solution.py:82
  32.1 0.0 collective-permute-start.7
  32.1 2.4 %collective-permute-done.10.refs_2_ = bf16[32,3712]{1,0:T(8,128)(2,1)S(1)} collective-permute-done((bf16[32,3712]{1,0:T(8,128)(2,1)S(1)}, bf16[32,3712]{1,0:T(8,128)(2,1)S(1)}, u32[]{:S(2)}, u32[]{:S(2)}) %collective-permute-start.10) | collective-permute-done | bytes 237600 | tf_op jit(solution)/shard_map/ppermute | solution.py:82
  34.5 2.6 %shard_map.68 = (bf16[32,1024]{1,0:T(8,128)(2,1)S(1)}, bf16[32,1024]{1,0:T(8,128)(2,1)S(1)}, bf16[32,1024]{1,0:T(8,128)(2,1)S(1)}, bf16[32,1024]{1,0:T(8,128)(2,1)S(1)}) custom-call(bf16[32,3712]{1,0:T(8,128)(2,1)S(1)} %collective-permute-done.8.refs_0_, bf16[32,3712]{1,0:T(8,128)(2,1)S(1)} %collective-permute-done.9.refs_1_, ...), custom_call_target="tpu_custom_call" | custom-call | flops 1409286144 | bytes 9000000 | tf_op jit(solution)/shard_map/pallas_call | solution.py:96
  37.2 2.4 %collective-permute-start.12 = (bf16[32,1024]{1,0:T(8,128)(2,1)S(1)}, bf16[32,1024]{1,0:T(8,128)(2,1)S(1)}, u32[]{:S(2)}, u32[]{:S(2)}) collective-permute-start(bf16[32,1024]{1,0:T(8,128)(2,1)S(1)} %get-tuple-element.23), channel_id=1, source_target_pairs={{0,14},{1,15},{2,12},{3,13},{4,10},{5,11},{6,8},{7,9},{8,6},{9,7},... | collective-permute-start | bytes 196616 | tf_op jit(solution)/shard_map/ppermute | solution.py:82
  39.6 2.3 %collective-permute-start.14 = (bf16[32,1024]{1,0:T(8,128)(2,1)S(1)}, bf16[32,1024]{1,0:T(8,128)(2,1)S(1)}, u32[]{:S(2)}, u32[]{:S(2)}) collective-permute-start(bf16[32,1024]{1,0:T(8,128)(2,1)S(1)} %get-tuple-element.25), channel_id=1, source_target_pairs={{0,6},{1,7},{2,4},{3,5},{4,2},{5,3},{6,0},{7,1},{8,14},{9,15},{10,... | collective-permute-start | bytes 196616 | tf_op jit(solution)/shard_map/ppermute | solution.py:82
  42.0 2.9 %collective-permute-start.15 = (bf16[32,1024]{1,0:T(8,128)(2,1)S(1)}, bf16[32,1024]{1,0:T(8,128)(2,1)S(1)}, u32[]{:S(2)}, u32[]{:S(2)}) collective-permute-start(bf16[32,1024]{1,0:T(8,128)(2,1)S(1)} %get-tuple-element.26), channel_id=1, source_target_pairs={{0,12},{1,13},{2,14},{3,15},{4,8},{5,9},{6,10},{7,11},{8,4},{9,5},... | collective-permute-start | bytes 196616 | tf_op jit(solution)/shard_map/ppermute | solution.py:82
  44.9 1.9 %collective-permute-done.13.refs_5_ = bf16[32,1024]{1,0:T(8,128)(2,1)S(1)} collective-permute-done((bf16[32,1024]{1,0:T(8,128)(2,1)S(1)}, bf16[32,1024]{1,0:T(8,128)(2,1)S(1)}, u32[]{:S(2)}, u32[]{:S(2)}) %collective-permute-start.13) | collective-permute-done | bytes 65568 | tf_op jit(solution)/shard_map/ppermute | solution.py:82
  46.8 1.2 %collective-permute-done.15.refs_7_ = bf16[32,1024]{1,0:T(8,128)(2,1)S(1)} collective-permute-done((bf16[32,1024]{1,0:T(8,128)(2,1)S(1)}, bf16[32,1024]{1,0:T(8,128)(2,1)S(1)}, u32[]{:S(2)}, u32[]{:S(2)}) %collective-permute-start.15) | collective-permute-done | bytes 65568 | tf_op jit(solution)/shard_map/ppermute | solution.py:82
  48.0 0.7 %shard_map.69 = bf16[32,1024]{1,0:T(8,128)(2,1)} custom-call(bf16[32,1024]{1,0:T(8,128)(2,1)S(1)} %shard_map.66.refs_0_, bf16[32,1024]{1,0:T(8,128)(2,1)S(1)} %collective-permute-done.5.refs_1_, bf16[32,1024]{1,0:T(8,128)(2,1)S(1)} %collective-permute-done.6.refs_2_, bf16[32,1024]{1,0:T(8,128)(2,1)S(1)} %collective-permute-done.7.refs_3_, ...), custom_call_target="tpu_custom_call" | custom-call | bytes 2000000 | tf_op jit(solution)/shard_map/pallas_call | solution.py:164
  (17 shorter events, 0.0 us)
Async XLA Ops:
  0.0 9.6 %collective-permute-start.1 = (bf16[2,3584,128]{2,1,0:T(8,128)(2,1)}, bf16[2,3584,128]{2,1,0:T(8,128)(2,1)S(1)}, u32[]{:S(2)}, u32[]{:S(2)}) collective-permute-start(bf16[2,3584,128]{2,1,0:T(8,128)(2,1)} %own_ref.1), channel_id=1, source_target_pairs={{0,1},{1,0},{2,3},{3,2},{4,5},{5,4},{6,7},{7,6},{8,9},{9,8},{10,11... | collective-permute-start | bytes 5505032 | tf_op jit(solution)/shard_map/ppermute | solution.py:82
  0.5 14.8 %collective-permute-start.2 = (bf16[2,128,1024]{2,1,0:T(8,128)(2,1)}, bf16[2,128,1024]{2,1,0:T(8,128)(2,1)S(1)}, u32[]{:S(2)}, u32[]{:S(2)}) collective-permute-start(bf16[2,128,1024]{2,1,0:T(8,128)(2,1)} %refs_6_.1), channel_id=1, source_target_pairs={{0,1},{1,0},{2,3},{3,2},{4,5},{5,4},{6,7},{7,6},{8,9},{9,8},{10,11... | collective-permute-start | bytes 1572872 | tf_op jit(solution)/shard_map/ppermute | solution.py:82
  1.2 0.9 %copy-start.4 = (bf16[32,3584]{1,0:T(8,128)(2,1)S(1)}, bf16[32,3584]{1,0:T(8,128)(2,1)}, u32[]{:S(2)}) copy-start(bf16[32,3584]{1,0:T(8,128)(2,1)} %tokens_ref.1) | copy-start | bytes 688132
  2.4 12.8 %copy-start = (bf16[3584,1024]{1,0:T(8,128)(2,1)S(1)}, bf16[3584,1024]{1,0:T(8,128)(2,1)}, u32[]{:S(2)}) copy-start(bf16[3584,1024]{1,0:T(8,128)(2,1)} %refs_4_.1) | copy-start | bytes 22020100
  2.4 9.3 %collective-permute-start = (bf16[32,3712]{1,0:T(8,128)(2,1)S(1)}, bf16[32,3712]{1,0:T(8,128)(2,1)S(1)}, u32[]{:S(2)}, u32[]{:S(2)}) collective-permute-start(bf16[32,3712]{1,0:T(8,128)(2,1)S(1)} %shard_map.64.refs_0_), channel_id=1, source_target_pairs={{0,2},{1,3},{2,0},{3,1},{4,6},{5,7},{6,4},{7,5},{8,10},{9,11},{10,... | collective-permute-start | bytes 712712 | tf_op jit(solution)/shard_map/ppermute | solution.py:82
  5.5 19.7 %collective-permute-start.3 = (bf16[32,3712]{1,0:T(8,128)(2,1)S(1)}, bf16[32,3712]{1,0:T(8,128)(2,1)S(1)}, u32[]{:S(2)}, u32[]{:S(2)}) collective-permute-start(bf16[32,3712]{1,0:T(8,128)(2,1)S(1)} %shard_map.64.refs_0_), channel_id=1, source_target_pairs={{0,8},{1,9},{2,10},{3,11},{4,12},{5,13},{6,14},{7,15},{8,0},{9,1},... | collective-permute-start | bytes 712712 | tf_op jit(solution)/shard_map/ppermute | solution.py:82
  8.0 17.1 %collective-permute-start.4 = (bf16[32,3712]{1,0:T(8,128)(2,1)S(1)}, bf16[32,3712]{1,0:T(8,128)(2,1)S(1)}, u32[]{:S(2)}, u32[]{:S(2)}) collective-permute-start(bf16[32,3712]{1,0:T(8,128)(2,1)S(1)} %shard_map.64.refs_0_), channel_id=1, source_target_pairs={{0,4},{1,5},{2,6},{3,7},{4,0},{5,1},{6,2},{7,3},{8,12},{9,13},{10,... | collective-permute-start | bytes 712712 | tf_op jit(solution)/shard_map/ppermute | solution.py:82
  9.6 1.5 %copy-start.3 = (bf16[2,3584,128]{2,1,0:T(8,128)(2,1)S(1)}, bf16[2,3584,128]{2,1,0:T(8,128)(2,1)}, u32[]{:S(2)}) copy-start(bf16[2,3584,128]{2,1,0:T(8,128)(2,1)} %own_ref.1) | copy-start | bytes 5505028
  11.8 18.2 %collective-permute-start.8 = (bf16[32,3712]{1,0:T(8,128)(2,1)S(1)}, bf16[32,3712]{1,0:T(8,128)(2,1)S(1)}, u32[]{:S(2)}, u32[]{:S(2)}) collective-permute-start(bf16[32,3712]{1,0:T(8,128)(2,1)S(1)} %collective-permute-done.refs_2_), channel_id=1, source_target_pairs={{0,12},{1,13},{2,14},{3,15},{4,8},{5,9},{6,10},{7,11},{8,4},{9,5},... | collective-permute-start | bytes 712712 | tf_op jit(solution)/shard_map/ppermute | solution.py:82
  15.2 1.0 %copy-start.1 = (bf16[2,128,1024]{2,1,0:T(8,128)(2,1)S(1)}, bf16[2,128,1024]{2,1,0:T(8,128)(2,1)}, u32[]{:S(2)}) copy-start(bf16[2,128,1024]{2,1,0:T(8,128)(2,1)} %refs_6_.1) | copy-start | bytes 1572868
  16.3 10.9 %copy-start.2 = (bf16[2,128,1024]{2,1,0:T(8,128)(2,1)S(1)}, bf16[2,128,1024]{2,1,0:T(8,128)(2,1)}, u32[]{:S(2)}) copy-start(bf16[2,128,1024]{2,1,0:T(8,128)(2,1)} %refs_6_.1) | copy-start | bytes 1572868
  25.2 6.9 %collective-permute-start.9 = (bf16[32,3712]{1,0:T(8,128)(2,1)S(1)}, bf16[32,3712]{1,0:T(8,128)(2,1)S(1)}, u32[]{:S(2)}, u32[]{:S(2)}) collective-permute-start(bf16[32,3712]{1,0:T(8,128)(2,1)S(1)} %collective-permute-done.3.refs_0_), channel_id=1, source_target_pairs={{0,2},{1,3},{2,0},{3,1},{4,6},{5,7},{6,4},{7,5},{8,10},{9,11},{10,... | collective-permute-start | bytes 712712 | tf_op jit(solution)/shard_map/ppermute | solution.py:82
  25.2 9.4 %collective-permute-start.10 = (bf16[32,3712]{1,0:T(8,128)(2,1)S(1)}, bf16[32,3712]{1,0:T(8,128)(2,1)S(1)}, u32[]{:S(2)}, u32[]{:S(2)}) collective-permute-start(bf16[32,3712]{1,0:T(8,128)(2,1)S(1)} %collective-permute-done.4.refs_1_), channel_id=1, source_target_pairs={{0,2},{1,3},{2,0},{3,1},{4,6},{5,7},{6,4},{7,5},{8,10},{9,11},{10,... | collective-permute-start | bytes 712712 | tf_op jit(solution)/shard_map/ppermute | solution.py:82
  27.2 7.3 %collective-permute-start.11 = (bf16[32,3712]{1,0:T(8,128)(2,1)S(1)}, bf16[32,3712]{1,0:T(8,128)(2,1)S(1)}, u32[]{:S(2)}, u32[]{:S(2)}) collective-permute-start(bf16[32,3712]{1,0:T(8,128)(2,1)S(1)} %collective-permute-done.3.refs_0_), channel_id=1, source_target_pairs={{0,4},{1,5},{2,6},{3,7},{4,0},{5,1},{6,2},{7,3},{8,12},{9,13},{10,... | collective-permute-start | bytes 712712 | tf_op jit(solution)/shard_map/ppermute | solution.py:82
  29.9 9.7 %collective-permute-start.5 = (bf16[32,1024]{1,0:T(8,128)(2,1)S(1)}, bf16[32,1024]{1,0:T(8,128)(2,1)S(1)}, u32[]{:S(2)}, u32[]{:S(2)}) collective-permute-start(bf16[32,1024]{1,0:T(8,128)(2,1)S(1)} %get-tuple-element.20), channel_id=1, source_target_pairs={{0,8},{1,9},{2,10},{3,11},{4,12},{5,13},{6,14},{7,15},{8,0},{9,1},... | collective-permute-start | bytes 196616 | tf_op jit(solution)/shard_map/ppermute | solution.py:82
  30.0 12.0 %collective-permute-start.6 = (bf16[32,1024]{1,0:T(8,128)(2,1)S(1)}, bf16[32,1024]{1,0:T(8,128)(2,1)S(1)}, u32[]{:S(2)}, u32[]{:S(2)}) collective-permute-start(bf16[32,1024]{1,0:T(8,128)(2,1)S(1)} %get-tuple-element.21), channel_id=1, source_target_pairs={{0,4},{1,5},{2,6},{3,7},{4,0},{5,1},{6,2},{7,3},{8,12},{9,13},{10,... | collective-permute-start | bytes 196616 | tf_op jit(solution)/shard_map/ppermute | solution.py:82
  32.1 12.8 %collective-permute-start.7 = (bf16[32,1024]{1,0:T(8,128)(2,1)S(1)}, bf16[32,1024]{1,0:T(8,128)(2,1)S(1)}, u32[]{:S(2)}, u32[]{:S(2)}) collective-permute-start(bf16[32,1024]{1,0:T(8,128)(2,1)S(1)} %get-tuple-element.22), channel_id=1, source_target_pairs={{0,2},{1,3},{2,0},{3,1},{4,6},{5,7},{6,4},{7,5},{8,10},{9,11},{10,... | collective-permute-start | bytes 196616 | tf_op jit(solution)/shard_map/ppermute | solution.py:82
  37.2 7.7 %collective-permute-start.12 = (bf16[32,1024]{1,0:T(8,128)(2,1)S(1)}, bf16[32,1024]{1,0:T(8,128)(2,1)S(1)}, u32[]{:S(2)}, u32[]{:S(2)}) collective-permute-start(bf16[32,1024]{1,0:T(8,128)(2,1)S(1)} %get-tuple-element.23), channel_id=1, source_target_pairs={{0,14},{1,15},{2,12},{3,13},{4,10},{5,11},{6,8},{7,9},{8,6},{9,7},... | collective-permute-start | bytes 196616 | tf_op jit(solution)/shard_map/ppermute | solution.py:82
  39.6 7.2 %collective-permute-start.13 = (bf16[32,1024]{1,0:T(8,128)(2,1)S(1)}, bf16[32,1024]{1,0:T(8,128)(2,1)S(1)}, u32[]{:S(2)}, u32[]{:S(2)}) collective-permute-start(bf16[32,1024]{1,0:T(8,128)(2,1)S(1)} %get-tuple-element.24), channel_id=1, source_target_pairs={{0,10},{1,11},{2,8},{3,9},{4,14},{5,15},{6,12},{7,13},{8,2},{9,3},... | collective-permute-start | bytes 196616 | tf_op jit(solution)/shard_map/ppermute | solution.py:82
  39.6 7.2 %collective-permute-start.14 = (bf16[32,1024]{1,0:T(8,128)(2,1)S(1)}, bf16[32,1024]{1,0:T(8,128)(2,1)S(1)}, u32[]{:S(2)}, u32[]{:S(2)}) collective-permute-start(bf16[32,1024]{1,0:T(8,128)(2,1)S(1)} %get-tuple-element.25), channel_id=1, source_target_pairs={{0,6},{1,7},{2,4},{3,5},{4,2},{5,3},{6,0},{7,1},{8,14},{9,15},{10,... | collective-permute-start | bytes 196616 | tf_op jit(solution)/shard_map/ppermute | solution.py:82
  42.0 6.1 %collective-permute-start.15 = (bf16[32,1024]{1,0:T(8,128)(2,1)S(1)}, bf16[32,1024]{1,0:T(8,128)(2,1)S(1)}, u32[]{:S(2)}, u32[]{:S(2)}) collective-permute-start(bf16[32,1024]{1,0:T(8,128)(2,1)S(1)} %get-tuple-element.26), channel_id=1, source_target_pairs={{0,12},{1,13},{2,14},{3,15},{4,8},{5,9},{6,10},{7,11},{8,4},{9,5},... | collective-permute-start | bytes 196616 | tf_op jit(solution)/shard_map/ppermute | solution.py:82

commit v5 on v4

--- a/solution.py
+++ b/solution.py
@@ -151,7 +151,8 @@
     fetch(crossing)
     tie((held, [m for m in of[1] if m >= minor]), (parts, of[0]))
     fetch([m for m in of[2] if m not in crossing])
-    compute(of[1])
+    first = sorted(of[1], key=lambda m: (m < minor, m))
+    compute(first)
     send_home(of[1])
     for stage in range(3, stages):
         fetch(of[stage])
@@ -159,7 +160,7 @@
         send_home(of[stage - 1])
     last = sorted(of[-1], key=lambda m: (m not in crossing, hop_of(m) >= minor, -m))
     compute(last)
-    send_home(last)
+    send_home([m for m in last if m >= 2 * minor] + [m for m in last if m < 2 * minor])
     partial = list(home.values())
     return small(sum_body, (rows, hidden_units), chips, 8, 2000000)(*partial)
 

time: 49 us -> 48.5 us (0.990)
  starting transfers between devices: 23.1 us -> 22.2 us
  waiting for transfers between devices: 12.1 us -> 12.6 us
    ppermute x16, starting transfers between devices: 23.1 us -> 22.2 us  [exchange(): lax.ppermute(value, 'expert', [(i, i ^ mask) for i in range(devices_count)])]
  transfers between devices with their start and end apart: 16 -> 16, of which waited for: 4 -> 5; matrix products, arithmetic and copies ran while one was open for 1% -> 1% of each run, Pallas kernels for 17% -> 18%
where the time goes in v5:
time: 48.5 us; the launch traced here: 48.3 us
  starting transfers between devices  22.2 us (46%)
  waiting for transfers between devices  12.6 us (26%)
  Pallas kernels  9.22 us (19%)
  local copies, waits for them, and re-layouts  3.49 us (7%)
  other arithmetic  0.71 us (1%)
    ppermute x16, starting transfers between devices, exchange(): lax.ppermute(value, 'expert', [(i, i ^ mask) for i in range(devices_count)])  22.2 us
    ppermute x16, waiting for transfers between devices, exchange(): lax.ppermute(value, 'expert', [(i, i ^ mask) for i in range(devices_count)])  12.6 us
    pallas_call x3, Pallas kernels, experts_on(): pl.pallas_call(functools.partial(expert_body, features, count), out_shape...  7.65 us
    unnamed x10, local copies, waits for them, and re-layouts  3.49 us
  transfers between devices with their start and end apart: 16, of which 5 were waited for; matrix products, arithmetic and copies ran while one was open for 1% of the time, Pallas kernels for 18%

profile of v5, /device:TPU:0, one launch (start us, length us, event | category | flops | bytes accessed | tf_op | source)
XLA Modules:
  0.0 48.3 jit_solution(15791767150461385364)
XLA Ops:
  0.0 0.5 collective-permute-start.1
  0.5 0.1 collective-permute-start.2
  0.5 0.7 %add_bitcast_fusion.marks_ref = s32[8,32]{1,0:T(8,128)S(1)} fusion(s32[32,8]{0,1:T(8,128)} %param.8, s32[32,8]{0,1:T(8,128)} %param.7), kind=kLoop, calls=%fused_computation | loop fusion | flops 512 | bytes 3072 | tf_op jit(solution)/shard_map/add | solution.py:110
  1.2 0.9 %copy-done.4 = bf16[32,3584]{1,0:T(8,128)(2,1)S(1)} copy-done((bf16[32,3584]{1,0:T(8,128)(2,1)S(1)}, bf16[32,3584]{1,0:T(8,128)(2,1)}, u32[]{:S(2)}) %copy-start.4) | copy-done | bytes 229400
  2.2 0.2 shard_map.64.refs_0_
  2.4 0.0 copy-start
  2.4 3.0 %collective-permute-start = (bf16[32,3712]{1,0:T(8,128)(2,1)S(1)}, bf16[32,3712]{1,0:T(8,128)(2,1)S(1)}, u32[]{:S(2)}, u32[]{:S(2)}) collective-permute-start(bf16[32,3712]{1,0:T(8,128)(2,1)S(1)} %shard_map.64.refs_0_), channel_id=1, source_target_pairs={{0,2},{1,3},{2,0},{3,1},{4,6},{5,7},{6,4},{7,5},{8,10},{9,11},{10,... | collective-permute-start | bytes 712712 | tf_op jit(solution)/shard_map/ppermute | solution.py:82
  5.5 2.6 %collective-permute-start.3 = (bf16[32,3712]{1,0:T(8,128)(2,1)S(1)}, bf16[32,3712]{1,0:T(8,128)(2,1)S(1)}, u32[]{:S(2)}, u32[]{:S(2)}) collective-permute-start(bf16[32,3712]{1,0:T(8,128)(2,1)S(1)} %shard_map.64.refs_0_), channel_id=1, source_target_pairs={{0,8},{1,9},{2,10},{3,11},{4,12},{5,13},{6,14},{7,15},{8,0},{9,1},... | collective-permute-start | bytes 712712 | tf_op jit(solution)/shard_map/ppermute | solution.py:82
  8.0 1.6 %collective-permute-start.4 = (bf16[32,3712]{1,0:T(8,128)(2,1)S(1)}, bf16[32,3712]{1,0:T(8,128)(2,1)S(1)}, u32[]{:S(2)}, u32[]{:S(2)}) collective-permute-start(bf16[32,3712]{1,0:T(8,128)(2,1)S(1)} %shard_map.64.refs_0_), channel_id=1, source_target_pairs={{0,4},{1,5},{2,6},{3,7},{4,0},{5,1},{6,2},{7,3},{8,12},{9,13},{10,... | collective-permute-start | bytes 712712 | tf_op jit(solution)/shard_map/ppermute | solution.py:82
  9.6 0.0 collective-permute-done.1.peer_ref
  9.6 1.5 %copy-done.3 = bf16[2,3584,128]{2,1,0:T(8,128)(2,1)S(1)} copy-done((bf16[2,3584,128]{2,1,0:T(8,128)(2,1)S(1)}, bf16[2,3584,128]{2,1,0:T(8,128)(2,1)}, u32[]{:S(2)}) %copy-start.3) | copy-done | bytes 1835032
  11.1 0.6 %shard_map.65.refs_2_.refs_4_.refs_5_ = bf16[3584,512]{1,0:T(8,128)(2,1)S(1)} custom-call(bf16[2,3584,128]{2,1,0:T(8,128)(2,1)S(1)} %copy-done.3, bf16[2,3584,128]{2,1,0:T(8,128)(2,1)S(1)} %collective-permute-done.1.peer_ref), custom_call_target="tpu_custom_call" | custom-call | bytes 4000000 | tf_op jit(solution)/shard_map/pallas_call | solution.py:112
  11.8 0.0 collective-permute-done.refs_2_
  11.8 3.5 %collective-permute-start.8 = (bf16[32,3712]{1,0:T(8,128)(2,1)S(1)}, bf16[32,3712]{1,0:T(8,128)(2,1)S(1)}, u32[]{:S(2)}, u32[]{:S(2)}) collective-permute-start(bf16[32,3712]{1,0:T(8,128)(2,1)S(1)} %collective-permute-done.refs_2_), channel_id=1, source_target_pairs={{0,12},{1,13},{2,14},{3,15},{4,8},{5,9},{6,10},{7,11},{8,4},{9,5},... | collective-permute-start | bytes 712712 | tf_op jit(solution)/shard_map/ppermute | solution.py:82
  15.2 0.0 collective-permute-done.2.refs_4_.refs_6_.refs_7_
  15.2 1.0 %copy-done.1 = bf16[2,128,1024]{2,1,0:T(8,128)(2,1)S(1)} copy-done((bf16[2,128,1024]{2,1,0:T(8,128)(2,1)S(1)}, bf16[2,128,1024]{2,1,0:T(8,128)(2,1)}, u32[]{:S(2)}) %copy-start.1) | copy-done | bytes 524312
  16.3 2.3 %shard_map.66.refs_0_ = bf16[32,1024]{1,0:T(8,128)(2,1)S(1)} custom-call(bf16[32,3712]{1,0:T(8,128)(2,1)S(1)} %shard_map.64.refs_0_, bf16[3584,1024]{1,0:T(8,128)(2,1)S(1)} %copy-done, bf16[3584,512]{1,0:T(8,128)(2,1)S(1)} %shard_map.65.refs_2_.refs_4_.refs_5_, bf16[2,128,1024]{2,1,0:T(8,128)(2,1)S(1)} %copy-done.1, ...), custom_call_target="tpu_custom_call" | custom-call | flops 352321536 | bytes 9000000 | tf_op jit(solution)/shard_map/pallas_call | solution.py:96
  18.6 6.6 %collective-permute-done.3.refs_1_ = bf16[32,3712]{1,0:T(8,128)(2,1)S(1)} collective-permute-done((bf16[32,3712]{1,0:T(8,128)(2,1)S(1)}, bf16[32,3712]{1,0:T(8,128)(2,1)S(1)}, u32[]{:S(2)}, u32[]{:S(2)}) %collective-permute-start.3) | collective-permute-done | bytes 237600 | tf_op jit(solution)/shard_map/ppermute | solution.py:82
  25.2 2.0 %collective-permute-start.10 = (bf16[32,3712]{1,0:T(8,128)(2,1)S(1)}, bf16[32,3712]{1,0:T(8,128)(2,1)S(1)}, u32[]{:S(2)}, u32[]{:S(2)}) collective-permute-start(bf16[32,3712]{1,0:T(8,128)(2,1)S(1)} %collective-permute-done.4.refs_0_), channel_id=1, source_target_pairs={{0,2},{1,3},{2,0},{3,1},{4,6},{5,7},{6,4},{7,5},{8,10},{9,11},{10,... | collective-permute-start | bytes 712712 | tf_op jit(solution)/shard_map/ppermute | solution.py:82
  27.2 2.7 %shard_map.67 = (bf16[32,1024]{1,0:T(8,128)(2,1)S(1)}, bf16[32,1024]{1,0:T(8,128)(2,1)S(1)}, bf16[32,1024]{1,0:T(8,128)(2,1)S(1)}) custom-call(bf16[32,3712]{1,0:T(8,128)(2,1)S(1)} %collective-permute-done.4.refs_0_, bf16[32,3712]{1,0:T(8,128)(2,1)S(1)} %collective-permute-done.3.refs_1_, bf16[32,3712]{1,0:T(8,128)(2,1)S(1)} %collective-permute-done.refs_2_, ...), custom_call_target="tpu_custom_call" | custom-call | flops 1056964608 | bytes 9000000 | tf_op jit(solution)/shard_map/pallas_call | solution.py:96
  29.9 0.1 collective-permute-start.5
  30.0 2.1 %collective-permute-start.6 = (bf16[32,1024]{1,0:T(8,128)(2,1)S(1)}, bf16[32,1024]{1,0:T(8,128)(2,1)S(1)}, u32[]{:S(2)}, u32[]{:S(2)}) collective-permute-start(bf16[32,1024]{1,0:T(8,128)(2,1)S(1)} %get-tuple-element.21), channel_id=1, source_target_pairs={{0,4},{1,5},{2,6},{3,7},{4,0},{5,1},{6,2},{7,3},{8,12},{9,13},{10,... | collective-permute-start | bytes 196616 | tf_op jit(solution)/shard_map/ppermute | solution.py:82
  32.1 0.0 collective-permute-start.7
  32.1 2.4 %collective-permute-done.10.refs_2_ = bf16[32,3712]{1,0:T(8,128)(2,1)S(1)} collective-permute-done((bf16[32,3712]{1,0:T(8,128)(2,1)S(1)}, bf16[32,3712]{1,0:T(8,128)(2,1)S(1)}, u32[]{:S(2)}, u32[]{:S(2)}) %collective-permute-start.10) | collective-permute-done | bytes 237600 | tf_op jit(solution)/shard_map/ppermute | solution.py:82
  34.5 2.6 %shard_map.68 = (bf16[32,1024]{1,0:T(8,128)(2,1)S(1)}, bf16[32,1024]{1,0:T(8,128)(2,1)S(1)}, bf16[32,1024]{1,0:T(8,128)(2,1)S(1)}, bf16[32,1024]{1,0:T(8,128)(2,1)S(1)}) custom-call(bf16[32,3712]{1,0:T(8,128)(2,1)S(1)} %collective-permute-done.8.refs_0_, bf16[32,3712]{1,0:T(8,128)(2,1)S(1)} %collective-permute-done.9.refs_1_, ...), custom_call_target="tpu_custom_call" | custom-call | flops 1409286144 | bytes 9000000 | tf_op jit(solution)/shard_map/pallas_call | solution.py:96
  37.2 2.4 %collective-permute-start.12 = (bf16[32,1024]{1,0:T(8,128)(2,1)S(1)}, bf16[32,1024]{1,0:T(8,128)(2,1)S(1)}, u32[]{:S(2)}, u32[]{:S(2)}) collective-permute-start(bf16[32,1024]{1,0:T(8,128)(2,1)S(1)} %get-tuple-element.23), channel_id=1, source_target_pairs={{0,14},{1,15},{2,12},{3,13},{4,10},{5,11},{6,8},{7,9},{8,6},{9,7},... | collective-permute-start | bytes 196616 | tf_op jit(solution)/shard_map/ppermute | solution.py:82
  39.6 1.9 %collective-permute-start.14 = (bf16[32,1024]{1,0:T(8,128)(2,1)S(1)}, bf16[32,1024]{1,0:T(8,128)(2,1)S(1)}, u32[]{:S(2)}, u32[]{:S(2)}) collective-permute-start(bf16[32,1024]{1,0:T(8,128)(2,1)S(1)} %get-tuple-element.25), channel_id=1, source_target_pairs={{0,12},{1,13},{2,14},{3,15},{4,8},{5,9},{6,10},{7,11},{8,4},{9,5},... | collective-permute-start | bytes 196616 | tf_op jit(solution)/shard_map/ppermute | solution.py:82
  41.5 2.5 %collective-permute-start.15 = (bf16[32,1024]{1,0:T(8,128)(2,1)S(1)}, bf16[32,1024]{1,0:T(8,128)(2,1)S(1)}, u32[]{:S(2)}, u32[]{:S(2)}) collective-permute-start(bf16[32,1024]{1,0:T(8,128)(2,1)S(1)} %get-tuple-element.26), channel_id=1, source_target_pairs={{0,6},{1,7},{2,4},{3,5},{4,2},{5,3},{6,0},{7,1},{8,14},{9,15},{10,... | collective-permute-start | bytes 196616 | tf_op jit(solution)/shard_map/ppermute | solution.py:82
  44.0 0.6 %collective-permute-done.12.refs_4_ = bf16[32,1024]{1,0:T(8,128)(2,1)S(1)} collective-permute-done((bf16[32,1024]{1,0:T(8,128)(2,1)S(1)}, bf16[32,1024]{1,0:T(8,128)(2,1)S(1)}, u32[]{:S(2)}, u32[]{:S(2)}) %collective-permute-start.12) | collective-permute-done | bytes 65568 | tf_op jit(solution)/shard_map/ppermute | solution.py:82
  44.6 2.3 %collective-permute-done.13.refs_5_ = bf16[32,1024]{1,0:T(8,128)(2,1)S(1)} collective-permute-done((bf16[32,1024]{1,0:T(8,128)(2,1)S(1)}, bf16[32,1024]{1,0:T(8,128)(2,1)S(1)}, u32[]{:S(2)}, u32[]{:S(2)}) %collective-permute-start.13) | collective-permute-done | bytes 65568 | tf_op jit(solution)/shard_map/ppermute | solution.py:82
  46.9 0.7 %collective-permute-done.15.refs_7_ = bf16[32,1024]{1,0:T(8,128)(2,1)S(1)} collective-permute-done((bf16[32,1024]{1,0:T(8,128)(2,1)S(1)}, bf16[32,1024]{1,0:T(8,128)(2,1)S(1)}, u32[]{:S(2)}, u32[]{:S(2)}) %collective-permute-start.15) | collective-permute-done | bytes 65568 | tf_op jit(solution)/shard_map/ppermute | solution.py:82
  47.6 0.7 %shard_map.69 = bf16[32,1024]{1,0:T(8,128)(2,1)} custom-call(bf16[32,1024]{1,0:T(8,128)(2,1)S(1)} %shard_map.66.refs_0_, bf16[32,1024]{1,0:T(8,128)(2,1)S(1)} %collective-permute-done.5.refs_1_, bf16[32,1024]{1,0:T(8,128)(2,1)S(1)} %collective-permute-done.6.refs_2_, bf16[32,1024]{1,0:T(8,128)(2,1)S(1)} %collective-permute-done.7.refs_3_, ...), custom_call_target="tpu_custom_call" | custom-call | bytes 2000000 | tf_op jit(solution)/shard_map/pallas_call | solution.py:165
  (17 shorter events, 0.0 us)
Async XLA Ops:
  0.0 9.6 %collective-permute-start.1 = (bf16[2,3584,128]{2,1,0:T(8,128)(2,1)}, bf16[2,3584,128]{2,1,0:T(8,128)(2,1)S(1)}, u32[]{:S(2)}, u32[]{:S(2)}) collective-permute-start(bf16[2,3584,128]{2,1,0:T(8,128)(2,1)} %own_ref.1), channel_id=1, source_target_pairs={{0,1},{1,0},{2,3},{3,2},{4,5},{5,4},{6,7},{7,6},{8,9},{9,8},{10,11... | collective-permute-start | bytes 5505032 | tf_op jit(solution)/shard_map/ppermute | solution.py:82
  0.5 14.8 %collective-permute-start.2 = (bf16[2,128,1024]{2,1,0:T(8,128)(2,1)}, bf16[2,128,1024]{2,1,0:T(8,128)(2,1)S(1)}, u32[]{:S(2)}, u32[]{:S(2)}) collective-permute-start(bf16[2,128,1024]{2,1,0:T(8,128)(2,1)} %refs_6_.1), channel_id=1, source_target_pairs={{0,1},{1,0},{2,3},{3,2},{4,5},{5,4},{6,7},{7,6},{8,9},{9,8},{10,11... | collective-permute-start | bytes 1572872 | tf_op jit(solution)/shard_map/ppermute | solution.py:82
  1.2 0.9 %copy-start.4 = (bf16[32,3584]{1,0:T(8,128)(2,1)S(1)}, bf16[32,3584]{1,0:T(8,128)(2,1)}, u32[]{:S(2)}) copy-start(bf16[32,3584]{1,0:T(8,128)(2,1)} %tokens_ref.1) | copy-start | bytes 688132
  2.4 12.8 %copy-start = (bf16[3584,1024]{1,0:T(8,128)(2,1)S(1)}, bf16[3584,1024]{1,0:T(8,128)(2,1)}, u32[]{:S(2)}) copy-start(bf16[3584,1024]{1,0:T(8,128)(2,1)} %refs_4_.1) | copy-start | bytes 22020100
  2.4 9.3 %collective-permute-start = (bf16[32,3712]{1,0:T(8,128)(2,1)S(1)}, bf16[32,3712]{1,0:T(8,128)(2,1)S(1)}, u32[]{:S(2)}, u32[]{:S(2)}) collective-permute-start(bf16[32,3712]{1,0:T(8,128)(2,1)S(1)} %shard_map.64.refs_0_), channel_id=1, source_target_pairs={{0,2},{1,3},{2,0},{3,1},{4,6},{5,7},{6,4},{7,5},{8,10},{9,11},{10,... | collective-permute-start | bytes 712712 | tf_op jit(solution)/shard_map/ppermute | solution.py:82
  5.5 19.7 %collective-permute-start.3 = (bf16[32,3712]{1,0:T(8,128)(2,1)S(1)}, bf16[32,3712]{1,0:T(8,128)(2,1)S(1)}, u32[]{:S(2)}, u32[]{:S(2)}) collective-permute-start(bf16[32,3712]{1,0:T(8,128)(2,1)S(1)} %shard_map.64.refs_0_), channel_id=1, source_target_pairs={{0,8},{1,9},{2,10},{3,11},{4,12},{5,13},{6,14},{7,15},{8,0},{9,1},... | collective-permute-start | bytes 712712 | tf_op jit(solution)/shard_map/ppermute | solution.py:82
  8.0 17.1 %collective-permute-start.4 = (bf16[32,3712]{1,0:T(8,128)(2,1)S(1)}, bf16[32,3712]{1,0:T(8,128)(2,1)S(1)}, u32[]{:S(2)}, u32[]{:S(2)}) collective-permute-start(bf16[32,3712]{1,0:T(8,128)(2,1)S(1)} %shard_map.64.refs_0_), channel_id=1, source_target_pairs={{0,4},{1,5},{2,6},{3,7},{4,0},{5,1},{6,2},{7,3},{8,12},{9,13},{10,... | collective-permute-start | bytes 712712 | tf_op jit(solution)/shard_map/ppermute | solution.py:82
  9.6 1.5 %copy-start.3 = (bf16[2,3584,128]{2,1,0:T(8,128)(2,1)S(1)}, bf16[2,3584,128]{2,1,0:T(8,128)(2,1)}, u32[]{:S(2)}) copy-start(bf16[2,3584,128]{2,1,0:T(8,128)(2,1)} %own_ref.1) | copy-start | bytes 5505028
  11.8 18.2 %collective-permute-start.8 = (bf16[32,3712]{1,0:T(8,128)(2,1)S(1)}, bf16[32,3712]{1,0:T(8,128)(2,1)S(1)}, u32[]{:S(2)}, u32[]{:S(2)}) collective-permute-start(bf16[32,3712]{1,0:T(8,128)(2,1)S(1)} %collective-permute-done.refs_2_), channel_id=1, source_target_pairs={{0,12},{1,13},{2,14},{3,15},{4,8},{5,9},{6,10},{7,11},{8,4},{9,5},... | collective-permute-start | bytes 712712 | tf_op jit(solution)/shard_map/ppermute | solution.py:82
  15.2 1.0 %copy-start.1 = (bf16[2,128,1024]{2,1,0:T(8,128)(2,1)S(1)}, bf16[2,128,1024]{2,1,0:T(8,128)(2,1)}, u32[]{:S(2)}) copy-start(bf16[2,128,1024]{2,1,0:T(8,128)(2,1)} %refs_6_.1) | copy-start | bytes 1572868
  16.3 10.9 %copy-start.2 = (bf16[2,128,1024]{2,1,0:T(8,128)(2,1)S(1)}, bf16[2,128,1024]{2,1,0:T(8,128)(2,1)}, u32[]{:S(2)}) copy-start(bf16[2,128,1024]{2,1,0:T(8,128)(2,1)} %refs_6_.1) | copy-start | bytes 1572868
  25.2 6.9 %collective-permute-start.9 = (bf16[32,3712]{1,0:T(8,128)(2,1)S(1)}, bf16[32,3712]{1,0:T(8,128)(2,1)S(1)}, u32[]{:S(2)}, u32[]{:S(2)}) collective-permute-start(bf16[32,3712]{1,0:T(8,128)(2,1)S(1)} %collective-permute-done.3.refs_1_), channel_id=1, source_target_pairs={{0,2},{1,3},{2,0},{3,1},{4,6},{5,7},{6,4},{7,5},{8,10},{9,11},{10,... | collective-permute-start | bytes 712712 | tf_op jit(solution)/shard_map/ppermute | solution.py:82
  25.2 9.4 %collective-permute-start.10 = (bf16[32,3712]{1,0:T(8,128)(2,1)S(1)}, bf16[32,3712]{1,0:T(8,128)(2,1)S(1)}, u32[]{:S(2)}, u32[]{:S(2)}) collective-permute-start(bf16[32,3712]{1,0:T(8,128)(2,1)S(1)} %collective-permute-done.4.refs_0_), channel_id=1, source_target_pairs={{0,2},{1,3},{2,0},{3,1},{4,6},{5,7},{6,4},{7,5},{8,10},{9,11},{10,... | collective-permute-start | bytes 712712 | tf_op jit(solution)/shard_map/ppermute | solution.py:82
  27.2 7.3 %collective-permute-start.11 = (bf16[32,3712]{1,0:T(8,128)(2,1)S(1)}, bf16[32,3712]{1,0:T(8,128)(2,1)S(1)}, u32[]{:S(2)}, u32[]{:S(2)}) collective-permute-start(bf16[32,3712]{1,0:T(8,128)(2,1)S(1)} %collective-permute-done.3.refs_1_), channel_id=1, source_target_pairs={{0,4},{1,5},{2,6},{3,7},{4,0},{5,1},{6,2},{7,3},{8,12},{9,13},{10,... | collective-permute-start | bytes 712712 | tf_op jit(solution)/shard_map/ppermute | solution.py:82
  29.9 9.7 %collective-permute-start.5 = (bf16[32,1024]{1,0:T(8,128)(2,1)S(1)}, bf16[32,1024]{1,0:T(8,128)(2,1)S(1)}, u32[]{:S(2)}, u32[]{:S(2)}) collective-permute-start(bf16[32,1024]{1,0:T(8,128)(2,1)S(1)} %get-tuple-element.20), channel_id=1, source_target_pairs={{0,8},{1,9},{2,10},{3,11},{4,12},{5,13},{6,14},{7,15},{8,0},{9,1},... | collective-permute-start | bytes 196616 | tf_op jit(solution)/shard_map/ppermute | solution.py:82
  30.0 11.5 %collective-permute-start.6 = (bf16[32,1024]{1,0:T(8,128)(2,1)S(1)}, bf16[32,1024]{1,0:T(8,128)(2,1)S(1)}, u32[]{:S(2)}, u32[]{:S(2)}) collective-permute-start(bf16[32,1024]{1,0:T(8,128)(2,1)S(1)} %get-tuple-element.21), channel_id=1, source_target_pairs={{0,4},{1,5},{2,6},{3,7},{4,0},{5,1},{6,2},{7,3},{8,12},{9,13},{10,... | collective-permute-start | bytes 196616 | tf_op jit(solution)/shard_map/ppermute | solution.py:82
  32.1 11.9 %collective-permute-start.7 = (bf16[32,1024]{1,0:T(8,128)(2,1)S(1)}, bf16[32,1024]{1,0:T(8,128)(2,1)S(1)}, u32[]{:S(2)}, u32[]{:S(2)}) collective-permute-start(bf16[32,1024]{1,0:T(8,128)(2,1)S(1)} %get-tuple-element.22), channel_id=1, source_target_pairs={{0,2},{1,3},{2,0},{3,1},{4,6},{5,7},{6,4},{7,5},{8,10},{9,11},{10,... | collective-permute-start | bytes 196616 | tf_op jit(solution)/shard_map/ppermute | solution.py:82
  37.2 7.4 %collective-permute-start.12 = (bf16[32,1024]{1,0:T(8,128)(2,1)S(1)}, bf16[32,1024]{1,0:T(8,128)(2,1)S(1)}, u32[]{:S(2)}, u32[]{:S(2)}) collective-permute-start(bf16[32,1024]{1,0:T(8,128)(2,1)S(1)} %get-tuple-element.23), channel_id=1, source_target_pairs={{0,14},{1,15},{2,12},{3,13},{4,10},{5,11},{6,8},{7,9},{8,6},{9,7},... | collective-permute-start | bytes 196616 | tf_op jit(solution)/shard_map/ppermute | solution.py:82
  39.6 7.3 %collective-permute-start.13 = (bf16[32,1024]{1,0:T(8,128)(2,1)S(1)}, bf16[32,1024]{1,0:T(8,128)(2,1)S(1)}, u32[]{:S(2)}, u32[]{:S(2)}) collective-permute-start(bf16[32,1024]{1,0:T(8,128)(2,1)S(1)} %get-tuple-element.24), channel_id=1, source_target_pairs={{0,10},{1,11},{2,8},{3,9},{4,14},{5,15},{6,12},{7,13},{8,2},{9,3},... | collective-permute-start | bytes 196616 | tf_op jit(solution)/shard_map/ppermute | solution.py:82
  39.6 7.3 %collective-permute-start.14 = (bf16[32,1024]{1,0:T(8,128)(2,1)S(1)}, bf16[32,1024]{1,0:T(8,128)(2,1)S(1)}, u32[]{:S(2)}, u32[]{:S(2)}) collective-permute-start(bf16[32,1024]{1,0:T(8,128)(2,1)S(1)} %get-tuple-element.25), channel_id=1, source_target_pairs={{0,12},{1,13},{2,14},{3,15},{4,8},{5,9},{6,10},{7,11},{8,4},{9,5},... | collective-permute-start | bytes 196616 | tf_op jit(solution)/shard_map/ppermute | solution.py:82
  41.5 6.1 %collective-permute-start.15 = (bf16[32,1024]{1,0:T(8,128)(2,1)S(1)}, bf16[32,1024]{1,0:T(8,128)(2,1)S(1)}, u32[]{:S(2)}, u32[]{:S(2)}) collective-permute-start(bf16[32,1024]{1,0:T(8,128)(2,1)S(1)} %get-tuple-element.26), channel_id=1, source_target_pairs={{0,6},{1,7},{2,4},{3,5},{4,2},{5,3},{6,0},{7,1},{8,14},{9,15},{10,... | collective-permute-start | bytes 196616 | tf_op jit(solution)/shard_map/ppermute | solution.py:82

commit v6 on v5

--- a/solution.py
+++ b/solution.py
@@ -9,6 +9,7 @@
 levels = 16
 lanes = 128
 most = 8
+anywhere = pl.BlockSpec(memory_space=pl.ANY)
 vmem = pl.BlockSpec(memory_space=pltpu.VMEM)
 
 
@@ -31,6 +32,10 @@
     for j in range(local):
         out_ref[:, j * rank : (j + 1) * rank] = own_ref[j]
         out_ref[:, (local + j) * rank : (local + j + 1) * rank] = peer_ref[j]
+
+
+def gate_body(after_ref, block_ref, out_ref):
+    del after_ref, block_ref, out_ref
 
 
 def expert_body(features, blocks, *refs):
@@ -148,6 +153,15 @@
     compute(of[0])
     send_home(of[0])
     crossing = [m for m in of[2] if hop_of(m) >= minor and m & (minor - 1)]
+    held[near] = pl.pallas_call(
+        gate_body,
+        out_shape=jax.ShapeDtypeStruct(packed.shape, packed.dtype),
+        in_specs=[anywhere] * 2,
+        out_specs=anywhere,
+        input_output_aliases={1: 0},
+        compiler_params=pltpu.CompilerParams(vmem_limit_bytes=1 << 20),
+        cost_estimate=pl.CostEstimate(flops=0, bytes_accessed=0, transcendentals=0),
+    )(parts[0], held[near])
     fetch(crossing)
     tie((held, [m for m in of[1] if m >= minor]), (parts, of[0]))
     fetch([m for m in of[2] if m not in crossing])

time: 48.5 us -> 47 us (0.969)
  waiting for transfers between devices: 12.6 us -> 5.84 us
  starting transfers between devices: 22.2 us -> 27.4 us
    ppermute x16, waiting for transfers between devices: 12.6 us -> 5.84 us  [exchange(): lax.ppermute(value, 'expert', [(i, i ^ mask) for i in range(devices_count)])]
    ppermute x16, starting transfers between devices: 22.2 us -> 27.4 us  [exchange(): lax.ppermute(value, 'expert', [(i, i ^ mask) for i in range(devices_count)])]
  transfers between devices with their start and end apart: 16 -> 16, of which waited for: 5 -> 4; matrix products, arithmetic and copies ran while one was open for 1% -> 2% of each run, Pallas kernels for 18% -> 18%
where the time goes in v6:
time: 47 us; the launch traced here: 46.8 us
  starting transfers between devices  27.4 us (58%)
  Pallas kernels  9.24 us (20%)
  waiting for transfers between devices  5.84 us (12%)
  local copies, waits for them, and re-layouts  3.48 us (7%)
  other arithmetic  0.71 us (2%)
    ppermute x16, starting transfers between devices, exchange(): lax.ppermute(value, 'expert', [(i, i ^ mask) for i in range(devices_count)])  27.4 us
    pallas_call x3, Pallas kernels, experts_on(): pl.pallas_call(functools.partial(expert_body, features, count), out_shape...  7.66 us
    ppermute x16, waiting for transfers between devices, exchange(): lax.ppermute(value, 'expert', [(i, i ^ mask) for i in range(devices_count)])  5.84 us
    unnamed x10, local copies, waits for them, and re-layouts  3.48 us
  transfers between devices with their start and end apart: 16, of which 4 were waited for; matrix products, arithmetic and copies ran while one was open for 2% of the time, Pallas kernels for 18%

profile of v6, /device:TPU:0, one launch (start us, length us, event | category | flops | bytes accessed | tf_op | source)
XLA Modules:
  0.0 46.8 jit_solution(12208849503535961015)
XLA Ops:
  0.0 0.5 collective-permute-start.1
  0.5 0.1 collective-permute-start.2
  0.5 0.7 %add_bitcast_fusion.marks_ref = s32[8,32]{1,0:T(8,128)S(1)} fusion(s32[32,8]{0,1:T(8,128)} %param.8, s32[32,8]{0,1:T(8,128)} %param.7), kind=kLoop, calls=%fused_computation | loop fusion | flops 512 | bytes 3072 | tf_op jit(solution)/shard_map/add | solution.py:115
  1.2 0.9 %copy-done.4 = bf16[32,3584]{1,0:T(8,128)(2,1)S(1)} copy-done((bf16[32,3584]{1,0:T(8,128)(2,1)S(1)}, bf16[32,3584]{1,0:T(8,128)(2,1)}, u32[]{:S(2)}) %copy-start.4) | copy-done | bytes 229400
  2.2 0.2 shard_map.64.refs_0_
  2.4 0.0 copy-start
  2.4 3.0 %collective-permute-start = (bf16[32,3712]{1,0:T(8,128)(2,1)S(1)}, bf16[32,3712]{1,0:T(8,128)(2,1)S(1)}, u32[]{:S(2)}, u32[]{:S(2)}) collective-permute-start(bf16[32,3712]{1,0:T(8,128)(2,1)S(1)} %shard_map.64.refs_0_), channel_id=1, source_target_pairs={{0,2},{1,3},{2,0},{3,1},{4,6},{5,7},{6,4},{7,5},{8,10},{9,11},{10,... | collective-permute-start | bytes 712712 | tf_op jit(solution)/shard_map/ppermute | solution.py:87
  5.5 2.6 %collective-permute-start.3 = (bf16[32,3712]{1,0:T(8,128)(2,1)S(1)}, bf16[32,3712]{1,0:T(8,128)(2,1)S(1)}, u32[]{:S(2)}, u32[]{:S(2)}) collective-permute-start(bf16[32,3712]{1,0:T(8,128)(2,1)S(1)} %shard_map.64.refs_0_), channel_id=1, source_target_pairs={{0,8},{1,9},{2,10},{3,11},{4,12},{5,13},{6,14},{7,15},{8,0},{9,1},... | collective-permute-start | bytes 712712 | tf_op jit(solution)/shard_map/ppermute | solution.py:87
  8.0 1.6 %collective-permute-start.4 = (bf16[32,3712]{1,0:T(8,128)(2,1)S(1)}, bf16[32,3712]{1,0:T(8,128)(2,1)S(1)}, u32[]{:S(2)}, u32[]{:S(2)}) collective-permute-start(bf16[32,3712]{1,0:T(8,128)(2,1)S(1)} %shard_map.64.refs_0_), channel_id=1, source_target_pairs={{0,4},{1,5},{2,6},{3,7},{4,0},{5,1},{6,2},{7,3},{8,12},{9,13},{10,... | collective-permute-start | bytes 712712 | tf_op jit(solution)/shard_map/ppermute | solution.py:87
  9.6 1.5 %copy-done.3 = bf16[2,3584,128]{2,1,0:T(8,128)(2,1)S(1)} copy-done((bf16[2,3584,128]{2,1,0:T(8,128)(2,1)S(1)}, bf16[2,3584,128]{2,1,0:T(8,128)(2,1)}, u32[]{:S(2)}) %copy-start.3) | copy-done | bytes 1835032
  11.1 0.6 %shard_map.65.refs_2_.refs_4_.refs_5_ = bf16[3584,512]{1,0:T(8,128)(2,1)S(1)} custom-call(bf16[2,3584,128]{2,1,0:T(8,128)(2,1)S(1)} %copy-done.3, bf16[2,3584,128]{2,1,0:T(8,128)(2,1)S(1)} %collective-permute-done.1.peer_ref), custom_call_target="tpu_custom_call" | custom-call | bytes 4000000 | tf_op jit(solution)/shard_map/pallas_call | solution.py:117
  11.8 0.0 collective-permute-done.2.refs_4_.refs_6_.refs_7_
  11.8 0.0 copy-start.1
  11.8 1.0 %copy-done.1 = bf16[2,128,1024]{2,1,0:T(8,128)(2,1)S(1)} copy-done((bf16[2,128,1024]{2,1,0:T(8,128)(2,1)S(1)}, bf16[2,128,1024]{2,1,0:T(8,128)(2,1)}, u32[]{:S(2)}) %copy-start.1) | copy-done | bytes 524312
  12.8 2.3 %shard_map.66.after_ref.refs_0_ = bf16[32,1024]{1,0:T(8,128)(2,1)S(1)} custom-call(bf16[32,3712]{1,0:T(8,128)(2,1)S(1)} %shard_map.64.refs_0_, bf16[3584,1024]{1,0:T(8,128)(2,1)S(1)} %copy-done, bf16[3584,512]{1,0:T(8,128)(2,1)S(1)} %shard_map.65.refs_2_.refs_4_.refs_5_, bf16[2,128,1024]{2,1,0:T(8,128)(2,1)S(1)} %copy-done.1, ...), custom_call_target="tpu_custom_call" | custom-call | flops 352321536 | bytes 9000000 | tf_op jit(solution)/shard_map/pallas_call | solution.py:101
  15.2 3.5 %collective-permute-start.8 = (bf16[32,3712]{1,0:T(8,128)(2,1)S(1)}, bf16[32,3712]{1,0:T(8,128)(2,1)S(1)}, u32[]{:S(2)}, u32[]{:S(2)}) collective-permute-start(bf16[32,3712]{1,0:T(8,128)(2,1)S(1)} %shard_map.67.refs_2_), channel_id=1, source_target_pairs={{0,12},{1,13},{2,14},{3,15},{4,8},{5,9},{6,10},{7,11},{8,4},{9,5},... | collective-permute-start | bytes 712712 | tf_op jit(solution)/shard_map/ppermute | solution.py:87
  18.7 2.2 %collective-permute-done.3.refs_1_ = bf16[32,3712]{1,0:T(8,128)(2,1)S(1)} collective-permute-done((bf16[32,3712]{1,0:T(8,128)(2,1)S(1)}, bf16[32,3712]{1,0:T(8,128)(2,1)S(1)}, u32[]{:S(2)}, u32[]{:S(2)}) %collective-permute-start.3) | collective-permute-done | bytes 237600 | tf_op jit(solution)/shard_map/ppermute | solution.py:87
  20.9 2.0 %collective-permute-start.10 = (bf16[32,3712]{1,0:T(8,128)(2,1)S(1)}, bf16[32,3712]{1,0:T(8,128)(2,1)S(1)}, u32[]{:S(2)}, u32[]{:S(2)}) collective-permute-start(bf16[32,3712]{1,0:T(8,128)(2,1)S(1)} %collective-permute-done.4.refs_0_), channel_id=1, source_target_pairs={{0,2},{1,3},{2,0},{3,1},{4,6},{5,7},{6,4},{7,5},{8,10},{9,11},{10,... | collective-permute-start | bytes 712712 | tf_op jit(solution)/shard_map/ppermute | solution.py:87
  22.9 2.7 %shard_map.68 = (bf16[32,1024]{1,0:T(8,128)(2,1)S(1)}, bf16[32,1024]{1,0:T(8,128)(2,1)S(1)}, bf16[32,1024]{1,0:T(8,128)(2,1)S(1)}) custom-call(bf16[32,3712]{1,0:T(8,128)(2,1)S(1)} %collective-permute-done.4.refs_0_, bf16[32,3712]{1,0:T(8,128)(2,1)S(1)} %collective-permute-done.3.refs_1_, bf16[32,3712]{1,0:T(8,128)(2,1)S(1)} %shard_map.67.refs_2_, ...), custom_call_target="tpu_custom_call" | custom-call | flops 1056964608 | bytes 9000000 | tf_op jit(solution)/shard_map/pallas_call | solution.py:101
  25.6 2.3 %collective-permute-start.5 = (bf16[32,1024]{1,0:T(8,128)(2,1)S(1)}, bf16[32,1024]{1,0:T(8,128)(2,1)S(1)}, u32[]{:S(2)}, u32[]{:S(2)}) collective-permute-start(bf16[32,1024]{1,0:T(8,128)(2,1)S(1)} %get-tuple-element.20), channel_id=1, source_target_pairs={{0,8},{1,9},{2,10},{3,11},{4,12},{5,13},{6,14},{7,15},{8,0},{9,1},... | collective-permute-start | bytes 196616 | tf_op jit(solution)/shard_map/ppermute | solution.py:87
  27.9 0.0 collective-permute-done.8.refs_0_
  27.9 3.2 %collective-permute-start.6 = (bf16[32,1024]{1,0:T(8,128)(2,1)S(1)}, bf16[32,1024]{1,0:T(8,128)(2,1)S(1)}, u32[]{:S(2)}, u32[]{:S(2)}) collective-permute-start(bf16[32,1024]{1,0:T(8,128)(2,1)S(1)} %get-tuple-element.21), channel_id=1, source_target_pairs={{0,4},{1,5},{2,6},{3,7},{4,0},{5,1},{6,2},{7,3},{8,12},{9,13},{10,... | collective-permute-start | bytes 196616 | tf_op jit(solution)/shard_map/ppermute | solution.py:87
  31.0 0.6 %collective-permute-start.7 = (bf16[32,1024]{1,0:T(8,128)(2,1)S(1)}, bf16[32,1024]{1,0:T(8,128)(2,1)S(1)}, u32[]{:S(2)}, u32[]{:S(2)}) collective-permute-start(bf16[32,1024]{1,0:T(8,128)(2,1)S(1)} %get-tuple-element.22), channel_id=1, source_target_pairs={{0,2},{1,3},{2,0},{3,1},{4,6},{5,7},{6,4},{7,5},{8,10},{9,11},{10,... | collective-permute-start | bytes 196616 | tf_op jit(solution)/shard_map/ppermute | solution.py:87
  31.6 0.0 collective-permute-done.10.refs_2_
  31.6 0.2 collective-permute-done.11.refs_3_
  31.8 2.7 %shard_map.69 = (bf16[32,1024]{1,0:T(8,128)(2,1)S(1)}, bf16[32,1024]{1,0:T(8,128)(2,1)S(1)}, bf16[32,1024]{1,0:T(8,128)(2,1)S(1)}, bf16[32,1024]{1,0:T(8,128)(2,1)S(1)}) custom-call(bf16[32,3712]{1,0:T(8,128)(2,1)S(1)} %collective-permute-done.8.refs_0_, bf16[32,3712]{1,0:T(8,128)(2,1)S(1)} %collective-permute-done.9.refs_1_, ...), custom_call_target="tpu_custom_call" | custom-call | flops 1409286144 | bytes 9000000 | tf_op jit(solution)/shard_map/pallas_call | solution.py:101
  34.5 3.8 %collective-permute-start.12 = (bf16[32,1024]{1,0:T(8,128)(2,1)S(1)}, bf16[32,1024]{1,0:T(8,128)(2,1)S(1)}, u32[]{:S(2)}, u32[]{:S(2)}) collective-permute-start(bf16[32,1024]{1,0:T(8,128)(2,1)S(1)} %get-tuple-element.23), channel_id=1, source_target_pairs={{0,14},{1,15},{2,12},{3,13},{4,10},{5,11},{6,8},{7,9},{8,6},{9,7},... | collective-permute-start | bytes 196616 | tf_op jit(solution)/shard_map/ppermute | solution.py:87
  38.3 1.8 %collective-permute-start.14 = (bf16[32,1024]{1,0:T(8,128)(2,1)S(1)}, bf16[32,1024]{1,0:T(8,128)(2,1)S(1)}, u32[]{:S(2)}, u32[]{:S(2)}) collective-permute-start(bf16[32,1024]{1,0:T(8,128)(2,1)S(1)} %get-tuple-element.25), channel_id=1, source_target_pairs={{0,12},{1,13},{2,14},{3,15},{4,8},{5,9},{6,10},{7,11},{8,4},{9,5},... | collective-permute-start | bytes 196616 | tf_op jit(solution)/shard_map/ppermute | solution.py:87
  40.1 2.5 %collective-permute-start.15 = (bf16[32,1024]{1,0:T(8,128)(2,1)S(1)}, bf16[32,1024]{1,0:T(8,128)(2,1)S(1)}, u32[]{:S(2)}, u32[]{:S(2)}) collective-permute-start(bf16[32,1024]{1,0:T(8,128)(2,1)S(1)} %get-tuple-element.26), channel_id=1, source_target_pairs={{0,6},{1,7},{2,4},{3,5},{4,2},{5,3},{6,0},{7,1},{8,14},{9,15},{10,... | collective-permute-start | bytes 196616 | tf_op jit(solution)/shard_map/ppermute | solution.py:87
  42.7 3.1 %collective-permute-done.13.refs_5_ = bf16[32,1024]{1,0:T(8,128)(2,1)S(1)} collective-permute-done((bf16[32,1024]{1,0:T(8,128)(2,1)S(1)}, bf16[32,1024]{1,0:T(8,128)(2,1)S(1)}, u32[]{:S(2)}, u32[]{:S(2)}) %collective-permute-start.13) | collective-permute-done | bytes 65568 | tf_op jit(solution)/shard_map/ppermute | solution.py:87
  45.8 0.3 collective-permute-done.15.refs_7_
  46.1 0.7 %shard_map.70 = bf16[32,1024]{1,0:T(8,128)(2,1)} custom-call(bf16[32,1024]{1,0:T(8,128)(2,1)S(1)} %shard_map.66.after_ref.refs_0_, bf16[32,1024]{1,0:T(8,128)(2,1)S(1)} %collective-permute-done.5.refs_1_, bf16[32,1024]{1,0:T(8,128)(2,1)S(1)} %collective-permute-done.6.refs_2_, bf16[32,1024]{1,0:T(8,128)(2,1)S(1)} %collective-permute-done.7.refs_3_, ...), custom_call_target="tpu_custom_call" | custom-call | bytes 2000000 | tf_op jit(solution)/shard_map/pallas_call | solution.py:179
  (18 shorter events, 0.0 us)
Async XLA Ops:
  0.0 9.6 %collective-permute-start.1 = (bf16[2,3584,128]{2,1,0:T(8,128)(2,1)}, bf16[2,3584,128]{2,1,0:T(8,128)(2,1)S(1)}, u32[]{:S(2)}, u32[]{:S(2)}) collective-permute-start(bf16[2,3584,128]{2,1,0:T(8,128)(2,1)} %own_ref.1), channel_id=1, source_target_pairs={{0,1},{1,0},{2,3},{3,2},{4,5},{5,4},{6,7},{7,6},{8,9},{9,8},{10,11... | collective-permute-start | bytes 5505032 | tf_op jit(solution)/shard_map/ppermute | solution.py:87
  0.5 11.3 %collective-permute-start.2 = (bf16[2,128,1024]{2,1,0:T(8,128)(2,1)}, bf16[2,128,1024]{2,1,0:T(8,128)(2,1)S(1)}, u32[]{:S(2)}, u32[]{:S(2)}) collective-permute-start(bf16[2,128,1024]{2,1,0:T(8,128)(2,1)} %refs_6_.1), channel_id=1, source_target_pairs={{0,1},{1,0},{2,3},{3,2},{4,5},{5,4},{6,7},{7,6},{8,9},{9,8},{10,11... | collective-permute-start | bytes 1572872 | tf_op jit(solution)/shard_map/ppermute | solution.py:87
  1.2 0.9 %copy-start.4 = (bf16[32,3584]{1,0:T(8,128)(2,1)S(1)}, bf16[32,3584]{1,0:T(8,128)(2,1)}, u32[]{:S(2)}) copy-start(bf16[32,3584]{1,0:T(8,128)(2,1)} %tokens_ref.1) | copy-start | bytes 688132
  2.4 9.4 %copy-start = (bf16[3584,1024]{1,0:T(8,128)(2,1)S(1)}, bf16[3584,1024]{1,0:T(8,128)(2,1)}, u32[]{:S(2)}) copy-start(bf16[3584,1024]{1,0:T(8,128)(2,1)} %refs_4_.1) | copy-start | bytes 22020100
  2.4 9.3 %collective-permute-start = (bf16[32,3712]{1,0:T(8,128)(2,1)S(1)}, bf16[32,3712]{1,0:T(8,128)(2,1)S(1)}, u32[]{:S(2)}, u32[]{:S(2)}) collective-permute-start(bf16[32,3712]{1,0:T(8,128)(2,1)S(1)} %shard_map.64.refs_0_), channel_id=1, source_target_pairs={{0,2},{1,3},{2,0},{3,1},{4,6},{5,7},{6,4},{7,5},{8,10},{9,11},{10,... | collective-permute-start | bytes 712712 | tf_op jit(solution)/shard_map/ppermute | solution.py:87
  5.5 15.4 %collective-permute-start.3 = (bf16[32,3712]{1,0:T(8,128)(2,1)S(1)}, bf16[32,3712]{1,0:T(8,128)(2,1)S(1)}, u32[]{:S(2)}, u32[]{:S(2)}) collective-permute-start(bf16[32,3712]{1,0:T(8,128)(2,1)S(1)} %shard_map.64.refs_0_), channel_id=1, source_target_pairs={{0,8},{1,9},{2,10},{3,11},{4,12},{5,13},{6,14},{7,15},{8,0},{9,1},... | collective-permute-start | bytes 712712 | tf_op jit(solution)/shard_map/ppermute | solution.py:87
  8.0 12.8 %collective-permute-start.4 = (bf16[32,3712]{1,0:T(8,128)(2,1)S(1)}, bf16[32,3712]{1,0:T(8,128)(2,1)S(1)}, u32[]{:S(2)}, u32[]{:S(2)}) collective-permute-start(bf16[32,3712]{1,0:T(8,128)(2,1)S(1)} %shard_map.64.refs_0_), channel_id=1, source_target_pairs={{0,4},{1,5},{2,6},{3,7},{4,0},{5,1},{6,2},{7,3},{8,12},{9,13},{10,... | collective-permute-start | bytes 712712 | tf_op jit(solution)/shard_map/ppermute | solution.py:87
  9.6 1.5 %copy-start.3 = (bf16[2,3584,128]{2,1,0:T(8,128)(2,1)S(1)}, bf16[2,3584,128]{2,1,0:T(8,128)(2,1)}, u32[]{:S(2)}) copy-start(bf16[2,3584,128]{2,1,0:T(8,128)(2,1)} %own_ref.1) | copy-start | bytes 5505028
  11.8 1.0 %copy-start.1 = (bf16[2,128,1024]{2,1,0:T(8,128)(2,1)S(1)}, bf16[2,128,1024]{2,1,0:T(8,128)(2,1)}, u32[]{:S(2)}) copy-start(bf16[2,128,1024]{2,1,0:T(8,128)(2,1)} %refs_6_.1) | copy-start | bytes 1572868
  12.8 10.1 %copy-start.2 = (bf16[2,128,1024]{2,1,0:T(8,128)(2,1)S(1)}, bf16[2,128,1024]{2,1,0:T(8,128)(2,1)}, u32[]{:S(2)}) copy-start(bf16[2,128,1024]{2,1,0:T(8,128)(2,1)} %refs_6_.1) | copy-start | bytes 1572868
  15.2 12.7 %collective-permute-start.8 = (bf16[32,3712]{1,0:T(8,128)(2,1)S(1)}, bf16[32,3712]{1,0:T(8,128)(2,1)S(1)}, u32[]{:S(2)}, u32[]{:S(2)}) collective-permute-start(bf16[32,3712]{1,0:T(8,128)(2,1)S(1)} %shard_map.67.refs_2_), channel_id=1, source_target_pairs={{0,12},{1,13},{2,14},{3,15},{4,8},{5,9},{6,10},{7,11},{8,4},{9,5},... | collective-permute-start | bytes 712712 | tf_op jit(solution)/shard_map/ppermute | solution.py:87
  20.9 10.2 %collective-permute-start.9 = (bf16[32,3712]{1,0:T(8,128)(2,1)S(1)}, bf16[32,3712]{1,0:T(8,128)(2,1)S(1)}, u32[]{:S(2)}, u32[]{:S(2)}) collective-permute-start(bf16[32,3712]{1,0:T(8,128)(2,1)S(1)} %collective-permute-done.3.refs_1_), channel_id=1, source_target_pairs={{0,2},{1,3},{2,0},{3,1},{4,6},{5,7},{6,4},{7,5},{8,10},{9,11},{10,... | collective-permute-start | bytes 712712 | tf_op jit(solution)/shard_map/ppermute | solution.py:87
  20.9 10.7 %collective-permute-start.10 = (bf16[32,3712]{1,0:T(8,128)(2,1)S(1)}, bf16[32,3712]{1,0:T(8,128)(2,1)S(1)}, u32[]{:S(2)}, u32[]{:S(2)}) collective-permute-start(bf16[32,3712]{1,0:T(8,128)(2,1)S(1)} %collective-permute-done.4.refs_0_), channel_id=1, source_target_pairs={{0,2},{1,3},{2,0},{3,1},{4,6},{5,7},{6,4},{7,5},{8,10},{9,11},{10,... | collective-permute-start | bytes 712712 | tf_op jit(solution)/shard_map/ppermute | solution.py:87
  22.9 8.9 %collective-permute-start.11 = (bf16[32,3712]{1,0:T(8,128)(2,1)S(1)}, bf16[32,3712]{1,0:T(8,128)(2,1)S(1)}, u32[]{:S(2)}, u32[]{:S(2)}) collective-permute-start(bf16[32,3712]{1,0:T(8,128)(2,1)S(1)} %collective-permute-done.3.refs_1_), channel_id=1, source_target_pairs={{0,4},{1,5},{2,6},{3,7},{4,0},{5,1},{6,2},{7,3},{8,12},{9,13},{10,... | collective-permute-start | bytes 712712 | tf_op jit(solution)/shard_map/ppermute | solution.py:87
  25.6 12.7 %collective-permute-start.5 = (bf16[32,1024]{1,0:T(8,128)(2,1)S(1)}, bf16[32,1024]{1,0:T(8,128)(2,1)S(1)}, u32[]{:S(2)}, u32[]{:S(2)}) collective-permute-start(bf16[32,1024]{1,0:T(8,128)(2,1)S(1)} %get-tuple-element.20), channel_id=1, source_target_pairs={{0,8},{1,9},{2,10},{3,11},{4,12},{5,13},{6,14},{7,15},{8,0},{9,1},... | collective-permute-start | bytes 196616 | tf_op jit(solution)/shard_map/ppermute | solution.py:87
  27.9 12.2 %collective-permute-start.6 = (bf16[32,1024]{1,0:T(8,128)(2,1)S(1)}, bf16[32,1024]{1,0:T(8,128)(2,1)S(1)}, u32[]{:S(2)}, u32[]{:S(2)}) collective-permute-start(bf16[32,1024]{1,0:T(8,128)(2,1)S(1)} %get-tuple-element.21), channel_id=1, source_target_pairs={{0,4},{1,5},{2,6},{3,7},{4,0},{5,1},{6,2},{7,3},{8,12},{9,13},{10,... | collective-permute-start | bytes 196616 | tf_op jit(solution)/shard_map/ppermute | solution.py:87
  31.0 11.6 %collective-permute-start.7 = (bf16[32,1024]{1,0:T(8,128)(2,1)S(1)}, bf16[32,1024]{1,0:T(8,128)(2,1)S(1)}, u32[]{:S(2)}, u32[]{:S(2)}) collective-permute-start(bf16[32,1024]{1,0:T(8,128)(2,1)S(1)} %get-tuple-element.22), channel_id=1, source_target_pairs={{0,2},{1,3},{2,0},{3,1},{4,6},{5,7},{6,4},{7,5},{8,10},{9,11},{10,... | collective-permute-start | bytes 196616 | tf_op jit(solution)/shard_map/ppermute | solution.py:87
  34.5 8.2 %collective-permute-start.12 = (bf16[32,1024]{1,0:T(8,128)(2,1)S(1)}, bf16[32,1024]{1,0:T(8,128)(2,1)S(1)}, u32[]{:S(2)}, u32[]{:S(2)}) collective-permute-start(bf16[32,1024]{1,0:T(8,128)(2,1)S(1)} %get-tuple-element.23), channel_id=1, source_target_pairs={{0,14},{1,15},{2,12},{3,13},{4,10},{5,11},{6,8},{7,9},{8,6},{9,7},... | collective-permute-start | bytes 196616 | tf_op jit(solution)/shard_map/ppermute | solution.py:87
  38.3 7.5 %collective-permute-start.13 = (bf16[32,1024]{1,0:T(8,128)(2,1)S(1)}, bf16[32,1024]{1,0:T(8,128)(2,1)S(1)}, u32[]{:S(2)}, u32[]{:S(2)}) collective-permute-start(bf16[32,1024]{1,0:T(8,128)(2,1)S(1)} %get-tuple-element.24), channel_id=1, source_target_pairs={{0,10},{1,11},{2,8},{3,9},{4,14},{5,15},{6,12},{7,13},{8,2},{9,3},... | collective-permute-start | bytes 196616 | tf_op jit(solution)/shard_map/ppermute | solution.py:87
  38.3 7.5 %collective-permute-start.14 = (bf16[32,1024]{1,0:T(8,128)(2,1)S(1)}, bf16[32,1024]{1,0:T(8,128)(2,1)S(1)}, u32[]{:S(2)}, u32[]{:S(2)}) collective-permute-start(bf16[32,1024]{1,0:T(8,128)(2,1)S(1)} %get-tuple-element.25), channel_id=1, source_target_pairs={{0,12},{1,13},{2,14},{3,15},{4,8},{5,9},{6,10},{7,11},{8,4},{9,5},... | collective-permute-start | bytes 196616 | tf_op jit(solution)/shard_map/ppermute | solution.py:87
  40.1 6.0 %collective-permute-start.15 = (bf16[32,1024]{1,0:T(8,128)(2,1)S(1)}, bf16[32,1024]{1,0:T(8,128)(2,1)S(1)}, u32[]{:S(2)}, u32[]{:S(2)}) collective-permute-start(bf16[32,1024]{1,0:T(8,128)(2,1)S(1)} %get-tuple-element.26), channel_id=1, source_target_pairs={{0,6},{1,7},{2,4},{3,5},{4,2},{5,3},{6,0},{7,1},{8,14},{9,15},{10,... | collective-permute-start | bytes 196616 | tf_op jit(solution)/shard_map/ppermute | solution.py:87
